TPU v7x, 128 devices: a whole 4x4x4 slice. The times are simulated.
128 devices in a mesh: dp: 4 (over z), seq: 32 (over x, y, core).
Axes of the slice: x: 4, y: 4, z: 4, core: 2. Of those that a mesh axis runs over, the one named last changes fastest.
Arguments:
- merged_product_embeddings: bfloat16 [65536, 4096], P(('dp', 'seq')), may hold values from -10 to 10
- fetched_home_chip: int32 [4, 32, 264, 1], P('dp', 'seq'), may hold values from 0 to 127; in each aligned block of 264 rows (0 to 263, 264 to 527, ..., all dimensions but the last counted through in order) at most 4 rows name the same one
- fetched_home_slot: int32 [4, 32, 264, 1], P('dp', 'seq'), may hold values from 0 to 511
- memory_fading_speeds: float32 [128, 32], P(('dp', 'seq')), may hold values from 0.00078125 to 0.0333333333
- forgetting_fraction: float32 [128, 256], P(('dp', 'seq')), may hold values from 0 to 0.5
- magnitude_scaling: float32 [4096], replicated, may hold values from 0.5 to 1.5
Outputs:
- row_loss: float32 [128, 256], P(('dp', 'seq'))
- user_grad: bfloat16 [128, 256, 4096], P(('dp', 'seq'))
- item_grad: float32 [65536, 4096], P(('dp', 'seq'))
Inputs may be any that keep to these rules, and one draw needn't show every extreme that they name: `fetched_home_chip`: at most 4 of the 264 requests of one device name one owner; some owner receives exactly 4 from a device.
All inputs are finite; a program needn't handle non-finite values.
Results may differ from a plain program's by a relative error of at most 0.015.
Values may be sent and summed in bfloat16 or wider, within the bound.
No kernel may reach another device: no remote copies, remote signals or barrier semaphores. Data moves between devices by JAX's collectives and lax.ppermute only.
A program may use at most 128 MiB of HBM per device.

v0:
```python
import functools

import jax
import jax.numpy as jnp
from jax import lax
from jax.experimental import pallas as pl
from jax.experimental.pallas import tpu as pltpu
from jax.sharding import PartitionSpec as P

D = 4096
HEADS = 32
HEAD_DIM = 128
STEPS = 256
OWN_NEG = 8
REQ = STEPS + OWN_NEG
NEG = 256
ITEMS = 512
DEVICES = 128
CAP = 4
SLOTS = DEVICES * CAP
SIGMA = 4.0 / 64.0
BLOCK = 1024
F32 = jnp.float32
BF16 = jnp.bfloat16
I32 = jnp.int32
AXES = ("dp", "seq")
PARAMS = pltpu.CompilerParams(vmem_limit_bytes=48 * 2**20)


def iota(shape, dim):
    return lax.broadcasted_iota(I32, shape, dim)


def call(kernel, out_shape, name, **kw):
    return pl.pallas_call(kernel, out_shape=out_shape, name=name, compiler_params=PARAMS, **kw)


def matmul(a, b, dims):
    return lax.dot_general(a, b, ((dims[0], dims[1]), ((), ())), preferred_element_type=F32)


def route_kernel(owner_col, owner_row, item_row, wanted, slots):
    col, row = owner_col[...], owner_row[...]

    def key(i):
        return jnp.where(i >= STEPS, i - 2 * STEPS, i)

    earlier = key(iota((REQ, REQ), 0)) < key(iota((REQ, REQ), 1))
    rank = jnp.sum(jnp.where((col == row) & earlier, 1.0, 0.0), axis=0, keepdims=True).astype(I32)
    slots[...] = row * CAP + rank
    item = (item_row[...] + 1).astype(F32)
    here = iota((DEVICES, REQ), 0) == row
    out = jnp.full((DEVICES, 128), -1.0, F32)
    lane = iota((DEVICES, 128), 1)
    for s in range(CAP):
        named = jnp.sum(jnp.where(here & (rank == s), item, 0.0), axis=1, keepdims=True)
        out = jnp.where(lane == s, named - 1.0, out)
    wanted[...] = out.astype(I32)


def onehot_items(asked):
    asked = asked.astype(F32)
    device, slot = iota((DEVICES, SLOTS), 0), iota((DEVICES, SLOTS), 1)
    row = jnp.zeros((DEVICES, SLOTS), F32)
    for s in range(CAP):
        row = row + jnp.where(slot == device * CAP + s, asked[:, s : s + 1], 0.0)
    row = jnp.sum(row, axis=0, keepdims=True)
    return (iota((ITEMS, SLOTS), 0).astype(F32) == row).astype(F32).astype(BF16)


def pick_kernel(asked, table, out, hot):
    @pl.when(pl.program_id(0) == 0)
    def _():
        hot[...] = onehot_items(asked[...])

    rows = matmul(hot[...], table[...], ((0,), (0,)))
    out[...] = rows.astype(BF16).reshape(out.shape)


def place_kernel(asked, arrived, out, hot):
    @pl.when(pl.program_id(0) == 0)
    def _():
        hot[...] = onehot_items(asked[...])

    out[...] = matmul(hot[...], arrived[...].reshape(SLOTS, arrived.shape[2]), ((1,), (0,)))


def onehot_slots(slots):
    return (iota((SLOTS, slots.shape[1]), 0) == slots).astype(F32).astype(BF16)


def own_negatives_kernel(slots, rows, out):
    hot = onehot_slots(slots[:, STEPS:REQ])
    out[...] = matmul(hot, rows[...].reshape(SLOTS, rows.shape[2]), ((0,), (0,))).astype(BF16)


def decay_kernel(speeds, forget_row, forget_col, out, base):
    step, source = iota((STEPS, STEPS), 0), iota((STEPS, STEPS), 1)

    @pl.when(pl.program_id(0) == 0)
    def _():
        log_row, log_col = jnp.log(1.0 - forget_row[...]), jnp.log(1.0 - forget_col[...])
        until = jnp.sum(jnp.where(source < step, log_row, 0.0), axis=1, keepdims=True)
        through = jnp.sum(jnp.where(step <= source, log_col, 0.0), axis=0, keepdims=True)
        base[...] = jnp.where(source < step, until - through, -1e30)

    span = (step - 1 - source).astype(F32)
    for k in range(out.shape[0]):
        speed = speeds[0, pl.program_id(0) * out.shape[0] + k]
        full = jnp.exp(base[...] - speed * span)
        high = full.astype(BF16)
        out[k, :, :STEPS] = high
        out[k, :, STEPS:] = (full - high.astype(F32)).astype(BF16)


def state_kernel(slots, rows, decay, gain, x_out, rep_out, pos_out, hot, prior, total):
    j, last = pl.program_id(0), pl.num_programs(0) - 1
    width = rows.shape[2]

    @pl.when(j == 0)
    def _():
        hot[...] = onehot_slots(slots[:, :STEPS])
        total[...] = jnp.zeros_like(total)

    x = matmul(hot[...], rows[...].reshape(SLOTS, width), ((0,), (0,))).astype(BF16)
    columns = pl.ds(pl.multiple_of(j * width, width), width)
    x_out[:, columns] = x
    for k in range(width // HEAD_DIM):
        part = slice(k * HEAD_DIM, (k + 1) * HEAD_DIM)
        xk = x[:, part]
        state = matmul(decay[k, :, :STEPS], xk, ((1,), (0,))) + matmul(
            decay[k, :, STEPS:], xk, ((1,), (0,))
        )
        total[...] += state * state
        prior[:, pl.ds(pl.multiple_of(j * width + k * HEAD_DIM, HEAD_DIM), HEAD_DIM)] = state

    @pl.when(j == last)
    def _():
        norm = lax.rsqrt(jnp.sum(total[...], axis=1, keepdims=True) * (1.0 / D) + 1e-06)
        pos = jnp.zeros((STEPS, HEAD_DIM), F32)
        for c in range(0, D, HEAD_DIM):
            part = slice(c, c + HEAD_DIM)
            rep = (prior[:, part] * norm * gain[:, part]).astype(BF16)
            rep_out[:, part] = rep
            pos = pos + rep.astype(F32) * x_out[:, part].astype(F32)
        pos_out[...] = SIGMA * jnp.sum(pos, axis=1, keepdims=True)


def loss_kernel(rep, near, far, pos_logit, loss, d_pos, d_neg, neg_part):
    u = rep[...]
    half = NEG // 2
    logits = [SIGMA * matmul(u, n[...], ((1,), (1,))) for n in (near, far)]
    pos = pos_logit[...]
    top = jnp.maximum(jnp.max(jnp.maximum(*logits), axis=1, keepdims=True), pos)
    summed = sum(jnp.sum(jnp.exp(l - top), axis=1, keepdims=True) for l in logits)
    log_total = top + jnp.log(jnp.exp(pos - top) + summed)
    valid = jnp.where(iota((STEPS, 1), 0) > 0, 1.0, 0.0)
    loss[...] = (log_total - pos) * valid
    d_pos[...] = (jnp.exp(pos - log_total) - 1.0) * valid
    for k, l in enumerate(logits):
        share = (jnp.exp(l - log_total) * valid).astype(BF16)
        d_neg[:, k * half : (k + 1) * half] = share
        neg_part[k * half : (k + 1) * half, :] = (SIGMA * matmul(share, u, ((0,), (0,)))).astype(BF16)


def outgoing_kernel(slots, rep, d_pos, neg_grad, out, hot, hot_neg):
    @pl.when(pl.program_id(0) == 0)
    def _():
        hot[...] = onehot_slots(slots[:, :STEPS])
        hot_neg[...] = onehot_slots(slots[:, STEPS:REQ])

    grad = (SIGMA * d_pos[...] * rep[...].astype(F32)).astype(BF16)
    rows = matmul(hot[...], grad, ((1,), (0,))) + matmul(hot_neg[...], neg_grad[...], ((1,), (0,)))
    out[...] = rows.astype(BF16).reshape(out.shape)


def user_grad_kernel(x, d_pos, d_neg, near, far, out):
    half = NEG // 2
    from_neg = matmul(d_neg[:, :half], near[...], ((1,), (0,))) + matmul(
        d_neg[:, half:], far[...], ((1,), (0,))
    )
    out[0] = (SIGMA * (d_pos[...] * x[...].astype(F32) + from_neg)).astype(BF16)


def shift(value, dx=0, dy=0, core=0):
    pairs = []
    for x in range(4):
        for y in range(4):
            for c in range(2):
                to = ((x + dx) % 4 * 4 + (y + dy) % 4) * 2 + (c ^ core)
                pairs.append(((x * 4 + y) * 2 + c, to))
    return lax.ppermute(value, "seq", pairs)


def spread_negatives(own):
    line = jnp.concatenate([own] + [shift(own, dy=k) for k in (1, 2, 3)], axis=0)
    near = jnp.concatenate([line] + [shift(line, dx=k) for k in (1, 2, 3)], axis=0)
    return near, shift(near, core=1)


def add(parts):
    return sum(p.astype(F32) for p in parts).astype(BF16)


def collect_negatives(part):
    half = NEG // 2
    plane = add([part[:half], shift(part[half:], core=1)])
    n = half // 4
    line = add([plane[:n]] + [shift(plane[k * n : (k + 1) * n], dx=-k) for k in (1, 2, 3)])
    n = n // 4
    return add([line[:n]] + [shift(line[k * n : (k + 1) * n], dy=-k) for k in (1, 2, 3)])


def exchange(rows):
    return lax.all_to_all(rows, AXES, split_axis=0, concat_axis=0, tiled=True)


def whole(shape):
    return pl.BlockSpec(shape, lambda j: (0,) * len(shape))


def on_device(table, home, item, speeds, forget, gain):
    grid = (D // BLOCK,)
    columns = lambda n: pl.BlockSpec((n, BLOCK), lambda j: (0, j))
    slots_block = pl.BlockSpec((DEVICES, CAP, BLOCK), lambda j: (0, 0, j))
    shape = jax.ShapeDtypeStruct
    wanted, slots = call(
        route_kernel, (shape((DEVICES, 128), I32), shape((1, REQ), I32)), "route"
    )(home.reshape(REQ, 1), home.reshape(1, REQ), item.reshape(1, REQ))
    asked = exchange(wanted.reshape(DEVICES, 1, 128)).reshape(DEVICES, 128)
    picked = call(
        pick_kernel,
        shape((DEVICES, CAP, D), BF16),
        "pick",
        grid=grid,
        in_specs=[whole((DEVICES, 128)), columns(ITEMS)],
        out_specs=slots_block,
        scratch_shapes=[pltpu.VMEM((ITEMS, SLOTS), BF16)],
    )(asked, table)
    fetched = exchange(picked)
    group = 4
    decay = call(
        decay_kernel,
        shape((HEADS, STEPS, 2 * STEPS), BF16),
        "decay",
        grid=(HEADS // group,),
        in_specs=[
            pl.BlockSpec(memory_space=pltpu.SMEM),
            whole((1, STEPS)),
            whole((STEPS, 1)),
        ],
        out_specs=pl.BlockSpec((group, STEPS, 2 * STEPS), lambda j: (j, 0, 0)),
        scratch_shapes=[pltpu.VMEM((STEPS, STEPS), F32)],
    )(speeds, forget, forget.reshape(STEPS, 1))
    own = call(
        own_negatives_kernel,
        shape((OWN_NEG, D), BF16),
        "own_negatives",
        grid=grid,
        in_specs=[whole((1, REQ)), slots_block],
        out_specs=columns(OWN_NEG),
    )(slots, fetched)
    near, far = spread_negatives(own)
    x, rep, pos_logit = call(
        state_kernel,
        (shape((STEPS, D), BF16), shape((STEPS, D), BF16), shape((STEPS, 1), F32)),
        "state",
        grid=grid,
        in_specs=[
            whole((1, REQ)),
            slots_block,
            pl.BlockSpec((BLOCK // HEAD_DIM, STEPS, 2 * STEPS), lambda j: (j, 0, 0)),
            whole((1, D)),
        ],
        out_specs=(whole((STEPS, D)), whole((STEPS, D)), whole((STEPS, 1))),
        scratch_shapes=[
            pltpu.VMEM((SLOTS, STEPS), BF16),
            pltpu.VMEM((STEPS, D), F32),
            pltpu.VMEM((STEPS, HEAD_DIM), F32),
        ],
    )(slots, fetched, decay, gain.reshape(1, D))
    loss, d_pos, d_neg, neg_part = call(
        loss_kernel,
        (
            shape((STEPS, 1), F32),
            shape((STEPS, 1), F32),
            shape((STEPS, NEG), BF16),
            shape((NEG, D), BF16),
        ),
        "loss",
    )(rep, near, far, pos_logit)
    neg_grad = collect_negatives(neg_part)
    outgoing = call(
        outgoing_kernel,
        shape((DEVICES, CAP, D), BF16),
        "outgoing",
        grid=grid,
        in_specs=[whole((1, REQ)), columns(STEPS), whole((STEPS, 1)), columns(OWN_NEG)],
        out_specs=slots_block,
        scratch_shapes=[pltpu.VMEM((SLOTS, STEPS), BF16), pltpu.VMEM((SLOTS, OWN_NEG), BF16)],
    )(slots, rep, d_pos, neg_grad)
    arrived = exchange(outgoing)
    user_grad = call(
        user_grad_kernel,
        shape((1, STEPS, D), BF16),
        "user_grad",
        grid=grid,
        in_specs=[
            columns(STEPS),
            whole((STEPS, 1)),
            whole((STEPS, NEG)),
            columns(NEG // 2),
            columns(NEG // 2),
        ],
        out_specs=pl.BlockSpec((1, STEPS, BLOCK), lambda j: (0, 0, j)),
    )(x, d_pos, d_neg, near, far)
    item_grad = call(
        place_kernel,
        shape((ITEMS, D), F32),
        "place",
        grid=grid,
        in_specs=[whole((DEVICES, 128)), slots_block],
        out_specs=columns(ITEMS),
        scratch_shapes=[pltpu.VMEM((ITEMS, SLOTS), BF16)],
    )(asked, arrived)
    return loss.reshape(1, STEPS), user_grad, item_grad


def solution(mesh):
    return jax.shard_map(
        on_device,
        mesh=mesh,
        in_specs=(
            P(AXES, None),
            P("dp", "seq", None, None),
            P("dp", "seq", None, None),
            P(AXES, None),
            P(AXES, None),
            P(),
        ),
        out_specs=(P(AXES, None), P(AXES, None, None), P(AXES, None)),
        check_vma=False,
    )
```

profile of v0, /device:TPU:1, one launch (start us, length us, event | category | flops | bytes accessed | tf_op | source)
XLA Modules:
  0.0 230.5 jit_solution(12028576568557160640)
XLA Ops:
  3.1 20.9 %all_to_all.15 = s32[128,1,128]{2,1,0:T(1,128)S(1)} all-to-all(s32[128,1,128]{2,1,0:T(1,128)S(1)} %bitcast.12), channel_id=1, replica_groups=mesh['dp'=4,'seq'=32] {'dp','seq'}, dimensions={0} | all-to-all | bytes 131072 | tf_op jit(solution)/shard_map/all_to_all | solution.py:215
  24.0 5.4 %pick.1 = bf16[128,4,4096]{2,1,0:T(4,128)(2,1)S(1)} custom-call(s32[128,128]{1,0:T(8,128)S(1)} %bitcast.10, bf16[512,4096]{1,0:T(8,128)(2,1)} %table.1), custom_call_target="tpu_custom_call" | custom-call | tf_op jit(solution)/shard_map/pick/pallas_call | solution.py:231
  29.4 57.4 %all_to_all.16.rows = bf16[128,4,4096]{2,1,0:T(4,128)(2,1)S(1)} all-to-all(bf16[128,4,4096]{2,1,0:T(4,128)(2,1)S(1)} %pick.1), channel_id=1, replica_groups=mesh['dp'=4,'seq'=32] {'dp','seq'}, dimensions={0} | all-to-all | bytes 8388608 | tf_op jit(solution)/shard_map/all_to_all | solution.py:215
  91.4 2.7 %collective-permute-done = bf16[8,4096]{1,0:T(8,128)(2,1)S(1)} collective-permute-done((bf16[8,4096]{1,0:T(8,128)(2,1)S(1)}, bf16[8,4096]{1,0:T(8,128)(2,1)S(1)}, u32[]{:S(2)}, u32[]{:S(2)}) %collective-permute-start) | collective-permute-done | bytes 65568 | tf_op jit(solution)/shard_map/ppermute | solution.py:192
  94.8 1.7 collective-permute-start.4
  97.6 6.0 %collective-permute-done.3 = bf16[32,4096]{1,0:T(8,128)(2,1)S(1)} collective-permute-done((bf16[32,4096]{1,0:T(8,128)(2,1)S(1)}, bf16[32,4096]{1,0:T(8,128)(2,1)S(1)}, u32[]{:S(2)}, u32[]{:S(2)}) %collective-permute-start.3) | collective-permute-done | bytes 262176 | tf_op jit(solution)/shard_map/ppermute | solution.py:192
  103.6 2.3 collective-permute-done.4
  105.9 3.2 %collective-permute-done.5 = bf16[32,4096]{1,0:T(8,128)(2,1)S(1)} collective-permute-done((bf16[32,4096]{1,0:T(8,128)(2,1)S(1)}, bf16[32,4096]{1,0:T(8,128)(2,1)S(1)}, u32[]{:S(2)}, u32[]{:S(2)}) %collective-permute-start.5) | collective-permute-done | bytes 262176 | tf_op jit(solution)/shard_map/ppermute | solution.py:192
  109.1 1.9 collective-permute-start.6
  111.2 6.2 %decay.1 = bf16[32,256,512]{2,1,0:T(8,128)(2,1)} custom-call(f32[1,32]{1,0:T(1,128)S(1)} %copy-done.9, f32[1,256]{1,0:T(1,128)S(1)} %copy-done.7, f32[256,1]{1,0:T(8,128)S(1)} %copy.13.forget_col), custom_call_target="tpu_custom_call" | custom-call | tf_op jit(solution)/shard_map/decay/pallas_call | solution.py:242
  117.3 8.8 %state.1 = (bf16[256,4096]{1,0:T(8,128)(2,1)S(1)}, bf16[256,4096]{1,0:T(8,128)(2,1)S(1)}, f32[256,1]{1,0:T(8,128)S(1)}) custom-call(s32[1,264]{1,0:T(1,128)S(1)} %get-tuple-element.12.slots, bf16[128,4,4096]{2,1,0:T(4,128)(2,1)} %copy-done, bf16[32,256,512]{2,1,0:T(8,128)(2,1)} %decay.1, f32[1,4096]{1,0:T(1,128)S(1)} %bitcast.13), custom_call_target="tpu_custom_call" | custom-call | tf_op jit(solution)/shard_map/state/pallas_call | solution.py:264
  128.9 3.9 %loss.1 = (f32[256,1]{1,0:T(8,128)S(1)}, f32[256,1]{1,0:T(8,128)S(1)}, bf16[256,256]{1,0:T(8,128)(2,1)S(1)}, bf16[256,4096]{1,0:T(8,128)(2,1)S(1)}) custom-call(bf16[256,4096]{1,0:T(8,128)(2,1)} %copy-done.1, bf16[128,4096]{1,0:T(8,128)(2,1)S(1)} %constant_dynamic-update-slice_fusion.near, bf16[128,4096]{1,0:T(8,128)(2,1)S(1)} %collective-permute-done.6.far, ...), custom_call_target="tpu_custom_call" | custom-call | tf_op jit(solution)/shard_map/loss/pallas_call | solution.py:282
  133.0 2.6 %collective-permute-done.7 = bf16[128,4096]{1,0:T(8,128)(2,1)S(1)} collective-permute-done((bf16[128,4096]{1,0:T(8,128)(2,1)S(1)}, bf16[128,4096]{1,0:T(8,128)(2,1)S(1)}, u32[]{:S(2)}, u32[]{:S(2)}) %collective-permute-start.7) | collective-permute-done | bytes 1048608 | tf_op jit(solution)/shard_map/ppermute | solution.py:192
  136.1 3.3 %collective-permute-start.9 = (bf16[32,4096]{1,0:T(8,128)(2,1)S(1)}, bf16[32,4096]{1,0:T(8,128)(2,1)S(1)}, u32[]{:S(2)}, u32[]{:S(2)}) collective-permute-start(bf16[32,4096]{1,0:T(8,128)(2,1)S(1)} %get-tuple-element.23), channel_id=1, source_target_pairs={{0,16},{1,17},{2,18},{3,19},{4,20},{5,21},{6,22},{7,23},{8,24},{9,... | collective-permute-start | bytes 786440 | tf_op jit(solution)/shard_map/ppermute | solution.py:192
  139.4 5.6 %collective-permute-done.10 = bf16[32,4096]{1,0:T(8,128)(2,1)S(1)} collective-permute-done((bf16[32,4096]{1,0:T(8,128)(2,1)S(1)}, bf16[32,4096]{1,0:T(8,128)(2,1)S(1)}, u32[]{:S(2)}, u32[]{:S(2)}) %collective-permute-start.10) | collective-permute-done | bytes 262176 | tf_op jit(solution)/shard_map/ppermute | solution.py:192
  145.0 6.3 %collective-permute-done.9 = bf16[32,4096]{1,0:T(8,128)(2,1)S(1)} collective-permute-done((bf16[32,4096]{1,0:T(8,128)(2,1)S(1)}, bf16[32,4096]{1,0:T(8,128)(2,1)S(1)}, u32[]{:S(2)}, u32[]{:S(2)}) %collective-permute-start.9) | collective-permute-done | bytes 262176 | tf_op jit(solution)/shard_map/ppermute | solution.py:192
  152.5 1.9 collective-permute-start.12
  155.8 1.7 collective-permute-done.12
  158.0 4.2 %outgoing.1 = bf16[128,4,4096]{2,1,0:T(4,128)(2,1)} custom-call(s32[1,264]{1,0:T(1,128)S(1)} %get-tuple-element.12.slots, bf16[256,4096]{1,0:T(8,128)(2,1)S(1)} %copy-done.2, f32[256,1]{1,0:T(8,128)S(1)} %get-tuple-element.18.d_pos, bf16[8,4096]{1,0:T(8,128)(2,1)S(1)} %add_convert_fusion.2.neg_grad), custom_call_target="tpu_custom_call" | custom-call | tf_op jit(solution)/shard_map/outgoing/pallas_call | solution.py:293
  162.2 8.0 %all-to-all-start.2 = ((bf16[128,4,4096]{2,1,0:T(4,128)(2,1)}), bf16[128,4,4096]{2,1,0:T(4,128)(2,1)}, u32[]{:S(2)}, u32[]{:S(2)}) async-start(bf16[128,4,4096]{2,1,0:T(4,128)(2,1)} %outgoing.1), calls=%async_computation.2 | async-start | bytes 8388608 | tf_op jit(solution)/shard_map/all_to_all | solution.py:215
  170.9 1.6 copy-done.4
  172.5 3.1 %user_grad.1 = bf16[1,256,4096]{2,1,0:T(8,128)(2,1)} custom-call(bf16[256,4096]{1,0:T(8,128)(2,1)S(1)} %copy-done.4, f32[256,1]{1,0:T(8,128)S(1)} %get-tuple-element.18.d_pos, bf16[256,256]{1,0:T(8,128)(2,1)S(1)} %get-tuple-element.19.d_neg, bf16[128,4096]{1,0:T(8,128)(2,1)S(1)} %constant_dynamic-update-slice_fusion.near, ...), custom_call_target="tpu_custom_call" | custom-call | tf_op jit(solution)/shard_map/user_grad/pallas_call | solution.py:303
  175.6 47.4 %all-to-all-done.2.arrived = bf16[128,4,4096]{2,1,0:T(4,128)(2,1)} async-done(((bf16[128,4,4096]{2,1,0:T(4,128)(2,1)}), bf16[128,4,4096]{2,1,0:T(4,128)(2,1)}, u32[]{:S(2)}, u32[]{:S(2)}) %all-to-all-start.2) | async-done | bytes 4194336 | tf_op jit(solution)/shard_map/all_to_all | solution.py:215
  223.0 7.5 %place.1 = f32[512,4096]{1,0:T(8,128)} custom-call(s32[128,128]{1,0:T(8,128)S(1)} %bitcast.11, bf16[128,4,4096]{2,1,0:T(4,128)(2,1)} %all-to-all-done.2.arrived), custom_call_target="tpu_custom_call" | custom-call | tf_op jit(solution)/shard_map/place/pallas_call | solution.py:317
  (54 shorter events, 16.1 us)
Async XLA Ops:
  1.4 0.7 copy-start.6
  86.8 1.9 copy-start
  88.7 22.3 %copy-start.7 = (f32[1,256]{1,0:T(1,128)S(1)}, f32[1,256]{1,0:T(1,128)}, u32[]{:S(2)}) copy-start(f32[1,256]{1,0:T(1,128)} %forget_row.1) | copy-start | bytes 3076
  88.7 22.4 %copy-start.9 = (f32[1,32]{1,0:T(1,128)S(1)}, f32[1,32]{1,0:T(1,128)}, u32[]{:S(2)}) copy-start(f32[1,32]{1,0:T(1,128)} %speeds.1) | copy-start | bytes 388
  88.7 5.4 %collective-permute-start = (bf16[8,4096]{1,0:T(8,128)(2,1)S(1)}, bf16[8,4096]{1,0:T(8,128)(2,1)S(1)}, u32[]{:S(2)}, u32[]{:S(2)}) collective-permute-start(bf16[8,4096]{1,0:T(8,128)(2,1)S(1)} %own_negatives.1), channel_id=1, source_target_pairs={{0,2},{1,3},{2,4},{3,5},{4,6},{5,7},{6,0},{7,1},{8,10},{9,11},{10,... | collective-permute-start | bytes 196616 | tf_op jit(solution)/shard_map/ppermute | solution.py:192
  88.8 5.4 %collective-permute-start.1 = (bf16[8,4096]{1,0:T(8,128)(2,1)S(1)}, bf16[8,4096]{1,0:T(8,128)(2,1)S(1)}, u32[]{:S(2)}, u32[]{:S(2)}) collective-permute-start(bf16[8,4096]{1,0:T(8,128)(2,1)S(1)} %own_negatives.1), channel_id=1, source_target_pairs={{0,4},{1,5},{2,6},{3,7},{4,0},{5,1},{6,2},{7,3},{8,12},{9,13},{10,... | collective-permute-start | bytes 196616 | tf_op jit(solution)/shard_map/ppermute | solution.py:192
  89.8 4.8 %collective-permute-start.2 = (bf16[8,4096]{1,0:T(8,128)(2,1)S(1)}, bf16[8,4096]{1,0:T(8,128)(2,1)S(1)}, u32[]{:S(2)}, u32[]{:S(2)}) collective-permute-start(bf16[8,4096]{1,0:T(8,128)(2,1)S(1)} %own_negatives.1), channel_id=1, source_target_pairs={{0,6},{1,7},{2,0},{3,1},{4,2},{5,3},{6,4},{7,5},{8,14},{9,15},{10,... | collective-permute-start | bytes 196616 | tf_op jit(solution)/shard_map/ppermute | solution.py:192
  94.7 8.9 %collective-permute-start.3 = (bf16[32,4096]{1,0:T(8,128)(2,1)S(1)}, bf16[32,4096]{1,0:T(8,128)(2,1)S(1)}, u32[]{:S(2)}, u32[]{:S(2)}) collective-permute-start(bf16[32,4096]{1,0:T(8,128)(2,1)S(1)} %pad_maximum_fusion), channel_id=1, source_target_pairs={{0,8},{1,9},{2,10},{3,11},{4,12},{5,13},{6,14},{7,15},{8,16},{9,17... | collective-permute-start | bytes 786440 | tf_op jit(solution)/shard_map/ppermute | solution.py:192
  94.8 11.1 %collective-permute-start.4 = (bf16[32,4096]{1,0:T(8,128)(2,1)S(1)}, bf16[32,4096]{1,0:T(8,128)(2,1)S(1)}, u32[]{:S(2)}, u32[]{:S(2)}) collective-permute-start(bf16[32,4096]{1,0:T(8,128)(2,1)S(1)} %pad_maximum_fusion), channel_id=1, source_target_pairs={{0,16},{1,17},{2,18},{3,19},{4,20},{5,21},{6,22},{7,23},{8,24},{9,... | collective-permute-start | bytes 786440 | tf_op jit(solution)/shard_map/ppermute | solution.py:192
  96.5 12.5 %collective-permute-start.5 = (bf16[32,4096]{1,0:T(8,128)(2,1)S(1)}, bf16[32,4096]{1,0:T(8,128)(2,1)S(1)}, u32[]{:S(2)}, u32[]{:S(2)}) collective-permute-start(bf16[32,4096]{1,0:T(8,128)(2,1)S(1)} %pad_maximum_fusion), channel_id=1, source_target_pairs={{0,24},{1,25},{2,26},{3,27},{4,28},{5,29},{6,30},{7,31},{8,0},{9,1... | collective-permute-start | bytes 786440 | tf_op jit(solution)/shard_map/ppermute | solution.py:192
  109.1 19.8 %collective-permute-start.6 = (bf16[128,4096]{1,0:T(8,128)(2,1)S(1)}, bf16[128,4096]{1,0:T(8,128)(2,1)S(1)}, u32[]{:S(2)}, u32[]{:S(2)}) collective-permute-start(bf16[128,4096]{1,0:T(8,128)(2,1)S(1)} %constant_dynamic-update-slice_fusion.near), channel_id=1, source_target_pairs={{0,1},{1,0},{2,3},{3,2},{4,5},{5,4},{6,7},{7,6},{8,9},{9,8},{10,11... | collective-permute-start | bytes 3145736 | tf_op jit(solution)/shard_map/ppermute | solution.py:192
  111.2 6.2 %copy-start.5 = (f32[4096]{0:T(1024)S(1)}, f32[4096]{0:T(1024)}, u32[]{:S(2)}) copy-start(f32[4096]{0:T(1024)} %param.11) | copy-start | bytes 49156
  126.2 1.3 copy-start.1
  127.5 1.4 copy-start.3
  132.9 2.7 %collective-permute-start.7 = (bf16[128,4096]{1,0:T(8,128)(2,1)S(1)}, bf16[128,4096]{1,0:T(8,128)(2,1)S(1)}, u32[]{:S(2)}, u32[]{:S(2)}) collective-permute-start(bf16[128,4096]{1,0:T(8,128)(2,1)S(1)} %slice.31), channel_id=1, source_target_pairs={{0,1},{1,0},{2,3},{3,2},{4,5},{5,4},{6,7},{7,6},{8,9},{9,8},{10,11... | collective-permute-start | bytes 3145736 | tf_op jit(solution)/shard_map/ppermute | solution.py:192
  135.8 22.1 %copy-start.2 = (bf16[256,4096]{1,0:T(8,128)(2,1)S(1)}, bf16[256,4096]{1,0:T(8,128)(2,1)}, u32[]{:S(2)}) copy-start(bf16[256,4096]{1,0:T(8,128)(2,1)} %copy-done.1) | copy-start | bytes 6291460
  135.9 9.0 %collective-permute-start.10 = (bf16[32,4096]{1,0:T(8,128)(2,1)S(1)}, bf16[32,4096]{1,0:T(8,128)(2,1)S(1)}, u32[]{:S(2)}, u32[]{:S(2)}) collective-permute-start(bf16[32,4096]{1,0:T(8,128)(2,1)S(1)} %get-tuple-element.22), channel_id=1, source_target_pairs={{0,8},{1,9},{2,10},{3,11},{4,12},{5,13},{6,14},{7,15},{8,16},{9,17... | collective-permute-start | bytes 786440 | tf_op jit(solution)/shard_map/ppermute | solution.py:192
  136.1 15.2 %collective-permute-start.9 = (bf16[32,4096]{1,0:T(8,128)(2,1)S(1)}, bf16[32,4096]{1,0:T(8,128)(2,1)S(1)}, u32[]{:S(2)}, u32[]{:S(2)}) collective-permute-start(bf16[32,4096]{1,0:T(8,128)(2,1)S(1)} %get-tuple-element.23), channel_id=1, source_target_pairs={{0,16},{1,17},{2,18},{3,19},{4,20},{5,21},{6,22},{7,23},{8,24},{9,... | collective-permute-start | bytes 786440 | tf_op jit(solution)/shard_map/ppermute | solution.py:192
  139.4 11.9 %collective-permute-start.8 = (bf16[32,4096]{1,0:T(8,128)(2,1)S(1)}, bf16[32,4096]{1,0:T(8,128)(2,1)S(1)}, u32[]{:S(2)}, u32[]{:S(2)}) collective-permute-start(bf16[32,4096]{1,0:T(8,128)(2,1)S(1)} %get-tuple-element.21), channel_id=1, source_target_pairs={{0,24},{1,25},{2,26},{3,27},{4,28},{5,29},{6,30},{7,31},{8,0},{9,1... | collective-permute-start | bytes 786440 | tf_op jit(solution)/shard_map/ppermute | solution.py:192
  151.5 4.4 %collective-permute-start.13 = (bf16[8,4096]{1,0:T(8,128)(2,1)S(1)}, bf16[8,4096]{1,0:T(8,128)(2,1)S(1)}, u32[]{:S(2)}, u32[]{:S(2)}) collective-permute-start(bf16[8,4096]{1,0:T(8,128)(2,1)S(1)} %get-tuple-element.25), channel_id=1, source_target_pairs={{0,2},{1,3},{2,4},{3,5},{4,6},{5,7},{6,0},{7,1},{8,10},{9,11},{10,... | collective-permute-start | bytes 196616 | tf_op jit(solution)/shard_map/ppermute | solution.py:192
  152.5 5.0 %collective-permute-start.12 = (bf16[8,4096]{1,0:T(8,128)(2,1)S(1)}, bf16[8,4096]{1,0:T(8,128)(2,1)S(1)}, u32[]{:S(2)}, u32[]{:S(2)}) collective-permute-start(bf16[8,4096]{1,0:T(8,128)(2,1)S(1)} %get-tuple-element.26), channel_id=1, source_target_pairs={{0,4},{1,5},{2,6},{3,7},{4,0},{5,1},{6,2},{7,3},{8,12},{9,13},{10,... | collective-permute-start | bytes 196616 | tf_op jit(solution)/shard_map/ppermute | solution.py:192
  154.4 3.5 %collective-permute-start.11 = (bf16[8,4096]{1,0:T(8,128)(2,1)S(1)}, bf16[8,4096]{1,0:T(8,128)(2,1)S(1)}, u32[]{:S(2)}, u32[]{:S(2)}) collective-permute-start(bf16[8,4096]{1,0:T(8,128)(2,1)S(1)} %get-tuple-element.24), channel_id=1, source_target_pairs={{0,6},{1,7},{2,0},{3,1},{4,2},{5,3},{6,4},{7,5},{8,14},{9,15},{10,... | collective-permute-start | bytes 196616 | tf_op jit(solution)/shard_map/ppermute | solution.py:192
  162.2 60.8 %all-to-all-start.2 = ((bf16[128,4,4096]{2,1,0:T(4,128)(2,1)}), bf16[128,4,4096]{2,1,0:T(4,128)(2,1)}, u32[]{:S(2)}, u32[]{:S(2)}) async-start(bf16[128,4,4096]{2,1,0:T(4,128)(2,1)} %outgoing.1), calls=%async_computation.2 | async-start | bytes 8388608 | tf_op jit(solution)/shard_map/all_to_all | solution.py:215
  170.9 1.6 copy-start.4
  (1 other events, 0.7 us)
where the time goes:
time: 231 us
  waiting for transfers between devices  79.5 us (34%)
  blocking collectives  78.3 us (34%)
  Pallas kernels  40.8 us (18%)
  starting transfers between devices  22.6 us (10%)
  local copies, waits for them, and re-layouts  7.32 us (3%)
    all_to_all x2, blocking collectives, exchange(): return lax.all_to_all(rows, AXES, split_axis=0, concat_axis=0, tiled=True)  78.3 us
    all_to_all x1, waiting for transfers between devices, exchange(): return lax.all_to_all(rows, AXES, split_axis=0, concat_axis=0, tiled=True)  47.4 us
    ppermute x14, waiting for transfers between devices, shift(): return lax.ppermute(value, 'seq', pairs)  32.1 us
    ppermute x14, starting transfers between devices, shift(): return lax.ppermute(value, 'seq', pairs)  14.6 us
    pallas_call x1, Pallas kernels, on_device(): call(state_kernel, (shape((STEPS, D), BF16), shape((STEPS, D), BF16), sha...  8.82 us
    all_to_all x1, starting transfers between devices, exchange(): return lax.all_to_all(rows, AXES, split_axis=0, concat_axis=0, tiled=True)  8.02 us
    pallas_call x1, Pallas kernels, on_device(): call(place_kernel, shape((ITEMS, D), F32), 'place', grid=grid, in_specs=[...  7.51 us
    unnamed x26, local copies, waits for them, and re-layouts  6.2 us
  transfers between devices with their start and end apart: 15, of which 12 were waited for; matrix products, arithmetic and copies ran while one was open for 0% of the time, Pallas kernels for 8%

commit v1 on v0

--- a/solution.py
+++ b/solution.py
@@ -1,5 +1,3 @@
-import functools
-
 import jax
 import jax.numpy as jnp
 from jax import lax
@@ -19,28 +17,33 @@
 CAP = 4
 SLOTS = DEVICES * CAP
 SIGMA = 4.0 / 64.0
-BLOCK = 1024
+BLOCK = dict(pick=1024, state=1024, base=1024, user_grad=1024, place=1024)
 F32 = jnp.float32
 BF16 = jnp.bfloat16
 I32 = jnp.int32
 AXES = ("dp", "seq")
-PARAMS = pltpu.CompilerParams(vmem_limit_bytes=48 * 2**20)
 
 
 def iota(shape, dim):
     return lax.broadcasted_iota(I32, shape, dim)
 
 
-def call(kernel, out_shape, name, **kw):
-    return pl.pallas_call(kernel, out_shape=out_shape, name=name, compiler_params=PARAMS, **kw)
+def call(kernel, out_shape, name, cost=None, vmem=60, **kw):
+    if cost is not None:
+        flops, size = cost
+        kw["cost_estimate"] = pl.CostEstimate(flops=flops, bytes_accessed=size, transcendentals=0)
+    params = pltpu.CompilerParams(vmem_limit_bytes=vmem * 2**20)
+    return pl.pallas_call(kernel, out_shape=out_shape, name=name, compiler_params=params, **kw)
 
 
 def matmul(a, b, dims):
     return lax.dot_general(a, b, ((dims[0], dims[1]), ((), ())), preferred_element_type=F32)
 
 
-def route_kernel(owner_col, owner_row, item_row, wanted, slots):
-    col, row = owner_col[...], owner_row[...]
+def route_kernel(owner_row, item_row, wanted, slots):
+    row = owner_row[...]
+    same = iota((REQ, REQ), 0) == iota((REQ, REQ), 1)
+    col = jnp.sum(jnp.where(same, row.astype(F32), 0.0), axis=1, keepdims=True).astype(I32)
 
     def key(i):
         return jnp.where(i >= STEPS, i - 2 * STEPS, i)
@@ -50,8 +53,8 @@
     slots[...] = row * CAP + rank
     item = (item_row[...] + 1).astype(F32)
     here = iota((DEVICES, REQ), 0) == row
+    lane = iota((DEVICES, 128), 1)
     out = jnp.full((DEVICES, 128), -1.0, F32)
-    lane = iota((DEVICES, 128), 1)
     for s in range(CAP):
         named = jnp.sum(jnp.where(here & (rank == s), item, 0.0), axis=1, keepdims=True)
         out = jnp.where(lane == s, named - 1.0, out)
@@ -77,21 +80,32 @@
     out[...] = rows.astype(BF16).reshape(out.shape)
 
 
-def place_kernel(asked, arrived, out, hot):
-    @pl.when(pl.program_id(0) == 0)
-    def _():
-        hot[...] = onehot_items(asked[...])
-
-    out[...] = matmul(hot[...], arrived[...].reshape(SLOTS, arrived.shape[2]), ((1,), (0,)))
+def marks_kernel(asked, hot):
+    hot[...] = onehot_items(asked[...])
+
+
+def place_kernel(hot, arrived, out):
+    out[...] = matmul(hot[...], arrived[...].reshape(SLOTS, out.shape[1]), ((1,), (0,)))
 
 
 def onehot_slots(slots):
     return (iota((SLOTS, slots.shape[1]), 0) == slots).astype(F32).astype(BF16)
 
 
-def own_negatives_kernel(slots, rows, out):
-    hot = onehot_slots(slots[:, STEPS:REQ])
-    out[...] = matmul(hot, rows[...].reshape(SLOTS, rows.shape[2]), ((0,), (0,))).astype(BF16)
+def own_negatives_kernel(slots, rows, out, held, sems):
+    copies = []
+    for k in range(OWN_NEG):
+        owner = slots[0, STEPS + k] // CAP
+        copies.append(pltpu.make_async_copy(rows.at[owner], held.at[k], sems.at[k]))
+        copies[-1].start()
+    total = jnp.zeros(out.shape, F32)
+    for k in range(OWN_NEG):
+        copies[k].wait()
+        rank = slots[0, STEPS + k] % CAP
+        tile = jnp.where(iota((CAP, D), 0) == rank, held[k].astype(F32), 0.0)
+        row = jnp.sum(tile, axis=0, keepdims=True)
+        total = jnp.where(iota(out.shape, 0) == k, row, total)
+    out[...] = total.astype(BF16)
 
 
 def decay_kernel(speeds, forget_row, forget_col, out, base):
@@ -146,7 +160,7 @@
         pos_out[...] = SIGMA * jnp.sum(pos, axis=1, keepdims=True)
 
 
-def loss_kernel(rep, near, far, pos_logit, loss, d_pos, d_neg, neg_part):
+def loss_kernel(rep, near, far, pos_logit, loss, d_pos, d_neg, near_part, far_part):
     u = rep[...]
     half = NEG // 2
     logits = [SIGMA * matmul(u, n[...], ((1,), (1,))) for n in (near, far)]
@@ -157,21 +171,48 @@
     valid = jnp.where(iota((STEPS, 1), 0) > 0, 1.0, 0.0)
     loss[...] = (log_total - pos) * valid
     d_pos[...] = (jnp.exp(pos - log_total) - 1.0) * valid
-    for k, l in enumerate(logits):
+    for k, (l, part) in enumerate(zip(logits, (near_part, far_part))):
         share = (jnp.exp(l - log_total) * valid).astype(BF16)
         d_neg[:, k * half : (k + 1) * half] = share
-        neg_part[k * half : (k + 1) * half, :] = (SIGMA * matmul(share, u, ((0,), (0,)))).astype(BF16)
-
-
-def outgoing_kernel(slots, rep, d_pos, neg_grad, out, hot, hot_neg):
+        part[...] = (SIGMA * matmul(share, u, ((0,), (0,)))).astype(BF16)
+
+
+def base_kernel(slots, rep, d_pos, out, hot):
     @pl.when(pl.program_id(0) == 0)
     def _():
         hot[...] = onehot_slots(slots[:, :STEPS])
-        hot_neg[...] = onehot_slots(slots[:, STEPS:REQ])
 
     grad = (SIGMA * d_pos[...] * rep[...].astype(F32)).astype(BF16)
-    rows = matmul(hot[...], grad, ((1,), (0,))) + matmul(hot_neg[...], neg_grad[...], ((1,), (0,)))
-    out[...] = rows.astype(BF16).reshape(out.shape)
+    out[...] = matmul(hot[...], grad, ((1,), (0,))).astype(BF16).reshape(out.shape)
+
+
+def insert_kernel(slots, base, *refs):
+    *parts, out, held, sems = refs
+    owners = [slots[0, STEPS + k] // CAP for k in range(OWN_NEG)]
+    reads = [
+        pltpu.make_async_copy(base.at[owners[k]], held.at[k], sems.at[k]) for k in range(OWN_NEG)
+    ]
+    for copy in reads:
+        copy.start()
+    total = sum(p[...].astype(F32) for p in parts)
+    for copy in reads:
+        copy.wait()
+    firsts = []
+    for k in range(OWN_NEG):
+        first = jnp.int32(k)
+        for j in reversed(range(k)):
+            first = jnp.where(owners[j] == owners[k], j, first)
+        firsts.append(first)
+        rank = slots[0, STEPS + k] % CAP
+        tile = jnp.where(iota((CAP, D), 0) == rank, total[k : k + 1], held[first].astype(F32))
+        held[first] = tile.astype(BF16)
+    writes = [
+        pltpu.make_async_copy(held.at[k], out.at[owners[k]], sems.at[k]) for k in range(OWN_NEG)
+    ]
+    for k, copy in enumerate(writes):
+        pl.when(firsts[k] == k)(copy.start)
+    for k, copy in enumerate(writes):
+        pl.when(firsts[k] == k)(copy.wait)
 
 
 def user_grad_kernel(x, d_pos, d_neg, near, far, out):
@@ -182,33 +223,32 @@
     out[0] = (SIGMA * (d_pos[...] * x[...].astype(F32) + from_neg)).astype(BF16)
 
 
-def shift(value, dx=0, dy=0, core=0):
+def turn(value, stage, by):
     pairs = []
     for x in range(4):
         for y in range(4):
             for c in range(2):
-                to = ((x + dx) % 4 * 4 + (y + dy) % 4) * 2 + (c ^ core)
+                dx, dy = (by, 0) if (stage + c) % 2 else (0, by)
+                to = ((x + dx) % 4 * 4 + (y + dy) % 4) * 2 + c
                 pairs.append(((x * 4 + y) * 2 + c, to))
     return lax.ppermute(value, "seq", pairs)
 
 
-def spread_negatives(own):
-    line = jnp.concatenate([own] + [shift(own, dy=k) for k in (1, 2, 3)], axis=0)
-    near = jnp.concatenate([line] + [shift(line, dx=k) for k in (1, 2, 3)], axis=0)
-    return near, shift(near, core=1)
+def swap(value):
+    return lax.ppermute(value, "seq", [(q, q ^ 1) for q in range(32)])
+
+
+def spread(rows, stage):
+    return jnp.concatenate([rows] + [turn(rows, stage, k) for k in (1, 2, 3)], axis=0)
 
 
 def add(parts):
     return sum(p.astype(F32) for p in parts).astype(BF16)
 
 
-def collect_negatives(part):
-    half = NEG // 2
-    plane = add([part[:half], shift(part[half:], core=1)])
-    n = half // 4
-    line = add([plane[:n]] + [shift(plane[k * n : (k + 1) * n], dx=-k) for k in (1, 2, 3)])
-    n = n // 4
-    return add([line[:n]] + [shift(line[k * n : (k + 1) * n], dy=-k) for k in (1, 2, 3)])
+def collect(rows, stage):
+    n = rows.shape[0] // 4
+    return [rows[:n]] + [turn(rows[k * n : (k + 1) * n], stage, -k) for k in (1, 2, 3)]
 
 
 def exchange(rows):
@@ -219,30 +259,43 @@
     return pl.BlockSpec(shape, lambda j: (0,) * len(shape))
 
 
+def columns(n, name):
+    return pl.BlockSpec((n, BLOCK[name]), lambda j: (0, j))
+
+
+def slot_columns(name):
+    return pl.BlockSpec((DEVICES, CAP, BLOCK[name]), lambda j: (0, 0, j))
+
+
+def over_columns(name):
+    return (D // BLOCK[name],)
+
+
 def on_device(table, home, item, speeds, forget, gain):
-    grid = (D // BLOCK,)
-    columns = lambda n: pl.BlockSpec((n, BLOCK), lambda j: (0, j))
-    slots_block = pl.BlockSpec((DEVICES, CAP, BLOCK), lambda j: (0, 0, j))
     shape = jax.ShapeDtypeStruct
+    slot_rows = shape((DEVICES, CAP, D), BF16)
     wanted, slots = call(
         route_kernel, (shape((DEVICES, 128), I32), shape((1, REQ), I32)), "route"
-    )(home.reshape(REQ, 1), home.reshape(1, REQ), item.reshape(1, REQ))
+    )(home.reshape(1, REQ), item.reshape(1, REQ))
     asked = exchange(wanted.reshape(DEVICES, 1, 128)).reshape(DEVICES, 128)
     picked = call(
         pick_kernel,
-        shape((DEVICES, CAP, D), BF16),
+        slot_rows,
         "pick",
-        grid=grid,
-        in_specs=[whole((DEVICES, 128)), columns(ITEMS)],
-        out_specs=slots_block,
+        grid=over_columns("pick"),
+        in_specs=[whole((DEVICES, 128)), columns(ITEMS, "pick")],
+        out_specs=slot_columns("pick"),
         scratch_shapes=[pltpu.VMEM((ITEMS, SLOTS), BF16)],
     )(asked, table)
+    picked, asked, speeds = lax.optimization_barrier((picked, asked, speeds))
     fetched = exchange(picked)
+    hot = call(marks_kernel, shape((ITEMS, SLOTS), BF16), "marks", cost=(10**6, 2**20))(asked)
     group = 4
     decay = call(
         decay_kernel,
         shape((HEADS, STEPS, 2 * STEPS), BF16),
         "decay",
+        cost=(10**9, 2**23),
         grid=(HEADS // group,),
         in_specs=[
             pl.BlockSpec(memory_space=pltpu.SMEM),
@@ -252,24 +305,31 @@
         out_specs=pl.BlockSpec((group, STEPS, 2 * STEPS), lambda j: (j, 0, 0)),
         scratch_shapes=[pltpu.VMEM((STEPS, STEPS), F32)],
     )(speeds, forget, forget.reshape(STEPS, 1))
+    fetched, decay, hot = lax.optimization_barrier((fetched, decay, hot))
     own = call(
         own_negatives_kernel,
         shape((OWN_NEG, D), BF16),
         "own_negatives",
-        grid=grid,
-        in_specs=[whole((1, REQ)), slots_block],
-        out_specs=columns(OWN_NEG),
+        in_specs=[pl.BlockSpec(memory_space=pltpu.SMEM), pl.BlockSpec(memory_space=pl.ANY)],
+        scratch_shapes=[
+            pltpu.VMEM((OWN_NEG, CAP, D), BF16),
+            pltpu.SemaphoreType.DMA((OWN_NEG,)),
+        ],
     )(slots, fetched)
-    near, far = spread_negatives(own)
+    line = spread(own, 0)
+    line, fetched, decay = lax.optimization_barrier((line, fetched, decay))
+    near = spread(line, 1)
     x, rep, pos_logit = call(
         state_kernel,
         (shape((STEPS, D), BF16), shape((STEPS, D), BF16), shape((STEPS, 1), F32)),
         "state",
-        grid=grid,
+        vmem=40,
+        cost=(3 * 10**9, 20 * 2**20),
+        grid=over_columns("state"),
         in_specs=[
             whole((1, REQ)),
-            slots_block,
-            pl.BlockSpec((BLOCK // HEAD_DIM, STEPS, 2 * STEPS), lambda j: (j, 0, 0)),
+            slot_columns("state"),
+            pl.BlockSpec((BLOCK["state"] // HEAD_DIM, STEPS, 2 * STEPS), lambda j: (j, 0, 0)),
             whole((1, D)),
         ],
         out_specs=(whole((STEPS, D)), whole((STEPS, D)), whole((STEPS, 1))),
@@ -279,50 +339,72 @@
             pltpu.VMEM((STEPS, HEAD_DIM), F32),
         ],
     )(slots, fetched, decay, gain.reshape(1, D))
-    loss, d_pos, d_neg, neg_part = call(
+    near, x, rep, pos_logit = lax.optimization_barrier((near, x, rep, pos_logit))
+    far = swap(near)
+    half_part = shape((NEG // 2, D), BF16)
+    loss, d_pos, d_neg, near_part, far_part = call(
         loss_kernel,
         (
             shape((STEPS, 1), F32),
             shape((STEPS, 1), F32),
             shape((STEPS, NEG), BF16),
-            shape((NEG, D), BF16),
+            half_part,
+            half_part,
         ),
         "loss",
+        vmem=40,
     )(rep, near, far, pos_logit)
-    neg_grad = collect_negatives(neg_part)
+    near_part = add([near_part, swap(far_part)])
+    base = call(
+        base_kernel,
+        slot_rows,
+        "base",
+        cost=(2 * 10**9, 6 * 2**20),
+        grid=over_columns("base"),
+        in_specs=[whole((1, REQ)), columns(STEPS, "base"), whole((STEPS, 1))],
+        out_specs=slot_columns("base"),
+        scratch_shapes=[pltpu.VMEM((SLOTS, STEPS), BF16)],
+    )(slots, rep, d_pos)
+    line_part = add(collect(near_part, 1))
+    base, line_part = lax.optimization_barrier((base, line_part))
+    parts = collect(line_part, 0)
     outgoing = call(
-        outgoing_kernel,
-        shape((DEVICES, CAP, D), BF16),
-        "outgoing",
-        grid=grid,
-        in_specs=[whole((1, REQ)), columns(STEPS), whole((STEPS, 1)), columns(OWN_NEG)],
-        out_specs=slots_block,
-        scratch_shapes=[pltpu.VMEM((SLOTS, STEPS), BF16), pltpu.VMEM((SLOTS, OWN_NEG), BF16)],
-    )(slots, rep, d_pos, neg_grad)
+        insert_kernel,
+        slot_rows,
+        "insert",
+        in_specs=[pl.BlockSpec(memory_space=pltpu.SMEM), pl.BlockSpec(memory_space=pl.ANY)]
+        + [pl.BlockSpec(memory_space=pltpu.VMEM)] * 4,
+        out_specs=pl.BlockSpec(memory_space=pl.ANY),
+        scratch_shapes=[
+            pltpu.VMEM((OWN_NEG, CAP, D), BF16),
+            pltpu.SemaphoreType.DMA((OWN_NEG,)),
+        ],
+        input_output_aliases={1: 0},
+    )(slots, base, *parts)
     arrived = exchange(outgoing)
     user_grad = call(
         user_grad_kernel,
         shape((1, STEPS, D), BF16),
         "user_grad",
-        grid=grid,
+        cost=(10**9, 6 * 2**20),
+        grid=over_columns("user_grad"),
         in_specs=[
-            columns(STEPS),
+            columns(STEPS, "user_grad"),
             whole((STEPS, 1)),
             whole((STEPS, NEG)),
-            columns(NEG // 2),
-            columns(NEG // 2),
-        ],
-        out_specs=pl.BlockSpec((1, STEPS, BLOCK), lambda j: (0, 0, j)),
+            columns(NEG // 2, "user_grad"),
+            columns(NEG // 2, "user_grad"),
+        ],
+        out_specs=pl.BlockSpec((1, STEPS, BLOCK["user_grad"]), lambda j: (0, 0, j)),
     )(x, d_pos, d_neg, near, far)
     item_grad = call(
         place_kernel,
         shape((ITEMS, D), F32),
         "place",
-        grid=grid,
-        in_specs=[whole((DEVICES, 128)), slots_block],
-        out_specs=columns(ITEMS),
-        scratch_shapes=[pltpu.VMEM((ITEMS, SLOTS), BF16)],
-    )(asked, arrived)
+        grid=over_columns("place"),
+        in_specs=[whole((ITEMS, SLOTS)), slot_columns("place")],
+        out_specs=columns(ITEMS, "place"),
+    )(hot, arrived)
     return loss.reshape(1, STEPS), user_grad, item_grad
 
 

time: 231 us -> 213 us (0.922)
  blocking collectives: 78.3 us -> 21.4 us
  waiting for transfers between devices: 79.5 us -> 105 us
  Pallas kernels: 40.8 us -> 50.9 us
  starting transfers between devices: 22.6 us -> 27.8 us
  local copies, waits for them, and re-layouts: 7.32 us -> 3.38 us
    all_to_all x2 -> x1, blocking collectives: 78.3 us -> 21.4 us  [exchange(): return lax.all_to_all(rows, AXES, split_axis=0, concat_axis=0, tiled=True)]
    all_to_all x1 -> x2, waiting for transfers between devices: 47.4 us -> 90.7 us  [exchange(): return lax.all_to_all(rows, AXES, split_axis=0, concat_axis=0, tiled=True)]
    ppermute x14, waiting for transfers between devices: 32.1 us -> 14.6 us  [the longest x12 10 us: turn(): return lax.ppermute(value, 'seq', pairs)]
    pallas_call x6 -> x8, Pallas kernels: 27.9 us -> 38.2 us  [the longest x1 7.25 us: on_device(): call(place_kernel, shape((ITEMS, D), F32), 'place', grid=over_columns('pl...]
    all_to_all x1 -> x2, starting transfers between devices: 8.02 us -> 13.1 us  [exchange(): return lax.all_to_all(rows, AXES, split_axis=0, concat_axis=0, tiled=True)]
    unnamed x26 -> x24, local copies, waits for them, and re-layouts: 6.2 us -> 1.88 us
  transfers between devices with their start and end apart: 15 -> 16, of which waited for: 12 -> 10; matrix products, arithmetic and copies ran while one was open for 0% -> 1% of each run, Pallas kernels for 8% -> 13%
where the time goes in v1:
time: 213 us; the launch traced here: 212 us
  waiting for transfers between devices  105 us (49%)
  Pallas kernels  50.9 us (24%)
  starting transfers between devices  27.8 us (13%)
  blocking collectives  21.4 us (10%)
  local copies, waits for them, and re-layouts  3.38 us (2%)
    all_to_all x2, waiting for transfers between devices, exchange(): return lax.all_to_all(rows, AXES, split_axis=0, concat_axis=0, tiled=True)  90.7 us
    all_to_all x1, blocking collectives, exchange(): return lax.all_to_all(rows, AXES, split_axis=0, concat_axis=0, tiled=True)  21.4 us
    all_to_all x2, starting transfers between devices, exchange(): return lax.all_to_all(rows, AXES, split_axis=0, concat_axis=0, tiled=True)  13.1 us
    ppermute x12, starting transfers between devices, turn(): return lax.ppermute(value, 'seq', pairs)  11.6 us
    ppermute x12, waiting for transfers between devices, turn(): return lax.ppermute(value, 'seq', pairs)  10 us
    pallas_call x1, Pallas kernels, on_device(): call(state_kernel, (shape((STEPS, D), BF16), shape((STEPS, D), BF16), sha...  8.77 us
    pallas_call x1, Pallas kernels, on_device(): call(place_kernel, shape((ITEMS, D), F32), 'place', grid=over_columns('pl...  7.25 us
    pallas_call x1, Pallas kernels, on_device(): call(pick_kernel, slot_rows, 'pick', grid=over_columns('pick'), in_specs=...  6.61 us
  transfers between devices with their start and end apart: 16, of which 10 were waited for; matrix products, arithmetic and copies ran while one was open for 1% of the time, Pallas kernels for 13%

profile of v1, /device:TPU:1, one launch (start us, length us, event | category | flops | bytes accessed | tf_op | source)
XLA Modules:
  0.0 211.7 jit_solution(12861023775849018979)
XLA Ops:
  0.6 1.6 route.1
  2.3 21.4 %all_to_all.15 = s32[128,1,128]{2,1,0:T(1,128)} all-to-all(s32[128,1,128]{2,1,0:T(1,128)} %bitcast.12), channel_id=1, replica_groups=mesh['dp'=4,'seq'=32] {'dp','seq'}, dimensions={0} | all-to-all | bytes 131072 | tf_op jit(solution)/shard_map/all_to_all | solution.py:255
  23.7 6.6 %pick.1 = bf16[128,4,4096]{2,1,0:T(4,128)(2,1)} custom-call(s32[128,128]{1,0:T(8,128)} %bitcast.10, bf16[512,4096]{1,0:T(8,128)(2,1)} %table.1), custom_call_target="tpu_custom_call" | custom-call | tf_op jit(solution)/shard_map/pick/pallas_call | solution.py:281
  30.3 5.5 %all-to-all-start.1 = ((bf16[128,4,4096]{2,1,0:T(4,128)(2,1)}), bf16[128,4,4096]{2,1,0:T(4,128)(2,1)}, u32[]{:S(2)}, u32[]{:S(2)}) async-start(bf16[128,4,4096]{2,1,0:T(4,128)(2,1)} %pick.1), calls=%async_computation.1 | async-start | bytes 8388608 | tf_op jit(solution)/shard_map/all_to_all | solution.py:255
  36.6 2.1 marks.1.hot
  38.7 6.5 %decay.1 = bf16[32,256,512]{2,1,0:T(8,128)(2,1)} custom-call(f32[1,32]{1,0:T(1,128)} %speeds, f32[1,256]{1,0:T(1,128)} %forget_row.1, f32[256,1]{1,0:T(8,128)} %copy.12.forget_col), custom_call_target="tpu_custom_call" | custom-call | flops 1000000000 | bytes 8388608 | tf_op jit(solution)/shard_map/decay/pallas_call | solution.py:294
  45.2 43.5 %all-to-all-done.1.rows = bf16[128,4,4096]{2,1,0:T(4,128)(2,1)} async-done(((bf16[128,4,4096]{2,1,0:T(4,128)(2,1)}), bf16[128,4,4096]{2,1,0:T(4,128)(2,1)}, u32[]{:S(2)}, u32[]{:S(2)}) %all-to-all-start.1) | async-done | bytes 4194336 | tf_op jit(solution)/shard_map/all_to_all | solution.py:255
  88.7 2.7 %own_negatives.1 = bf16[8,4096]{1,0:T(8,128)(2,1)} custom-call(s32[1,264]{1,0:T(1,128)} %get-tuple-element.28.slots, bf16[128,4,4096]{2,1,0:T(4,128)(2,1)} %all-to-all-done.1.rows), custom_call_target="tpu_custom_call" | custom-call | tf_op jit(solution)/shard_map/own_negatives/pallas_call | solution.py:309
  94.8 2.1 collective-permute-done.1
  99.0 2.0 collective-permute-start.4
  101.0 8.8 %state.1 = (bf16[256,4096]{1,0:T(8,128)(2,1)S(1)}, bf16[256,4096]{1,0:T(8,128)(2,1)S(1)}, f32[256,1]{1,0:T(8,128)S(1)}) custom-call(s32[1,264]{1,0:T(1,128)S(1)} %copy-done.7, bf16[128,4,4096]{2,1,0:T(4,128)(2,1)} %all-to-all-done.1.rows, bf16[32,256,512]{2,1,0:T(8,128)(2,1)} %decay.1, f32[1,4096]{1,0:T(1,128)S(1)} %bitcast.9), custom_call_target="tpu_custom_call" | custom-call | flops 3000000000 | bytes 20971520 | tf_op jit(solution)/shard_map/state/pallas_call | solution.py:322
  111.1 2.6 %collective-permute-start.6 = (bf16[128,4096]{1,0:T(8,128)(2,1)S(1)}, bf16[128,4096]{1,0:T(8,128)(2,1)S(1)}, u32[]{:S(2)}, u32[]{:S(2)}) collective-permute-start(bf16[128,4096]{1,0:T(8,128)(2,1)S(1)} %pad_maximum_fusion.near), channel_id=1, source_target_pairs={{0,1},{1,0},{2,3},{3,2},{4,5},{5,4},{6,7},{7,6},{8,9},{9,8},{10,11... | collective-permute-start | bytes 3145736 | tf_op jit(solution)/shard_map/ppermute | solution.py:238
  113.7 2.3 %collective-permute-done.6.far = bf16[128,4096]{1,0:T(8,128)(2,1)S(1)} collective-permute-done((bf16[128,4096]{1,0:T(8,128)(2,1)S(1)}, bf16[128,4096]{1,0:T(8,128)(2,1)S(1)}, u32[]{:S(2)}, u32[]{:S(2)}) %collective-permute-start.6) | collective-permute-done | bytes 1048608 | tf_op jit(solution)/shard_map/ppermute | solution.py:238
  116.0 2.3 %loss.1 = (f32[256,1]{1,0:T(8,128)S(1)}, f32[256,1]{1,0:T(8,128)S(1)}, bf16[256,256]{1,0:T(8,128)(2,1)S(1)}, bf16[128,4096]{1,0:T(8,128)(2,1)S(1)}, bf16[128,4096]{1,0:T(8,128)(2,1)S(1)}) custom-call(bf16[256,4096]{1,0:T(8,128)(2,1)S(1)} %get-tuple-element.41.rep, bf16[128,4096]{1,0:T(8,128)(2,1)S(1)} %pad_maximum_fusion.near, ...), custom_call_target="tpu_custom_call" | custom-call | tf_op jit(solution)/shard_map/loss/pallas_call | solution.py:345
  118.8 2.3 %collective-permute-done.7 = bf16[128,4096]{1,0:T(8,128)(2,1)S(1)} collective-permute-done((bf16[128,4096]{1,0:T(8,128)(2,1)S(1)}, bf16[128,4096]{1,0:T(8,128)(2,1)S(1)}, u32[]{:S(2)}, u32[]{:S(2)}) %collective-permute-start.7) | collective-permute-done | bytes 1048608 | tf_op jit(solution)/shard_map/ppermute | solution.py:238
  124.2 5.2 %base.1 = bf16[128,4,4096]{2,1,0:T(4,128)(2,1)} custom-call(s32[1,264]{1,0:T(1,128)} %get-tuple-element.28.slots, bf16[256,4096]{1,0:T(8,128)(2,1)} %copy-done.3, f32[256,1]{1,0:T(8,128)} %copy-done.4), custom_call_target="tpu_custom_call" | custom-call | flops 2000000000 | bytes 6291456 | tf_op jit(solution)/shard_map/base/pallas_call | solution.py:358
  129.4 2.9 %collective-permute-done.10 = bf16[32,4096]{1,0:T(8,128)(2,1)S(1)} collective-permute-done((bf16[32,4096]{1,0:T(8,128)(2,1)S(1)}, bf16[32,4096]{1,0:T(8,128)(2,1)S(1)}, u32[]{:S(2)}, u32[]{:S(2)}) %collective-permute-start.10) | collective-permute-done | bytes 262176 | tf_op jit(solution)/shard_map/ppermute | solution.py:234
  133.0 1.6 collective-permute-start.13
  134.7 2.3 %collective-permute-start.12 = (bf16[8,4096]{1,0:T(8,128)(2,1)S(1)}, bf16[8,4096]{1,0:T(8,128)(2,1)S(1)}, u32[]{:S(2)}, u32[]{:S(2)}) collective-permute-start(bf16[8,4096]{1,0:T(8,128)(2,1)S(1)} %get-tuple-element.57), channel_id=1, source_target_pairs={{0,4},{1,17},{2,6},{3,19},{4,0},{5,21},{6,2},{7,23},{8,12},{9,25},... | collective-permute-start | bytes 196616 | tf_op jit(solution)/shard_map/ppermute | solution.py:234
  141.1 2.8 %insert.1 = bf16[128,4,4096]{2,1,0:T(4,128)(2,1)} custom-call(s32[1,264]{1,0:T(1,128)} %get-tuple-element.28.slots, bf16[128,4,4096]{2,1,0:T(4,128)(2,1)} %base.1, bf16[8,4096]{1,0:T(8,128)(2,1)} %get-tuple-element.59.refs_0_, bf16[8,4096]{1,0:T(8,128)(2,1)} %copy-done.10, bf16[8,4096]{1,0:T(8,128)(2,1)} %copy-done.9, ...), custom_call_target="tpu_custom_call", output_to_operand_aliasing={{}: (1, {})} | custom-call | tf_op jit(solution)/shard_map/insert/pallas_call | solution.py:371
  143.8 7.7 %all-to-all-start.2 = ((bf16[128,4,4096]{2,1,0:T(4,128)(2,1)}), bf16[128,4,4096]{2,1,0:T(4,128)(2,1)}, u32[]{:S(2)}, u32[]{:S(2)}) async-start(bf16[128,4,4096]{2,1,0:T(4,128)(2,1)} %insert.1), calls=%async_computation.2 | async-start | bytes 8388608 | tf_op jit(solution)/shard_map/all_to_all | solution.py:255
  152.2 5.0 %user_grad.1 = bf16[1,256,4096]{2,1,0:T(8,128)(2,1)} custom-call(bf16[256,4096]{1,0:T(8,128)(2,1)} %copy-done.2, f32[256,1]{1,0:T(8,128)} %copy-done.4, bf16[256,256]{1,0:T(8,128)(2,1)} %copy-done.5, bf16[128,4096]{1,0:T(8,128)(2,1)} %copy-done, bf16[128,4096]{1,0:T(8,128)(2,1)} %copy-done.1), custom_call_target="tpu_custom_call" | custom-call | flops 1000000000 | bytes 6291456 | tf_op jit(solution)/shard_map/user_grad/pallas_call | solution.py:385
  157.2 47.2 %all-to-all-done.2.arrived = bf16[128,4,4096]{2,1,0:T(4,128)(2,1)} async-done(((bf16[128,4,4096]{2,1,0:T(4,128)(2,1)}), bf16[128,4,4096]{2,1,0:T(4,128)(2,1)}, u32[]{:S(2)}, u32[]{:S(2)}) %all-to-all-start.2) | async-done | bytes 4194336 | tf_op jit(solution)/shard_map/all_to_all | solution.py:255
  204.4 7.2 %place.1 = f32[512,4096]{1,0:T(8,128)} custom-call(bf16[512,512]{1,0:T(8,128)(2,1)} %marks.1.hot, bf16[128,4,4096]{2,1,0:T(4,128)(2,1)} %all-to-all-done.2.arrived), custom_call_target="tpu_custom_call" | custom-call | tf_op jit(solution)/shard_map/place/pallas_call | solution.py:400
  (52 shorter events, 16.6 us)
Async XLA Ops:
  30.3 5.5 %copy-start.11 = (f32[1,256]{1,0:T(1,128)S(1)}, f32[1,256]{1,0:T(1,128)}, u32[]{:S(2)}) copy-start(f32[1,256]{1,0:T(1,128)} %forget_row.1) | copy-start | bytes 3076
  30.3 58.4 %all-to-all-start.1 = ((bf16[128,4,4096]{2,1,0:T(4,128)(2,1)}), bf16[128,4,4096]{2,1,0:T(4,128)(2,1)}, u32[]{:S(2)}, u32[]{:S(2)}) async-start(bf16[128,4,4096]{2,1,0:T(4,128)(2,1)} %pick.1), calls=%async_computation.1 | async-start | bytes 8388608 | tf_op jit(solution)/shard_map/all_to_all | solution.py:255
  88.7 12.2 %copy-start.6 = (f32[4096]{0:T(1024)S(1)}, f32[4096]{0:T(1024)}, u32[]{:S(2)}) copy-start(f32[4096]{0:T(1024)} %param.11) | copy-start | bytes 49156
  88.7 12.2 %copy-start.7 = (s32[1,264]{1,0:T(1,128)S(1)}, s32[1,264]{1,0:T(1,128)}, u32[]{:S(2)}) copy-start(s32[1,264]{1,0:T(1,128)} %get-tuple-element.28.slots) | copy-start | bytes 3172
  91.4 3.4 %collective-permute-start.2 = (bf16[8,4096]{1,0:T(8,128)(2,1)}, bf16[8,4096]{1,0:T(8,128)(2,1)S(1)}, u32[]{:S(2)}, u32[]{:S(2)}) collective-permute-start(bf16[8,4096]{1,0:T(8,128)(2,1)} %own_negatives.1), channel_id=1, source_target_pairs={{0,6},{1,25},{2,0},{3,27},{4,2},{5,29},{6,4},{7,31},{8,14},{9,1},{... | collective-permute-start | bytes 196616 | tf_op jit(solution)/shard_map/ppermute | solution.py:234
  92.1 4.8 %collective-permute-start.1 = (bf16[8,4096]{1,0:T(8,128)(2,1)}, bf16[8,4096]{1,0:T(8,128)(2,1)S(1)}, u32[]{:S(2)}, u32[]{:S(2)}) collective-permute-start(bf16[8,4096]{1,0:T(8,128)(2,1)} %own_negatives.1), channel_id=1, source_target_pairs={{0,4},{1,17},{2,6},{3,19},{4,0},{5,21},{6,2},{7,23},{8,12},{9,25},... | collective-permute-start | bytes 196616 | tf_op jit(solution)/shard_map/ppermute | solution.py:234
  93.2 4.8 %collective-permute-start = (bf16[8,4096]{1,0:T(8,128)(2,1)}, bf16[8,4096]{1,0:T(8,128)(2,1)S(1)}, u32[]{:S(2)}, u32[]{:S(2)}) collective-permute-start(bf16[8,4096]{1,0:T(8,128)(2,1)} %own_negatives.1), channel_id=1, source_target_pairs={{0,2},{1,9},{2,4},{3,11},{4,6},{5,13},{6,0},{7,15},{8,10},{9,17},{... | collective-permute-start | bytes 196616 | tf_op jit(solution)/shard_map/ppermute | solution.py:234
  98.9 10.9 %collective-permute-start.5 = (bf16[32,4096]{1,0:T(8,128)(2,1)S(1)}, bf16[32,4096]{1,0:T(8,128)(2,1)S(1)}, u32[]{:S(2)}, u32[]{:S(2)}) collective-permute-start(bf16[32,4096]{1,0:T(8,128)(2,1)S(1)} %pad_maximum_fusion.1), channel_id=1, source_target_pairs={{0,24},{1,7},{2,26},{3,1},{4,28},{5,3},{6,30},{7,5},{8,0},{9,15},{... | collective-permute-start | bytes 786440 | tf_op jit(solution)/shard_map/ppermute | solution.py:234
  99.0 10.8 %collective-permute-start.4 = (bf16[32,4096]{1,0:T(8,128)(2,1)S(1)}, bf16[32,4096]{1,0:T(8,128)(2,1)S(1)}, u32[]{:S(2)}, u32[]{:S(2)}) collective-permute-start(bf16[32,4096]{1,0:T(8,128)(2,1)S(1)} %pad_maximum_fusion.1), channel_id=1, source_target_pairs={{0,16},{1,5},{2,18},{3,7},{4,20},{5,1},{6,22},{7,3},{8,24},{9,13},... | collective-permute-start | bytes 786440 | tf_op jit(solution)/shard_map/ppermute | solution.py:234
  101.0 8.8 %collective-permute-start.3 = (bf16[32,4096]{1,0:T(8,128)(2,1)S(1)}, bf16[32,4096]{1,0:T(8,128)(2,1)S(1)}, u32[]{:S(2)}, u32[]{:S(2)}) collective-permute-start(bf16[32,4096]{1,0:T(8,128)(2,1)S(1)} %pad_maximum_fusion.1), channel_id=1, source_target_pairs={{0,8},{1,3},{2,10},{3,5},{4,12},{5,7},{6,14},{7,1},{8,16},{9,11},{... | collective-permute-start | bytes 786440 | tf_op jit(solution)/shard_map/ppermute | solution.py:234
  109.8 8.5 %copy-start.3 = (bf16[256,4096]{1,0:T(8,128)(2,1)}, bf16[256,4096]{1,0:T(8,128)(2,1)S(1)}, u32[]{:S(2)}) copy-start(bf16[256,4096]{1,0:T(8,128)(2,1)S(1)} %get-tuple-element.41.rep) | copy-start | bytes 6291460
  109.9 8.4 %copy-start = (bf16[128,4096]{1,0:T(8,128)(2,1)}, bf16[128,4096]{1,0:T(8,128)(2,1)S(1)}, u32[]{:S(2)}) copy-start(bf16[128,4096]{1,0:T(8,128)(2,1)S(1)} %pad_maximum_fusion.near) | copy-start | bytes 3145732
  111.1 4.9 %collective-permute-start.6 = (bf16[128,4096]{1,0:T(8,128)(2,1)S(1)}, bf16[128,4096]{1,0:T(8,128)(2,1)S(1)}, u32[]{:S(2)}, u32[]{:S(2)}) collective-permute-start(bf16[128,4096]{1,0:T(8,128)(2,1)S(1)} %pad_maximum_fusion.near), channel_id=1, source_target_pairs={{0,1},{1,0},{2,3},{3,2},{4,5},{5,4},{6,7},{7,6},{8,9},{9,8},{10,11... | collective-permute-start | bytes 3145736 | tf_op jit(solution)/shard_map/ppermute | solution.py:238
  118.3 3.1 %copy-start.4 = (f32[256,1]{1,0:T(8,128)}, f32[256,1]{1,0:T(8,128)S(1)}, u32[]{:S(2)}) copy-start(f32[256,1]{1,0:T(8,128)S(1)} %get-tuple-element.46.d_pos) | copy-start | bytes 3076
  118.3 3.1 %copy-start.5 = (bf16[256,256]{1,0:T(8,128)(2,1)}, bf16[256,256]{1,0:T(8,128)(2,1)S(1)}, u32[]{:S(2)}) copy-start(bf16[256,256]{1,0:T(8,128)(2,1)S(1)} %get-tuple-element.47.d_neg) | copy-start | bytes 393220
  118.3 2.7 %collective-permute-start.7 = (bf16[128,4096]{1,0:T(8,128)(2,1)S(1)}, bf16[128,4096]{1,0:T(8,128)(2,1)S(1)}, u32[]{:S(2)}, u32[]{:S(2)}) collective-permute-start(bf16[128,4096]{1,0:T(8,128)(2,1)S(1)} %get-tuple-element.50), channel_id=1, source_target_pairs={{0,1},{1,0},{2,3},{3,2},{4,5},{5,4},{6,7},{7,6},{8,9},{9,8},{10,11... | collective-permute-start | bytes 3145736 | tf_op jit(solution)/shard_map/ppermute | solution.py:238
  121.4 7.9 %collective-permute-start.8 = (bf16[32,4096]{1,0:T(8,128)(2,1)S(1)}, bf16[32,4096]{1,0:T(8,128)(2,1)S(1)}, u32[]{:S(2)}, u32[]{:S(2)}) collective-permute-start(bf16[32,4096]{1,0:T(8,128)(2,1)S(1)} %get-tuple-element.53), channel_id=1, source_target_pairs={{0,24},{1,7},{2,26},{3,1},{4,28},{5,3},{6,30},{7,5},{8,0},{9,15},{... | collective-permute-start | bytes 786440 | tf_op jit(solution)/shard_map/ppermute | solution.py:234
  122.7 9.5 %collective-permute-start.10 = (bf16[32,4096]{1,0:T(8,128)(2,1)S(1)}, bf16[32,4096]{1,0:T(8,128)(2,1)S(1)}, u32[]{:S(2)}, u32[]{:S(2)}) collective-permute-start(bf16[32,4096]{1,0:T(8,128)(2,1)S(1)} %get-tuple-element.54), channel_id=1, source_target_pairs={{0,8},{1,3},{2,10},{3,5},{4,12},{5,7},{6,14},{7,1},{8,16},{9,11},{... | collective-permute-start | bytes 786440 | tf_op jit(solution)/shard_map/ppermute | solution.py:234
  123.0 9.3 %collective-permute-start.9 = (bf16[32,4096]{1,0:T(8,128)(2,1)S(1)}, bf16[32,4096]{1,0:T(8,128)(2,1)S(1)}, u32[]{:S(2)}, u32[]{:S(2)}) collective-permute-start(bf16[32,4096]{1,0:T(8,128)(2,1)S(1)} %get-tuple-element.55), channel_id=1, source_target_pairs={{0,16},{1,5},{2,18},{3,7},{4,20},{5,1},{6,22},{7,3},{8,24},{9,13},... | collective-permute-start | bytes 786440 | tf_op jit(solution)/shard_map/ppermute | solution.py:234
  133.0 5.1 %collective-permute-start.13 = (bf16[8,4096]{1,0:T(8,128)(2,1)S(1)}, bf16[8,4096]{1,0:T(8,128)(2,1)S(1)}, u32[]{:S(2)}, u32[]{:S(2)}) collective-permute-start(bf16[8,4096]{1,0:T(8,128)(2,1)S(1)} %get-tuple-element.56), channel_id=1, source_target_pairs={{0,2},{1,9},{2,4},{3,11},{4,6},{5,13},{6,0},{7,15},{8,10},{9,17},{... | collective-permute-start | bytes 196616 | tf_op jit(solution)/shard_map/ppermute | solution.py:234
  134.7 4.7 %collective-permute-start.12 = (bf16[8,4096]{1,0:T(8,128)(2,1)S(1)}, bf16[8,4096]{1,0:T(8,128)(2,1)S(1)}, u32[]{:S(2)}, u32[]{:S(2)}) collective-permute-start(bf16[8,4096]{1,0:T(8,128)(2,1)S(1)} %get-tuple-element.57), channel_id=1, source_target_pairs={{0,4},{1,17},{2,6},{3,19},{4,0},{5,21},{6,2},{7,23},{8,12},{9,25},... | collective-permute-start | bytes 196616 | tf_op jit(solution)/shard_map/ppermute | solution.py:234
  137.0 3.4 %collective-permute-start.11 = (bf16[8,4096]{1,0:T(8,128)(2,1)S(1)}, bf16[8,4096]{1,0:T(8,128)(2,1)S(1)}, u32[]{:S(2)}, u32[]{:S(2)}) collective-permute-start(bf16[8,4096]{1,0:T(8,128)(2,1)S(1)} %get-tuple-element.58), channel_id=1, source_target_pairs={{0,6},{1,25},{2,0},{3,27},{4,2},{5,29},{6,4},{7,31},{8,14},{9,1},{... | collective-permute-start | bytes 196616 | tf_op jit(solution)/shard_map/ppermute | solution.py:234
  138.1 2.3 %copy-start.8 = (bf16[8,4096]{1,0:T(8,128)(2,1)}, bf16[8,4096]{1,0:T(8,128)(2,1)S(1)}, u32[]{:S(2)}) copy-start(bf16[8,4096]{1,0:T(8,128)(2,1)S(1)} %collective-permute-done.13.refs_3_) | copy-start | bytes 196612
  143.8 60.6 %all-to-all-start.2 = ((bf16[128,4,4096]{2,1,0:T(4,128)(2,1)}), bf16[128,4,4096]{2,1,0:T(4,128)(2,1)}, u32[]{:S(2)}, u32[]{:S(2)}) async-start(bf16[128,4,4096]{2,1,0:T(4,128)(2,1)} %insert.1), calls=%async_computation.2 | async-start | bytes 8388608 | tf_op jit(solution)/shard_map/all_to_all | solution.py:255
  (4 other events, 5.4 us)

commit v2 on v1

--- a/solution.py
+++ b/solution.py
@@ -17,7 +17,7 @@
 CAP = 4
 SLOTS = DEVICES * CAP
 SIGMA = 4.0 / 64.0
-BLOCK = dict(pick=1024, state=1024, base=1024, user_grad=1024, place=1024)
+BLOCK = dict(pick=1024, state=2048, base=2048, user_grad=2048, place=512)
 F32 = jnp.float32
 BF16 = jnp.bfloat16
 I32 = jnp.int32
@@ -28,7 +28,7 @@
     return lax.broadcasted_iota(I32, shape, dim)
 
 
-def call(kernel, out_shape, name, cost=None, vmem=60, **kw):
+def call(kernel, out_shape, name, cost=None, vmem=40, **kw):
     if cost is not None:
         flops, size = cost
         kw["cost_estimate"] = pl.CostEstimate(flops=flops, bytes_accessed=size, transcendentals=0)
@@ -71,21 +71,28 @@
     return (iota((ITEMS, SLOTS), 0).astype(F32) == row).astype(F32).astype(BF16)
 
 
-def pick_kernel(asked, table, out, hot):
-    @pl.when(pl.program_id(0) == 0)
-    def _():
-        hot[...] = onehot_items(asked[...])
-
-    rows = matmul(hot[...], table[...], ((0,), (0,)))
-    out[...] = rows.astype(BF16).reshape(out.shape)
+def pick_kernel(asked, table, out):
+    hot = onehot_items(asked[...]).astype(F32).T.astype(BF16)
+    width = BLOCK["pick"]
+    for j in range(0, D, width):
+        rows = matmul(hot, table[:, j : j + width], ((1,), (0,)))
+        out[:, :, j : j + width] = rows.astype(BF16).reshape(DEVICES, CAP, width)
 
 
 def marks_kernel(asked, hot):
     hot[...] = onehot_items(asked[...])
 
 
-def place_kernel(hot, arrived, out):
-    out[...] = matmul(hot[...], arrived[...].reshape(SLOTS, out.shape[1]), ((1,), (0,)))
+def place_kernel(hot, arrived, out, held, sems):
+    width = held.shape[2]
+    stores = []
+    for j in range(D // width):
+        part = slice(j * width, (j + 1) * width)
+        held[j] = matmul(hot[...], arrived[:, :, part].reshape(SLOTS, width), ((1,), (0,)))
+        stores.append(pltpu.make_async_copy(held.at[j], out.at[:, part], sems.at[j]))
+        stores[-1].start()
+    for store in stores:
+        store.wait()
 
 
 def onehot_slots(slots):
@@ -108,43 +115,32 @@
     out[...] = total.astype(BF16)
 
 
-def decay_kernel(speeds, forget_row, forget_col, out, base):
+def state_kernel(
+    slots, rows, speeds, forget_row, forget_col, gain, x_out, rep_out, pos_out, hot, base, prior, total
+):
+    j, last = pl.program_id(0), pl.num_programs(0) - 1
+    width = rows.shape[2]
+    heads = width // HEAD_DIM
     step, source = iota((STEPS, STEPS), 0), iota((STEPS, STEPS), 1)
 
-    @pl.when(pl.program_id(0) == 0)
+    @pl.when(j == 0)
     def _():
+        hot[...] = onehot_slots(slots[:, :STEPS])
+        total[...] = jnp.zeros_like(total)
         log_row, log_col = jnp.log(1.0 - forget_row[...]), jnp.log(1.0 - forget_col[...])
         until = jnp.sum(jnp.where(source < step, log_row, 0.0), axis=1, keepdims=True)
         through = jnp.sum(jnp.where(step <= source, log_col, 0.0), axis=0, keepdims=True)
         base[...] = jnp.where(source < step, until - through, -1e30)
 
+    x = matmul(hot[...], rows[...].reshape(SLOTS, width), ((0,), (0,))).astype(BF16)
+    x_out[:, pl.ds(pl.multiple_of(j * width, width), width)] = x
     span = (step - 1 - source).astype(F32)
-    for k in range(out.shape[0]):
-        speed = speeds[0, pl.program_id(0) * out.shape[0] + k]
-        full = jnp.exp(base[...] - speed * span)
+    for k in range(heads):
+        full = jnp.exp(base[...] - speeds[0, j * heads + k] * span)
         high = full.astype(BF16)
-        out[k, :, :STEPS] = high
-        out[k, :, STEPS:] = (full - high.astype(F32)).astype(BF16)
-
-
-def state_kernel(slots, rows, decay, gain, x_out, rep_out, pos_out, hot, prior, total):
-    j, last = pl.program_id(0), pl.num_programs(0) - 1
-    width = rows.shape[2]
-
-    @pl.when(j == 0)
-    def _():
-        hot[...] = onehot_slots(slots[:, :STEPS])
-        total[...] = jnp.zeros_like(total)
-
-    x = matmul(hot[...], rows[...].reshape(SLOTS, width), ((0,), (0,))).astype(BF16)
-    columns = pl.ds(pl.multiple_of(j * width, width), width)
-    x_out[:, columns] = x
-    for k in range(width // HEAD_DIM):
-        part = slice(k * HEAD_DIM, (k + 1) * HEAD_DIM)
-        xk = x[:, part]
-        state = matmul(decay[k, :, :STEPS], xk, ((1,), (0,))) + matmul(
-            decay[k, :, STEPS:], xk, ((1,), (0,))
-        )
+        low = (full - high.astype(F32)).astype(BF16)
+        xk = x[:, k * HEAD_DIM : (k + 1) * HEAD_DIM]
+        state = matmul(high, xk, ((1,), (0,))) + matmul(low, xk, ((1,), (0,)))
         total[...] += state * state
         prior[:, pl.ds(pl.multiple_of(j * width + k * HEAD_DIM, HEAD_DIM), HEAD_DIM)] = state
 
@@ -160,10 +156,14 @@
         pos_out[...] = SIGMA * jnp.sum(pos, axis=1, keepdims=True)
 
 
-def loss_kernel(rep, near, far, pos_logit, loss, d_pos, d_neg, near_part, far_part):
+def logits_kernel(rep, negatives, out):
+    out[...] = SIGMA * matmul(rep[...], negatives[...], ((1,), (1,)))
+
+
+def loss_kernel(rep, near_logit, far, pos_logit, loss, d_pos, d_neg, far_part):
     u = rep[...]
     half = NEG // 2
-    logits = [SIGMA * matmul(u, n[...], ((1,), (1,))) for n in (near, far)]
+    logits = [near_logit[...], SIGMA * matmul(u, far[...], ((1,), (1,)))]
     pos = pos_logit[...]
     top = jnp.maximum(jnp.max(jnp.maximum(*logits), axis=1, keepdims=True), pos)
     summed = sum(jnp.sum(jnp.exp(l - top), axis=1, keepdims=True) for l in logits)
@@ -171,10 +171,14 @@
     valid = jnp.where(iota((STEPS, 1), 0) > 0, 1.0, 0.0)
     loss[...] = (log_total - pos) * valid
     d_pos[...] = (jnp.exp(pos - log_total) - 1.0) * valid
-    for k, (l, part) in enumerate(zip(logits, (near_part, far_part))):
-        share = (jnp.exp(l - log_total) * valid).astype(BF16)
-        d_neg[:, k * half : (k + 1) * half] = share
-        part[...] = (SIGMA * matmul(share, u, ((0,), (0,)))).astype(BF16)
+    shares = [(jnp.exp(l - log_total) * valid).astype(BF16) for l in logits]
+    d_neg[:, :half] = shares[0]
+    d_neg[:, half:] = shares[1]
+    far_part[...] = (SIGMA * matmul(shares[1], u, ((0,), (0,)))).astype(BF16)
+
+
+def near_part_kernel(d_neg, rep, out):
+    out[...] = (SIGMA * matmul(d_neg[:, : NEG // 2], rep[...], ((0,), (0,)))).astype(BF16)
 
 
 def base_kernel(slots, rep, d_pos, out, hot):
@@ -282,30 +286,8 @@
         pick_kernel,
         slot_rows,
         "pick",
-        grid=over_columns("pick"),
-        in_specs=[whole((DEVICES, 128)), columns(ITEMS, "pick")],
-        out_specs=slot_columns("pick"),
-        scratch_shapes=[pltpu.VMEM((ITEMS, SLOTS), BF16)],
     )(asked, table)
-    picked, asked, speeds = lax.optimization_barrier((picked, asked, speeds))
     fetched = exchange(picked)
-    hot = call(marks_kernel, shape((ITEMS, SLOTS), BF16), "marks", cost=(10**6, 2**20))(asked)
-    group = 4
-    decay = call(
-        decay_kernel,
-        shape((HEADS, STEPS, 2 * STEPS), BF16),
-        "decay",
-        cost=(10**9, 2**23),
-        grid=(HEADS // group,),
-        in_specs=[
-            pl.BlockSpec(memory_space=pltpu.SMEM),
-            whole((1, STEPS)),
-            whole((STEPS, 1)),
-        ],
-        out_specs=pl.BlockSpec((group, STEPS, 2 * STEPS), lambda j: (j, 0, 0)),
-        scratch_shapes=[pltpu.VMEM((STEPS, STEPS), F32)],
-    )(speeds, forget, forget.reshape(STEPS, 1))
-    fetched, decay, hot = lax.optimization_barrier((fetched, decay, hot))
     own = call(
         own_negatives_kernel,
         shape((OWN_NEG, D), BF16),
@@ -317,48 +299,54 @@
         ],
     )(slots, fetched)
     line = spread(own, 0)
-    line, fetched, decay = lax.optimization_barrier((line, fetched, decay))
+    line, speeds = lax.optimization_barrier((line, speeds))
     near = spread(line, 1)
     x, rep, pos_logit = call(
         state_kernel,
         (shape((STEPS, D), BF16), shape((STEPS, D), BF16), shape((STEPS, 1), F32)),
         "state",
-        vmem=40,
         cost=(3 * 10**9, 20 * 2**20),
         grid=over_columns("state"),
         in_specs=[
             whole((1, REQ)),
             slot_columns("state"),
-            pl.BlockSpec((BLOCK["state"] // HEAD_DIM, STEPS, 2 * STEPS), lambda j: (j, 0, 0)),
+            pl.BlockSpec(memory_space=pltpu.SMEM),
+            whole((1, STEPS)),
+            whole((STEPS, 1)),
             whole((1, D)),
         ],
         out_specs=(whole((STEPS, D)), whole((STEPS, D)), whole((STEPS, 1))),
         scratch_shapes=[
             pltpu.VMEM((SLOTS, STEPS), BF16),
+            pltpu.VMEM((STEPS, STEPS), F32),
             pltpu.VMEM((STEPS, D), F32),
             pltpu.VMEM((STEPS, HEAD_DIM), F32),
         ],
-    )(slots, fetched, decay, gain.reshape(1, D))
+    )(slots, fetched, speeds, forget, forget.reshape(STEPS, 1), gain.reshape(1, D))
     near, x, rep, pos_logit = lax.optimization_barrier((near, x, rep, pos_logit))
     far = swap(near)
+    near_logit = call(logits_kernel, shape((STEPS, NEG // 2), F32), "near_logits")(rep, near)
+    far, near_logit = lax.optimization_barrier((far, near_logit))
     half_part = shape((NEG // 2, D), BF16)
-    loss, d_pos, d_neg, near_part, far_part = call(
+    loss, d_pos, d_neg, far_part = call(
         loss_kernel,
         (
             shape((STEPS, 1), F32),
             shape((STEPS, 1), F32),
             shape((STEPS, NEG), BF16),
             half_part,
-            half_part,
         ),
         "loss",
-        vmem=40,
-    )(rep, near, far, pos_logit)
-    near_part = add([near_part, swap(far_part)])
+    )(rep, near_logit, far, pos_logit)
+    from_core = swap(far_part)
+    near_part = call(near_part_kernel, half_part, "near_part")(d_neg, rep)
+    from_core, near_part = lax.optimization_barrier((from_core, near_part))
+    near_part = add([near_part, from_core])
     base = call(
         base_kernel,
         slot_rows,
         "base",
+        vmem=62,
         cost=(2 * 10**9, 6 * 2**20),
         grid=over_columns("base"),
         in_specs=[whole((1, REQ)), columns(STEPS, "base"), whole((STEPS, 1))],
@@ -366,22 +354,6 @@
         scratch_shapes=[pltpu.VMEM((SLOTS, STEPS), BF16)],
     )(slots, rep, d_pos)
     line_part = add(collect(near_part, 1))
-    base, line_part = lax.optimization_barrier((base, line_part))
-    parts = collect(line_part, 0)
-    outgoing = call(
-        insert_kernel,
-        slot_rows,
-        "insert",
-        in_specs=[pl.BlockSpec(memory_space=pltpu.SMEM), pl.BlockSpec(memory_space=pl.ANY)]
-        + [pl.BlockSpec(memory_space=pltpu.VMEM)] * 4,
-        out_specs=pl.BlockSpec(memory_space=pl.ANY),
-        scratch_shapes=[
-            pltpu.VMEM((OWN_NEG, CAP, D), BF16),
-            pltpu.SemaphoreType.DMA((OWN_NEG,)),
-        ],
-        input_output_aliases={1: 0},
-    )(slots, base, *parts)
-    arrived = exchange(outgoing)
     user_grad = call(
         user_grad_kernel,
         shape((1, STEPS, D), BF16),
@@ -397,15 +369,39 @@
         ],
         out_specs=pl.BlockSpec((1, STEPS, BLOCK["user_grad"]), lambda j: (0, 0, j)),
     )(x, d_pos, d_neg, near, far)
+    asked, d_pos = lax.optimization_barrier((asked, d_pos))
+    hot = call(marks_kernel, shape((ITEMS, SLOTS), BF16), "marks", cost=(10**6, 2**20))(asked)
+    loss = loss.reshape(1, STEPS)
+    base, user_grad, line_part = lax.optimization_barrier((base, user_grad, line_part))
+    parts = collect(line_part, 0)
+    base, hot, loss = lax.optimization_barrier((base, hot, loss))
+    outgoing = call(
+        insert_kernel,
+        slot_rows,
+        "insert",
+        vmem=62,
+        in_specs=[pl.BlockSpec(memory_space=pltpu.SMEM), pl.BlockSpec(memory_space=pl.ANY)]
+        + [pl.BlockSpec(memory_space=pltpu.VMEM)] * 4,
+        out_specs=pl.BlockSpec(memory_space=pl.ANY),
+        scratch_shapes=[
+            pltpu.VMEM((OWN_NEG, CAP, D), BF16),
+            pltpu.SemaphoreType.DMA((OWN_NEG,)),
+        ],
+        input_output_aliases={1: 0},
+    )(slots, base, *parts)
+    arrived = exchange(outgoing)
     item_grad = call(
         place_kernel,
         shape((ITEMS, D), F32),
         "place",
-        grid=over_columns("place"),
-        in_specs=[whole((ITEMS, SLOTS)), slot_columns("place")],
-        out_specs=columns(ITEMS, "place"),
+        in_specs=[pl.BlockSpec(memory_space=pltpu.VMEM)] * 2,
+        out_specs=pl.BlockSpec(memory_space=pltpu.HBM),
+        scratch_shapes=[
+            pltpu.VMEM((D // BLOCK["place"], ITEMS, BLOCK["place"]), F32),
+            pltpu.SemaphoreType.DMA((D // BLOCK["place"],)),
+        ],
     )(hot, arrived)
-    return loss.reshape(1, STEPS), user_grad, item_grad
+    return loss, user_grad, item_grad
 
 
 def solution(mesh):

time: 213 us -> 203 us (0.953)
  blocking collectives: 21.4 us -> 138 us
  waiting for transfers between devices: 105 us -> 10.6 us
  Pallas kernels: 50.9 us -> 28.2 us
  starting transfers between devices: 27.8 us -> 14.6 us
  local copies, waits for them, and re-layouts: 3.38 us -> 8.61 us
    all_to_all x1 -> x3, blocking collectives: 21.4 us -> 138 us  [exchange(): return lax.all_to_all(rows, AXES, split_axis=0, concat_axis=0, tiled=True)]
    all_to_all x2 -> x0, waiting for transfers between devices: 90.7 us -> none  [exchange(): return lax.all_to_all(rows, AXES, split_axis=0, concat_axis=0, tiled=True)]
    pallas_call x5 -> x6, Pallas kernels: 28.4 us -> 14.7 us  [the longest x1 4.28 us: on_device(): call(base_kernel, slot_rows, 'base', vmem=62, cost=(2 * 10 ** 9, 6 * 2 **...]
    all_to_all x2 -> x0, starting transfers between devices: 13.1 us -> none  [exchange(): return lax.all_to_all(rows, AXES, split_axis=0, concat_axis=0, tiled=True)]
    unnamed x24 -> x28, local copies, waits for them, and re-layouts: 1.88 us -> 6.92 us
    ppermute x12, waiting for transfers between devices: 10 us -> 7.23 us  [turn(): return lax.ppermute(value, 'seq', pairs)]
    pallas_call x1, Pallas kernels: 5.04 us -> 2.68 us  [on_device(): call(user_grad_kernel, shape((1, STEPS, D), BF16), 'user_grad', cost=(10...]
  transfers between devices with their start and end apart: 16 -> 14, of which waited for: 10 -> 8; matrix products, arithmetic and copies ran while one was open for 1% -> 0% of each run, Pallas kernels for 13% -> 8%
where the time goes in v2:
time: 203 us
  blocking collectives  138 us (68%)
  Pallas kernels  28.2 us (14%)
  starting transfers between devices  14.6 us (7%)
  waiting for transfers between devices  10.6 us (5%)
  local copies, waits for them, and re-layouts  8.61 us (4%)
    all_to_all x3, blocking collectives, exchange(): return lax.all_to_all(rows, AXES, split_axis=0, concat_axis=0, tiled=True)  138 us
    ppermute x12, starting transfers between devices, turn(): return lax.ppermute(value, 'seq', pairs)  10.6 us
    ppermute x12, waiting for transfers between devices, turn(): return lax.ppermute(value, 'seq', pairs)  7.23 us
    unnamed x28, local copies, waits for them, and re-layouts  6.92 us
    pallas_call x1, Pallas kernels, on_device(): call(state_kernel, (shape((STEPS, D), BF16), shape((STEPS, D), BF16), sha...  6.68 us
    pallas_call x1, Pallas kernels, on_device(): call(base_kernel, slot_rows, 'base', vmem=62, cost=(2 * 10 ** 9, 6 * 2 **...  4.28 us
  transfers between devices with their start and end apart: 14, of which 8 were waited for; matrix products, arithmetic and copies ran while one was open for 0% of the time, Pallas kernels for 8%

profile of v2, /device:TPU:1, one launch (start us, length us, event | category | flops | bytes accessed | tf_op | source)
XLA Modules:
  0.0 202.6 jit_solution(10196128620192816961)
XLA Ops:
  2.3 20.9 %all_to_all.15 = s32[128,1,128]{2,1,0:T(1,128)S(1)} all-to-all(s32[128,1,128]{2,1,0:T(1,128)S(1)} %bitcast.11), channel_id=1, replica_groups=mesh['dp'=4,'seq'=32] {'dp','seq'}, dimensions={0} | all-to-all | bytes 131072 | tf_op jit(solution)/shard_map/all_to_all | solution.py:259
  23.2 2.2 %copy-done.3 = bf16[512,4096]{1,0:T(8,128)(2,1)S(1)} copy-done((bf16[512,4096]{1,0:T(8,128)(2,1)S(1)}, bf16[512,4096]{1,0:T(8,128)(2,1)}, u32[]{:S(2)}) %copy-start.3) | copy-done | bytes 4194328
  25.4 2.6 %pick.1 = bf16[128,4,4096]{2,1,0:T(4,128)(2,1)S(1)} custom-call(s32[128,128]{1,0:T(8,128)S(1)} %bitcast.9, bf16[512,4096]{1,0:T(8,128)(2,1)S(1)} %copy-done.3), custom_call_target="tpu_custom_call" | custom-call | tf_op jit(solution)/shard_map/pick/pallas_call | solution.py:285
  28.0 57.4 %all_to_all.16.rows = bf16[128,4,4096]{2,1,0:T(4,128)(2,1)S(1)} all-to-all(bf16[128,4,4096]{2,1,0:T(4,128)(2,1)S(1)} %pick.1), channel_id=1, replica_groups=mesh['dp'=4,'seq'=32] {'dp','seq'}, dimensions={0} | all-to-all | bytes 8388608 | tf_op jit(solution)/shard_map/all_to_all | solution.py:259
  85.4 1.5 own_negatives.1
  88.0 1.1 collective-permute-start.1
  89.3 1.3 collective-permute-done.2
  90.5 2.1 %collective-permute-done.1 = bf16[8,4096]{1,0:T(8,128)(2,1)S(1)} collective-permute-done((bf16[8,4096]{1,0:T(8,128)(2,1)S(1)}, bf16[8,4096]{1,0:T(8,128)(2,1)S(1)}, u32[]{:S(2)}, u32[]{:S(2)}) %collective-permute-start.1) | collective-permute-done | bytes 65568 | tf_op jit(solution)/shard_map/ppermute | solution.py:238
  93.8 2.0 %collective-permute-start.4 = (bf16[32,4096]{1,0:T(8,128)(2,1)S(1)}, bf16[32,4096]{1,0:T(8,128)(2,1)S(1)}, u32[]{:S(2)}, u32[]{:S(2)}) collective-permute-start(bf16[32,4096]{1,0:T(8,128)(2,1)S(1)} %pad_maximum_fusion.1), channel_id=1, source_target_pairs={{0,16},{1,5},{2,18},{3,7},{4,20},{5,1},{6,22},{7,3},{8,24},{9,13},... | collective-permute-start | bytes 786440 | tf_op jit(solution)/shard_map/ppermute | solution.py:238
  95.9 2.2 %copy-done.2 = bf16[128,4,4096]{2,1,0:T(4,128)(2,1)S(1)} copy-done((bf16[128,4,4096]{2,1,0:T(4,128)(2,1)S(1)}, bf16[128,4,4096]{2,1,0:T(4,128)(2,1)}, u32[]{:S(2)}) %copy-start.2) | copy-done | bytes 4194328
  98.1 6.7 %state.1 = (bf16[256,4096]{1,0:T(8,128)(2,1)S(1)}, bf16[256,4096]{1,0:T(8,128)(2,1)S(1)}, f32[256,1]{1,0:T(8,128)S(1)}) custom-call(s32[1,264]{1,0:T(1,128)S(1)} %get-tuple-element.29.slots, bf16[128,4,4096]{2,1,0:T(4,128)(2,1)S(1)} %copy-done.2, f32[1,32]{1,0:T(1,128)S(1)} %copy-done.10, f32[1,256]{1,0:T(1,128)S(1)} %copy-done.8, ...), custom_call_target="tpu_custom_call" | custom-call | flops 3000000000 | bytes 20971520 | tf_op jit(solution)/shard_map/state/pallas_call | solution.py:304
  104.9 3.5 %collective-permute-start.6 = (bf16[128,4096]{1,0:T(8,128)(2,1)S(1)}, bf16[128,4096]{1,0:T(8,128)(2,1)S(1)}, u32[]{:S(2)}, u32[]{:S(2)}) collective-permute-start(bf16[128,4096]{1,0:T(8,128)(2,1)S(1)} %pad_maximum_fusion.negatives.near), channel_id=1, source_target_pairs={{0,1},{1,0},{2,3},{3,2},{4,5},{5,4},{6,7},{7,6},{8,9},{9,8},{10,11... | collective-permute-start | bytes 3145736 | tf_op jit(solution)/shard_map/ppermute | solution.py:242
  109.1 1.6 collective-permute-done.6.far
  110.6 2.0 loss.1
  113.6 1.8 collective-permute-done.7
  118.7 2.7 %user_grad.1 = bf16[1,256,4096]{2,1,0:T(8,128)(2,1)} custom-call(bf16[256,4096]{1,0:T(8,128)(2,1)S(1)} %get-tuple-element.42.x, f32[256,1]{1,0:T(8,128)S(1)} %get-tuple-element.41.d_pos, bf16[256,256]{1,0:T(8,128)(2,1)S(1)} %get-tuple-element.43.d_neg, bf16[128,4096]{1,0:T(8,128)(2,1)S(1)} %pad_maximum_fusion.negatives.near, ...), custom_call_target="tpu_custom_call" | custom-call | flops 1000000000 | bytes 6291456 | tf_op jit(solution)/shard_map/user_grad/pallas_call | solution.py:357
  121.4 4.3 %base.1 = bf16[128,4,4096]{2,1,0:T(4,128)(2,1)} custom-call(s32[1,264]{1,0:T(1,128)} %copy-done.5, bf16[256,4096]{1,0:T(8,128)(2,1)} %copy-done, f32[256,1]{1,0:T(8,128)} %copy-done.4), custom_call_target="tpu_custom_call" | custom-call | flops 2000000000 | bytes 6291456 | tf_op jit(solution)/shard_map/base/pallas_call | solution.py:345
  125.6 1.6 collective-permute-done.10
  128.0 1.3 collective-permute-start.13
  129.3 2.3 %collective-permute-start.12 = (bf16[8,4096]{1,0:T(8,128)(2,1)S(1)}, bf16[8,4096]{1,0:T(8,128)(2,1)S(1)}, u32[]{:S(2)}, u32[]{:S(2)}) collective-permute-start(bf16[8,4096]{1,0:T(8,128)(2,1)S(1)} %get-tuple-element.59), channel_id=1, source_target_pairs={{0,4},{1,17},{2,6},{3,19},{4,0},{5,21},{6,2},{7,23},{8,12},{9,25},... | collective-permute-start | bytes 196616 | tf_op jit(solution)/shard_map/ppermute | solution.py:238
  131.6 1.1 collective-permute-start.11
  135.7 2.8 %insert.1 = bf16[128,4,4096]{2,1,0:T(4,128)(2,1)} custom-call(s32[1,264]{1,0:T(1,128)} %copy-done.5, bf16[128,4,4096]{2,1,0:T(4,128)(2,1)} %base.1, bf16[8,4096]{1,0:T(8,128)(2,1)} %get-tuple-element.61.refs_0_, bf16[8,4096]{1,0:T(8,128)(2,1)} %copy-done.13, bf16[8,4096]{1,0:T(8,128)(2,1)} %copy-done.12, ...), custom_call_target="tpu_custom_call", output_to_operand_aliasing={{}: (1, {})} | custom-call | tf_op jit(solution)/shard_map/insert/pallas_call | solution.py:378
  138.4 60.2 %all_to_all.17.arrived = bf16[128,4,4096]{2,1,0:T(4,128)(2,1)S(1)} all-to-all(bf16[128,4,4096]{2,1,0:T(4,128)(2,1)} %insert.1), channel_id=1, replica_groups=mesh['dp'=4,'seq'=32] {'dp','seq'}, dimensions={0} | all-to-all | bytes 8388608 | tf_op jit(solution)/shard_map/all_to_all | solution.py:259
  198.6 3.8 %place.1 = f32[512,4096]{1,0:T(8,128)} custom-call(bf16[512,512]{1,0:T(8,128)(2,1)S(1)} %marks.1.hot, bf16[128,4,4096]{2,1,0:T(4,128)(2,1)S(1)} %all_to_all.17.arrived), custom_call_target="tpu_custom_call" | custom-call | tf_op jit(solution)/shard_map/place/pallas_call | solution.py:393
  (55 shorter events, 12.7 us)
Async XLA Ops:
  2.3 93.6 %copy-start.5 = (s32[1,264]{1,0:T(1,128)}, s32[1,264]{1,0:T(1,128)S(1)}, u32[]{:S(2)}) copy-start(s32[1,264]{1,0:T(1,128)S(1)} %get-tuple-element.29.slots) | copy-start | bytes 3172
  23.2 2.2 %copy-start.3 = (bf16[512,4096]{1,0:T(8,128)(2,1)S(1)}, bf16[512,4096]{1,0:T(8,128)(2,1)}, u32[]{:S(2)}) copy-start(bf16[512,4096]{1,0:T(8,128)(2,1)} %table.1) | copy-start | bytes 12582916
  85.4 2.0 copy-start.1
  85.4 3.7 %copy-start.8 = (f32[1,256]{1,0:T(1,128)S(1)}, f32[1,256]{1,0:T(1,128)}, u32[]{:S(2)}) copy-start(f32[1,256]{1,0:T(1,128)} %forget_row.1) | copy-start | bytes 3076
  85.4 10.4 %copy-start.9 = (f32[4096]{0:T(1024)S(1)}, f32[4096]{0:T(1024)}, u32[]{:S(2)}) copy-start(f32[4096]{0:T(1024)} %param.11) | copy-start | bytes 49156
  85.4 10.4 %copy-start.10 = (f32[1,32]{1,0:T(1,128)S(1)}, f32[1,32]{1,0:T(1,128)}, u32[]{:S(2)}) copy-start(f32[1,32]{1,0:T(1,128)} %speeds) | copy-start | bytes 388
  87.4 3.1 %collective-permute-start.2 = (bf16[8,4096]{1,0:T(8,128)(2,1)S(1)}, bf16[8,4096]{1,0:T(8,128)(2,1)S(1)}, u32[]{:S(2)}, u32[]{:S(2)}) collective-permute-start(bf16[8,4096]{1,0:T(8,128)(2,1)S(1)} %own_negatives.1), channel_id=1, source_target_pairs={{0,6},{1,25},{2,0},{3,27},{4,2},{5,29},{6,4},{7,31},{8,14},{9,1},{... | collective-permute-start | bytes 196616 | tf_op jit(solution)/shard_map/ppermute | solution.py:238
  88.0 4.6 %collective-permute-start.1 = (bf16[8,4096]{1,0:T(8,128)(2,1)S(1)}, bf16[8,4096]{1,0:T(8,128)(2,1)S(1)}, u32[]{:S(2)}, u32[]{:S(2)}) collective-permute-start(bf16[8,4096]{1,0:T(8,128)(2,1)S(1)} %own_negatives.1), channel_id=1, source_target_pairs={{0,4},{1,17},{2,6},{3,19},{4,0},{5,21},{6,2},{7,23},{8,12},{9,25},... | collective-permute-start | bytes 196616 | tf_op jit(solution)/shard_map/ppermute | solution.py:238
  89.1 4.6 %collective-permute-start = (bf16[8,4096]{1,0:T(8,128)(2,1)S(1)}, bf16[8,4096]{1,0:T(8,128)(2,1)S(1)}, u32[]{:S(2)}, u32[]{:S(2)}) collective-permute-start(bf16[8,4096]{1,0:T(8,128)(2,1)S(1)} %own_negatives.1), channel_id=1, source_target_pairs={{0,2},{1,9},{2,4},{3,11},{4,6},{5,13},{6,0},{7,15},{8,10},{9,17},{... | collective-permute-start | bytes 196616 | tf_op jit(solution)/shard_map/ppermute | solution.py:238
  93.7 11.0 %collective-permute-start.5 = (bf16[32,4096]{1,0:T(8,128)(2,1)S(1)}, bf16[32,4096]{1,0:T(8,128)(2,1)S(1)}, u32[]{:S(2)}, u32[]{:S(2)}) collective-permute-start(bf16[32,4096]{1,0:T(8,128)(2,1)S(1)} %pad_maximum_fusion.1), channel_id=1, source_target_pairs={{0,24},{1,7},{2,26},{3,1},{4,28},{5,3},{6,30},{7,5},{8,0},{9,15},{... | collective-permute-start | bytes 786440 | tf_op jit(solution)/shard_map/ppermute | solution.py:238
  93.8 11.0 %collective-permute-start.4 = (bf16[32,4096]{1,0:T(8,128)(2,1)S(1)}, bf16[32,4096]{1,0:T(8,128)(2,1)S(1)}, u32[]{:S(2)}, u32[]{:S(2)}) collective-permute-start(bf16[32,4096]{1,0:T(8,128)(2,1)S(1)} %pad_maximum_fusion.1), channel_id=1, source_target_pairs={{0,16},{1,5},{2,18},{3,7},{4,20},{5,1},{6,22},{7,3},{8,24},{9,13},... | collective-permute-start | bytes 786440 | tf_op jit(solution)/shard_map/ppermute | solution.py:238
  95.8 8.9 %collective-permute-start.3 = (bf16[32,4096]{1,0:T(8,128)(2,1)S(1)}, bf16[32,4096]{1,0:T(8,128)(2,1)S(1)}, u32[]{:S(2)}, u32[]{:S(2)}) collective-permute-start(bf16[32,4096]{1,0:T(8,128)(2,1)S(1)} %pad_maximum_fusion.1), channel_id=1, source_target_pairs={{0,8},{1,3},{2,10},{3,5},{4,12},{5,7},{6,14},{7,1},{8,16},{9,11},{... | collective-permute-start | bytes 786440 | tf_op jit(solution)/shard_map/ppermute | solution.py:238
  95.9 2.2 %copy-start.2 = (bf16[128,4,4096]{2,1,0:T(4,128)(2,1)S(1)}, bf16[128,4,4096]{2,1,0:T(4,128)(2,1)}, u32[]{:S(2)}) copy-start(bf16[128,4,4096]{2,1,0:T(4,128)(2,1)} %copy-done.1) | copy-start | bytes 12582916
  104.7 8.4 %copy-start = (bf16[256,4096]{1,0:T(8,128)(2,1)}, bf16[256,4096]{1,0:T(8,128)(2,1)S(1)}, u32[]{:S(2)}) copy-start(bf16[256,4096]{1,0:T(8,128)(2,1)S(1)} %get-tuple-element.36.rep) | copy-start | bytes 6291460
  104.9 5.8 %collective-permute-start.6 = (bf16[128,4096]{1,0:T(8,128)(2,1)S(1)}, bf16[128,4096]{1,0:T(8,128)(2,1)S(1)}, u32[]{:S(2)}, u32[]{:S(2)}) collective-permute-start(bf16[128,4096]{1,0:T(8,128)(2,1)S(1)} %pad_maximum_fusion.negatives.near), channel_id=1, source_target_pairs={{0,1},{1,0},{2,3},{3,2},{4,5},{5,4},{6,7},{7,6},{8,9},{9,8},{10,11... | collective-permute-start | bytes 3145736 | tf_op jit(solution)/shard_map/ppermute | solution.py:242
  112.7 6.0 %copy-start.4 = (f32[256,1]{1,0:T(8,128)}, f32[256,1]{1,0:T(8,128)S(1)}, u32[]{:S(2)}) copy-start(f32[256,1]{1,0:T(8,128)S(1)} %get-tuple-element.41.d_pos) | copy-start | bytes 3076
  112.7 2.7 %collective-permute-start.7 = (bf16[128,4096]{1,0:T(8,128)(2,1)S(1)}, bf16[128,4096]{1,0:T(8,128)(2,1)S(1)}, u32[]{:S(2)}, u32[]{:S(2)}) collective-permute-start(bf16[128,4096]{1,0:T(8,128)(2,1)S(1)} %get-tuple-element.44), channel_id=1, source_target_pairs={{0,1},{1,0},{2,3},{3,2},{4,5},{5,4},{6,7},{7,6},{8,9},{9,8},{10,11... | collective-permute-start | bytes 3145736 | tf_op jit(solution)/shard_map/ppermute | solution.py:242
  116.6 9.1 %collective-permute-start.8 = (bf16[32,4096]{1,0:T(8,128)(2,1)}, bf16[32,4096]{1,0:T(8,128)(2,1)S(1)}, u32[]{:S(2)}, u32[]{:S(2)}) collective-permute-start(bf16[32,4096]{1,0:T(8,128)(2,1)} %get-tuple-element.55), channel_id=1, source_target_pairs={{0,24},{1,7},{2,26},{3,1},{4,28},{5,3},{6,30},{7,5},{8,0},{9,15},{... | collective-permute-start | bytes 786440 | tf_op jit(solution)/shard_map/ppermute | solution.py:238
  117.5 9.7 %collective-permute-start.10 = (bf16[32,4096]{1,0:T(8,128)(2,1)}, bf16[32,4096]{1,0:T(8,128)(2,1)S(1)}, u32[]{:S(2)}, u32[]{:S(2)}) collective-permute-start(bf16[32,4096]{1,0:T(8,128)(2,1)} %get-tuple-element.56), channel_id=1, source_target_pairs={{0,8},{1,3},{2,10},{3,5},{4,12},{5,7},{6,14},{7,1},{8,16},{9,11},{... | collective-permute-start | bytes 786440 | tf_op jit(solution)/shard_map/ppermute | solution.py:238
  118.1 9.2 %collective-permute-start.9 = (bf16[32,4096]{1,0:T(8,128)(2,1)}, bf16[32,4096]{1,0:T(8,128)(2,1)S(1)}, u32[]{:S(2)}, u32[]{:S(2)}) collective-permute-start(bf16[32,4096]{1,0:T(8,128)(2,1)} %get-tuple-element.57), channel_id=1, source_target_pairs={{0,16},{1,5},{2,18},{3,7},{4,20},{5,1},{6,22},{7,3},{8,24},{9,13},... | collective-permute-start | bytes 786440 | tf_op jit(solution)/shard_map/ppermute | solution.py:238
  128.0 5.8 %collective-permute-start.13 = (bf16[8,4096]{1,0:T(8,128)(2,1)S(1)}, bf16[8,4096]{1,0:T(8,128)(2,1)S(1)}, u32[]{:S(2)}, u32[]{:S(2)}) collective-permute-start(bf16[8,4096]{1,0:T(8,128)(2,1)S(1)} %get-tuple-element.58), channel_id=1, source_target_pairs={{0,2},{1,9},{2,4},{3,11},{4,6},{5,13},{6,0},{7,15},{8,10},{9,17},{... | collective-permute-start | bytes 196616 | tf_op jit(solution)/shard_map/ppermute | solution.py:238
  129.3 4.7 %collective-permute-start.12 = (bf16[8,4096]{1,0:T(8,128)(2,1)S(1)}, bf16[8,4096]{1,0:T(8,128)(2,1)S(1)}, u32[]{:S(2)}, u32[]{:S(2)}) collective-permute-start(bf16[8,4096]{1,0:T(8,128)(2,1)S(1)} %get-tuple-element.59), channel_id=1, source_target_pairs={{0,4},{1,17},{2,6},{3,19},{4,0},{5,21},{6,2},{7,23},{8,12},{9,25},... | collective-permute-start | bytes 196616 | tf_op jit(solution)/shard_map/ppermute | solution.py:238
  131.6 3.4 %collective-permute-start.11 = (bf16[8,4096]{1,0:T(8,128)(2,1)S(1)}, bf16[8,4096]{1,0:T(8,128)(2,1)S(1)}, u32[]{:S(2)}, u32[]{:S(2)}) collective-permute-start(bf16[8,4096]{1,0:T(8,128)(2,1)S(1)} %get-tuple-element.60), channel_id=1, source_target_pairs={{0,6},{1,25},{2,0},{3,27},{4,2},{5,29},{6,4},{7,31},{8,14},{9,1},{... | collective-permute-start | bytes 196616 | tf_op jit(solution)/shard_map/ppermute | solution.py:238
  133.8 1.2 copy-start.11
  (4 other events, 3.1 us)

commit v3 on v2

--- a/solution.py
+++ b/solution.py
@@ -17,7 +17,7 @@
 CAP = 4
 SLOTS = DEVICES * CAP
 SIGMA = 4.0 / 64.0
-BLOCK = dict(pick=1024, state=2048, base=2048, user_grad=2048, place=512)
+BLOCK = dict(pick=1024, state=2048, outgoing=1024, user_grad=2048, place=512)
 F32 = jnp.float32
 BF16 = jnp.bfloat16
 I32 = jnp.int32
@@ -181,42 +181,20 @@
     out[...] = (SIGMA * matmul(d_neg[:, : NEG // 2], rep[...], ((0,), (0,)))).astype(BF16)
 
 
-def base_kernel(slots, rep, d_pos, out, hot):
-    @pl.when(pl.program_id(0) == 0)
-    def _():
-        hot[...] = onehot_slots(slots[:, :STEPS])
-
-    grad = (SIGMA * d_pos[...] * rep[...].astype(F32)).astype(BF16)
-    out[...] = matmul(hot[...], grad, ((1,), (0,))).astype(BF16).reshape(out.shape)
-
-
-def insert_kernel(slots, base, *refs):
-    *parts, out, held, sems = refs
-    owners = [slots[0, STEPS + k] // CAP for k in range(OWN_NEG)]
-    reads = [
-        pltpu.make_async_copy(base.at[owners[k]], held.at[k], sems.at[k]) for k in range(OWN_NEG)
-    ]
-    for copy in reads:
-        copy.start()
-    total = sum(p[...].astype(F32) for p in parts)
-    for copy in reads:
-        copy.wait()
-    firsts = []
+def outgoing_kernel(slots, own_slots, rep, d_pos, *refs):
+    *parts, out = refs
+    hot = onehot_slots(slots[:, :STEPS])
+    width = BLOCK["outgoing"]
+    for j in range(0, D, width):
+        part = slice(j, j + width)
+        grad = (SIGMA * d_pos[...] * rep[:, part].astype(F32)).astype(BF16)
+        rows = matmul(hot, grad, ((1,), (0,))).astype(BF16)
+        out[:, :, part] = rows.reshape(DEVICES, CAP, width)
+    total = sum(p[...].astype(F32) for p in parts).astype(BF16).astype(F32)
     for k in range(OWN_NEG):
-        first = jnp.int32(k)
-        for j in reversed(range(k)):
-            first = jnp.where(owners[j] == owners[k], j, first)
-        firsts.append(first)
-        rank = slots[0, STEPS + k] % CAP
-        tile = jnp.where(iota((CAP, D), 0) == rank, total[k : k + 1], held[first].astype(F32))
-        held[first] = tile.astype(BF16)
-    writes = [
-        pltpu.make_async_copy(held.at[k], out.at[owners[k]], sems.at[k]) for k in range(OWN_NEG)
-    ]
-    for k, copy in enumerate(writes):
-        pl.when(firsts[k] == k)(copy.start)
-    for k, copy in enumerate(writes):
-        pl.when(firsts[k] == k)(copy.wait)
+        owner, rank = own_slots[0, STEPS + k] // CAP, own_slots[0, STEPS + k] % CAP
+        tile = jnp.where(iota((CAP, D), 0) == rank, total[k : k + 1], out[owner].astype(F32))
+        out[owner] = tile.astype(BF16)
 
 
 def user_grad_kernel(x, d_pos, d_neg, near, far, out):
@@ -342,17 +320,6 @@
     near_part = call(near_part_kernel, half_part, "near_part")(d_neg, rep)
     from_core, near_part = lax.optimization_barrier((from_core, near_part))
     near_part = add([near_part, from_core])
-    base = call(
-        base_kernel,
-        slot_rows,
-        "base",
-        vmem=62,
-        cost=(2 * 10**9, 6 * 2**20),
-        grid=over_columns("base"),
-        in_specs=[whole((1, REQ)), columns(STEPS, "base"), whole((STEPS, 1))],
-        out_specs=slot_columns("base"),
-        scratch_shapes=[pltpu.VMEM((SLOTS, STEPS), BF16)],
-    )(slots, rep, d_pos)
     line_part = add(collect(near_part, 1))
     user_grad = call(
         user_grad_kernel,
@@ -372,23 +339,16 @@
     asked, d_pos = lax.optimization_barrier((asked, d_pos))
     hot = call(marks_kernel, shape((ITEMS, SLOTS), BF16), "marks", cost=(10**6, 2**20))(asked)
     loss = loss.reshape(1, STEPS)
-    base, user_grad, line_part = lax.optimization_barrier((base, user_grad, line_part))
+    user_grad, line_part = lax.optimization_barrier((user_grad, line_part))
     parts = collect(line_part, 0)
-    base, hot, loss = lax.optimization_barrier((base, hot, loss))
+    parts, hot, loss = lax.optimization_barrier((parts, hot, loss))
     outgoing = call(
-        insert_kernel,
+        outgoing_kernel,
         slot_rows,
-        "insert",
-        vmem=62,
-        in_specs=[pl.BlockSpec(memory_space=pltpu.SMEM), pl.BlockSpec(memory_space=pl.ANY)]
-        + [pl.BlockSpec(memory_space=pltpu.VMEM)] * 4,
-        out_specs=pl.BlockSpec(memory_space=pl.ANY),
-        scratch_shapes=[
-            pltpu.VMEM((OWN_NEG, CAP, D), BF16),
-            pltpu.SemaphoreType.DMA((OWN_NEG,)),
-        ],
-        input_output_aliases={1: 0},
-    )(slots, base, *parts)
+        "outgoing",
+        in_specs=[pl.BlockSpec(memory_space=pltpu.VMEM), pl.BlockSpec(memory_space=pltpu.SMEM)]
+        + [pl.BlockSpec(memory_space=pltpu.VMEM)] * 6,
+    )(slots, slots, rep, d_pos, *parts)
     arrived = exchange(outgoing)
     item_grad = call(
         place_kernel,

time: 203 us -> 200 us (0.985)
  Pallas kernels: 28.2 us -> 23.3 us
  waiting for transfers between devices: 10.6 us -> 14.6 us
  local copies, waits for them, and re-layouts: 8.61 us -> 6.48 us
    pallas_call x2 -> x1, Pallas kernels: 7.05 us -> 2.14 us  [on_device(): call(outgoing_kernel, slot_rows, 'outgoing', in_specs=[pl.BlockSpec(memor...]
    ppermute x12, waiting for transfers between devices: 7.23 us -> 11.2 us  [turn(): return lax.ppermute(value, 'seq', pairs)]
    unnamed x28 -> x16, local copies, waits for them, and re-layouts: 6.92 us -> 6.28 us
  transfers between devices with their start and end apart: 14 -> 14, of which waited for: 8 -> 9; matrix products, arithmetic and copies ran while one was open for 0% -> 0% of each run, Pallas kernels for 8% -> 5%
where the time goes in v3:
time: 200 us
  blocking collectives  138 us (69%)
  Pallas kernels  23.3 us (12%)
  starting transfers between devices  14.8 us (7%)
  waiting for transfers between devices  14.6 us (7%)
  local copies, waits for them, and re-layouts  6.48 us (3%)
    all_to_all x3, blocking collectives, exchange(): return lax.all_to_all(rows, AXES, split_axis=0, concat_axis=0, tiled=True)  138 us
    ppermute x12, waiting for transfers between devices, turn(): return lax.ppermute(value, 'seq', pairs)  11.2 us
    ppermute x12, starting transfers between devices, turn(): return lax.ppermute(value, 'seq', pairs)  10.8 us
    pallas_call x1, Pallas kernels, on_device(): call(state_kernel, (shape((STEPS, D), BF16), shape((STEPS, D), BF16), sha...  6.69 us
    unnamed x16, local copies, waits for them, and re-layouts  6.28 us
  transfers between devices with their start and end apart: 14, of which 9 were waited for; matrix products, arithmetic and copies ran while one was open for 0% of the time, Pallas kernels for 5%

profile of v3, /device:TPU:1, one launch (start us, length us, event | category | flops | bytes accessed | tf_op | source)
XLA Modules:
  0.0 199.6 jit_solution(785749420354223867)
XLA Ops:
  2.3 20.9 %all_to_all.15 = s32[128,1,128]{2,1,0:T(1,128)S(1)} all-to-all(s32[128,1,128]{2,1,0:T(1,128)S(1)} %bitcast.11), channel_id=1, replica_groups=mesh['dp'=4,'seq'=32] {'dp','seq'}, dimensions={0} | all-to-all | bytes 131072 | tf_op jit(solution)/shard_map/all_to_all | solution.py:237
  23.2 2.2 %copy-done.2 = bf16[512,4096]{1,0:T(8,128)(2,1)S(1)} copy-done((bf16[512,4096]{1,0:T(8,128)(2,1)S(1)}, bf16[512,4096]{1,0:T(8,128)(2,1)}, u32[]{:S(2)}) %copy-start.2) | copy-done | bytes 4194328
  25.4 2.6 %pick.1 = bf16[128,4,4096]{2,1,0:T(4,128)(2,1)S(1)} custom-call(s32[128,128]{1,0:T(8,128)S(1)} %bitcast.9, bf16[512,4096]{1,0:T(8,128)(2,1)S(1)} %copy-done.2), custom_call_target="tpu_custom_call" | custom-call | tf_op jit(solution)/shard_map/pick/pallas_call | solution.py:263
  28.0 57.4 %all_to_all.16.rows = bf16[128,4,4096]{2,1,0:T(4,128)(2,1)S(1)} all-to-all(bf16[128,4,4096]{2,1,0:T(4,128)(2,1)S(1)} %pick.1), channel_id=1, replica_groups=mesh['dp'=4,'seq'=32] {'dp','seq'}, dimensions={0} | all-to-all | bytes 8388608 | tf_op jit(solution)/shard_map/all_to_all | solution.py:237
  85.4 1.5 own_negatives.1
  88.0 1.1 collective-permute-start.1
  89.3 1.3 collective-permute-done.2
  90.5 2.1 %collective-permute-done.1 = bf16[8,4096]{1,0:T(8,128)(2,1)S(1)} collective-permute-done((bf16[8,4096]{1,0:T(8,128)(2,1)S(1)}, bf16[8,4096]{1,0:T(8,128)(2,1)S(1)}, u32[]{:S(2)}, u32[]{:S(2)}) %collective-permute-start.1) | collective-permute-done | bytes 65568 | tf_op jit(solution)/shard_map/ppermute | solution.py:216
  92.6 1.1 collective-permute-done
  93.8 2.0 %collective-permute-start.4 = (bf16[32,4096]{1,0:T(8,128)(2,1)S(1)}, bf16[32,4096]{1,0:T(8,128)(2,1)S(1)}, u32[]{:S(2)}, u32[]{:S(2)}) collective-permute-start(bf16[32,4096]{1,0:T(8,128)(2,1)S(1)} %pad_maximum_fusion.1), channel_id=1, source_target_pairs={{0,16},{1,5},{2,18},{3,7},{4,20},{5,1},{6,22},{7,3},{8,24},{9,13},... | collective-permute-start | bytes 786440 | tf_op jit(solution)/shard_map/ppermute | solution.py:216
  95.9 2.2 %copy-done.1 = bf16[128,4,4096]{2,1,0:T(4,128)(2,1)S(1)} copy-done((bf16[128,4,4096]{2,1,0:T(4,128)(2,1)S(1)}, bf16[128,4,4096]{2,1,0:T(4,128)(2,1)}, u32[]{:S(2)}) %copy-start.1) | copy-done | bytes 4194328
  98.0 6.7 %state.1 = (bf16[256,4096]{1,0:T(8,128)(2,1)S(1)}, bf16[256,4096]{1,0:T(8,128)(2,1)S(1)}, f32[256,1]{1,0:T(8,128)S(1)}) custom-call(s32[1,264]{1,0:T(1,128)S(1)} %get-tuple-element.32.slots.own_slots, bf16[128,4,4096]{2,1,0:T(4,128)(2,1)S(1)} %copy-done.1, f32[1,32]{1,0:T(1,128)S(1)} %copy-done.7, f32[1,256]{1,0:T(1,128)S(1)} %copy-done.5, ...), custom_call_target="tpu_custom_call" | custom-call | flops 3000000000 | bytes 20971520 | tf_op jit(solution)/shard_map/state/pallas_call | solution.py:282
  104.9 3.5 %collective-permute-start.6 = (bf16[128,4096]{1,0:T(8,128)(2,1)S(1)}, bf16[128,4096]{1,0:T(8,128)(2,1)S(1)}, u32[]{:S(2)}, u32[]{:S(2)}) collective-permute-start(bf16[128,4096]{1,0:T(8,128)(2,1)S(1)} %pad_maximum_fusion.negatives.near), channel_id=1, source_target_pairs={{0,1},{1,0},{2,3},{3,2},{4,5},{5,4},{6,7},{7,6},{8,9},{9,8},{10,11... | collective-permute-start | bytes 3145736 | tf_op jit(solution)/shard_map/ppermute | solution.py:220
  109.0 1.6 collective-permute-done.6.far
  110.6 2.0 %loss.1 = (f32[256,1]{1,0:T(8,128)S(1)}, f32[256,1]{1,0:T(8,128)S(1)}, bf16[256,256]{1,0:T(8,128)(2,1)S(1)}, bf16[128,4096]{1,0:T(8,128)(2,1)S(1)}) custom-call(bf16[256,4096]{1,0:T(8,128)(2,1)S(1)} %get-tuple-element.40.rep, f32[256,128]{1,0:T(8,128)S(1)} %near_logits.1.near_logit, bf16[128,4096]{1,0:T(8,128)(2,1)S(1)} %collective-permute-done.6.far, ...), custom_call_target="tpu_custom_call" | custom-call | tf_op jit(solution)/shard_map/loss/pallas_call | solution.py:309
  113.6 1.8 collective-permute-done.7
  117.9 2.7 %user_grad.1 = bf16[1,256,4096]{2,1,0:T(8,128)(2,1)} custom-call(bf16[256,4096]{1,0:T(8,128)(2,1)S(1)} %get-tuple-element.39.x, f32[256,1]{1,0:T(8,128)S(1)} %get-tuple-element.56.d_pos, bf16[256,256]{1,0:T(8,128)(2,1)S(1)} %get-tuple-element.46.d_neg, bf16[128,4096]{1,0:T(8,128)(2,1)S(1)} %pad_maximum_fusion.negatives.near, ...), custom_call_target="tpu_custom_call" | custom-call | flops 1000000000 | bytes 6291456 | tf_op jit(solution)/shard_map/user_grad/pallas_call | solution.py:324
  121.3 4.9 %collective-permute-done.10 = bf16[32,4096]{1,0:T(8,128)(2,1)S(1)} collective-permute-done((bf16[32,4096]{1,0:T(8,128)(2,1)S(1)}, bf16[32,4096]{1,0:T(8,128)(2,1)S(1)}, u32[]{:S(2)}, u32[]{:S(2)}) %collective-permute-start.10) | collective-permute-done | bytes 262176 | tf_op jit(solution)/shard_map/ppermute | solution.py:216
  126.4 1.4 collective-permute-start.13
  127.7 2.3 %collective-permute-start.12 = (bf16[8,4096]{1,0:T(8,128)(2,1)S(1)}, bf16[8,4096]{1,0:T(8,128)(2,1)S(1)}, u32[]{:S(2)}, u32[]{:S(2)}) collective-permute-start(bf16[8,4096]{1,0:T(8,128)(2,1)S(1)} %get-tuple-element.65), channel_id=1, source_target_pairs={{0,4},{1,17},{2,6},{3,19},{4,0},{5,21},{6,2},{7,23},{8,12},{9,25},... | collective-permute-start | bytes 196616 | tf_op jit(solution)/shard_map/ppermute | solution.py:216
  130.0 1.1 collective-permute-start.11
  133.5 2.1 %outgoing.1 = bf16[128,4,4096]{2,1,0:T(4,128)(2,1)S(1)} custom-call(s32[1,264]{1,0:T(1,128)S(1)} %get-tuple-element.32.slots.own_slots, s32[1,264]{1,0:T(1,128)S(1)} %get-tuple-element.32.slots.own_slots, bf16[256,4096]{1,0:T(8,128)(2,1)S(1)} %get-tuple-element.40.rep, f32[256,1]{1,0:T(8,128)S(1)} %get-tuple-element.56.d_pos, ...), custom_call_target="tpu_custom_call" | custom-call | tf_op jit(solution)/shard_map/outgoing/pallas_call | solution.py:345
  135.6 60.0 %all_to_all.17.arrived = bf16[128,4,4096]{2,1,0:T(4,128)(2,1)S(1)} all-to-all(bf16[128,4,4096]{2,1,0:T(4,128)(2,1)S(1)} %outgoing.1), channel_id=1, replica_groups=mesh['dp'=4,'seq'=32] {'dp','seq'}, dimensions={0} | all-to-all | bytes 8388608 | tf_op jit(solution)/shard_map/all_to_all | solution.py:237
  195.6 3.8 %place.1 = f32[512,4096]{1,0:T(8,128)} custom-call(bf16[512,512]{1,0:T(8,128)(2,1)S(1)} %marks.1.hot, bf16[128,4,4096]{2,1,0:T(4,128)(2,1)S(1)} %all_to_all.17.arrived), custom_call_target="tpu_custom_call" | custom-call | tf_op jit(solution)/shard_map/place/pallas_call | solution.py:353
  (42 shorter events, 10.3 us)
Async XLA Ops:
  0.6 0.7 copy-start.3
  1.3 0.7 copy-start.4
  23.2 2.2 %copy-start.2 = (bf16[512,4096]{1,0:T(8,128)(2,1)S(1)}, bf16[512,4096]{1,0:T(8,128)(2,1)}, u32[]{:S(2)}) copy-start(bf16[512,4096]{1,0:T(8,128)(2,1)} %table.1) | copy-start | bytes 12582916
  85.4 2.0 %copy-start = (bf16[128,4,4096]{2,1,0:T(4,128)(2,1)}, bf16[128,4,4096]{2,1,0:T(4,128)(2,1)S(1)}, u32[]{:S(2)}) copy-start(bf16[128,4,4096]{2,1,0:T(4,128)(2,1)S(1)} %all_to_all.16.rows) | copy-start | bytes 12582916
  85.4 3.7 %copy-start.5 = (f32[1,256]{1,0:T(1,128)S(1)}, f32[1,256]{1,0:T(1,128)}, u32[]{:S(2)}) copy-start(f32[1,256]{1,0:T(1,128)} %forget_row.1) | copy-start | bytes 3076
  85.4 10.4 %copy-start.6 = (f32[4096]{0:T(1024)S(1)}, f32[4096]{0:T(1024)}, u32[]{:S(2)}) copy-start(f32[4096]{0:T(1024)} %param.11) | copy-start | bytes 49156
  85.4 10.4 %copy-start.7 = (f32[1,32]{1,0:T(1,128)S(1)}, f32[1,32]{1,0:T(1,128)}, u32[]{:S(2)}) copy-start(f32[1,32]{1,0:T(1,128)} %speeds) | copy-start | bytes 388
  87.4 3.1 %collective-permute-start.2 = (bf16[8,4096]{1,0:T(8,128)(2,1)S(1)}, bf16[8,4096]{1,0:T(8,128)(2,1)S(1)}, u32[]{:S(2)}, u32[]{:S(2)}) collective-permute-start(bf16[8,4096]{1,0:T(8,128)(2,1)S(1)} %own_negatives.1), channel_id=1, source_target_pairs={{0,6},{1,25},{2,0},{3,27},{4,2},{5,29},{6,4},{7,31},{8,14},{9,1},{... | collective-permute-start | bytes 196616 | tf_op jit(solution)/shard_map/ppermute | solution.py:216
  88.0 4.6 %collective-permute-start.1 = (bf16[8,4096]{1,0:T(8,128)(2,1)S(1)}, bf16[8,4096]{1,0:T(8,128)(2,1)S(1)}, u32[]{:S(2)}, u32[]{:S(2)}) collective-permute-start(bf16[8,4096]{1,0:T(8,128)(2,1)S(1)} %own_negatives.1), channel_id=1, source_target_pairs={{0,4},{1,17},{2,6},{3,19},{4,0},{5,21},{6,2},{7,23},{8,12},{9,25},... | collective-permute-start | bytes 196616 | tf_op jit(solution)/shard_map/ppermute | solution.py:216
  89.1 4.6 %collective-permute-start = (bf16[8,4096]{1,0:T(8,128)(2,1)S(1)}, bf16[8,4096]{1,0:T(8,128)(2,1)S(1)}, u32[]{:S(2)}, u32[]{:S(2)}) collective-permute-start(bf16[8,4096]{1,0:T(8,128)(2,1)S(1)} %own_negatives.1), channel_id=1, source_target_pairs={{0,2},{1,9},{2,4},{3,11},{4,6},{5,13},{6,0},{7,15},{8,10},{9,17},{... | collective-permute-start | bytes 196616 | tf_op jit(solution)/shard_map/ppermute | solution.py:216
  93.7 11.0 %collective-permute-start.5 = (bf16[32,4096]{1,0:T(8,128)(2,1)S(1)}, bf16[32,4096]{1,0:T(8,128)(2,1)S(1)}, u32[]{:S(2)}, u32[]{:S(2)}) collective-permute-start(bf16[32,4096]{1,0:T(8,128)(2,1)S(1)} %pad_maximum_fusion.1), channel_id=1, source_target_pairs={{0,24},{1,7},{2,26},{3,1},{4,28},{5,3},{6,30},{7,5},{8,0},{9,15},{... | collective-permute-start | bytes 786440 | tf_op jit(solution)/shard_map/ppermute | solution.py:216
  93.8 11.0 %collective-permute-start.4 = (bf16[32,4096]{1,0:T(8,128)(2,1)S(1)}, bf16[32,4096]{1,0:T(8,128)(2,1)S(1)}, u32[]{:S(2)}, u32[]{:S(2)}) collective-permute-start(bf16[32,4096]{1,0:T(8,128)(2,1)S(1)} %pad_maximum_fusion.1), channel_id=1, source_target_pairs={{0,16},{1,5},{2,18},{3,7},{4,20},{5,1},{6,22},{7,3},{8,24},{9,13},... | collective-permute-start | bytes 786440 | tf_op jit(solution)/shard_map/ppermute | solution.py:216
  95.8 8.9 %collective-permute-start.3 = (bf16[32,4096]{1,0:T(8,128)(2,1)S(1)}, bf16[32,4096]{1,0:T(8,128)(2,1)S(1)}, u32[]{:S(2)}, u32[]{:S(2)}) collective-permute-start(bf16[32,4096]{1,0:T(8,128)(2,1)S(1)} %pad_maximum_fusion.1), channel_id=1, source_target_pairs={{0,8},{1,3},{2,10},{3,5},{4,12},{5,7},{6,14},{7,1},{8,16},{9,11},{... | collective-permute-start | bytes 786440 | tf_op jit(solution)/shard_map/ppermute | solution.py:216
  95.8 2.2 %copy-start.1 = (bf16[128,4,4096]{2,1,0:T(4,128)(2,1)S(1)}, bf16[128,4,4096]{2,1,0:T(4,128)(2,1)}, u32[]{:S(2)}) copy-start(bf16[128,4,4096]{2,1,0:T(4,128)(2,1)} %copy-done) | copy-start | bytes 12582916
  104.9 5.8 %collective-permute-start.6 = (bf16[128,4096]{1,0:T(8,128)(2,1)S(1)}, bf16[128,4096]{1,0:T(8,128)(2,1)S(1)}, u32[]{:S(2)}, u32[]{:S(2)}) collective-permute-start(bf16[128,4096]{1,0:T(8,128)(2,1)S(1)} %pad_maximum_fusion.negatives.near), channel_id=1, source_target_pairs={{0,1},{1,0},{2,3},{3,2},{4,5},{5,4},{6,7},{7,6},{8,9},{9,8},{10,11... | collective-permute-start | bytes 3145736 | tf_op jit(solution)/shard_map/ppermute | solution.py:220
  112.6 2.7 %collective-permute-start.7 = (bf16[128,4096]{1,0:T(8,128)(2,1)S(1)}, bf16[128,4096]{1,0:T(8,128)(2,1)S(1)}, u32[]{:S(2)}, u32[]{:S(2)}) collective-permute-start(bf16[128,4096]{1,0:T(8,128)(2,1)S(1)} %get-tuple-element.47), channel_id=1, source_target_pairs={{0,1},{1,0},{2,3},{3,2},{4,5},{5,4},{6,7},{7,6},{8,9},{9,8},{10,11... | collective-permute-start | bytes 3145736 | tf_op jit(solution)/shard_map/ppermute | solution.py:220
  115.7 5.6 %collective-permute-start.8 = (bf16[32,4096]{1,0:T(8,128)(2,1)S(1)}, bf16[32,4096]{1,0:T(8,128)(2,1)S(1)}, u32[]{:S(2)}, u32[]{:S(2)}) collective-permute-start(bf16[32,4096]{1,0:T(8,128)(2,1)S(1)} %get-tuple-element.61), channel_id=1, source_target_pairs={{0,24},{1,7},{2,26},{3,1},{4,28},{5,3},{6,30},{7,5},{8,0},{9,15},{... | collective-permute-start | bytes 786440 | tf_op jit(solution)/shard_map/ppermute | solution.py:216
  116.7 9.5 %collective-permute-start.10 = (bf16[32,4096]{1,0:T(8,128)(2,1)S(1)}, bf16[32,4096]{1,0:T(8,128)(2,1)S(1)}, u32[]{:S(2)}, u32[]{:S(2)}) collective-permute-start(bf16[32,4096]{1,0:T(8,128)(2,1)S(1)} %get-tuple-element.62), channel_id=1, source_target_pairs={{0,8},{1,3},{2,10},{3,5},{4,12},{5,7},{6,14},{7,1},{8,16},{9,11},{... | collective-permute-start | bytes 786440 | tf_op jit(solution)/shard_map/ppermute | solution.py:216
  117.2 9.0 %collective-permute-start.9 = (bf16[32,4096]{1,0:T(8,128)(2,1)S(1)}, bf16[32,4096]{1,0:T(8,128)(2,1)S(1)}, u32[]{:S(2)}, u32[]{:S(2)}) collective-permute-start(bf16[32,4096]{1,0:T(8,128)(2,1)S(1)} %get-tuple-element.63), channel_id=1, source_target_pairs={{0,16},{1,5},{2,18},{3,7},{4,20},{5,1},{6,22},{7,3},{8,24},{9,13},... | collective-permute-start | bytes 786440 | tf_op jit(solution)/shard_map/ppermute | solution.py:216
  126.4 5.9 %collective-permute-start.13 = (bf16[8,4096]{1,0:T(8,128)(2,1)S(1)}, bf16[8,4096]{1,0:T(8,128)(2,1)S(1)}, u32[]{:S(2)}, u32[]{:S(2)}) collective-permute-start(bf16[8,4096]{1,0:T(8,128)(2,1)S(1)} %get-tuple-element.64), channel_id=1, source_target_pairs={{0,2},{1,9},{2,4},{3,11},{4,6},{5,13},{6,0},{7,15},{8,10},{9,17},{... | collective-permute-start | bytes 196616 | tf_op jit(solution)/shard_map/ppermute | solution.py:216
  127.7 4.7 %collective-permute-start.12 = (bf16[8,4096]{1,0:T(8,128)(2,1)S(1)}, bf16[8,4096]{1,0:T(8,128)(2,1)S(1)}, u32[]{:S(2)}, u32[]{:S(2)}) collective-permute-start(bf16[8,4096]{1,0:T(8,128)(2,1)S(1)} %get-tuple-element.65), channel_id=1, source_target_pairs={{0,4},{1,17},{2,6},{3,19},{4,0},{5,21},{6,2},{7,23},{8,12},{9,25},... | collective-permute-start | bytes 196616 | tf_op jit(solution)/shard_map/ppermute | solution.py:216
  130.0 3.4 %collective-permute-start.11 = (bf16[8,4096]{1,0:T(8,128)(2,1)S(1)}, bf16[8,4096]{1,0:T(8,128)(2,1)S(1)}, u32[]{:S(2)}, u32[]{:S(2)}) collective-permute-start(bf16[8,4096]{1,0:T(8,128)(2,1)S(1)} %get-tuple-element.66), channel_id=1, source_target_pairs={{0,6},{1,25},{2,0},{3,27},{4,2},{5,29},{6,4},{7,31},{8,14},{9,1},{... | collective-permute-start | bytes 196616 | tf_op jit(solution)/shard_map/ppermute | solution.py:216

commit v4 on v3

--- a/solution.py
+++ b/solution.py
@@ -40,7 +40,15 @@
     return lax.dot_general(a, b, ((dims[0], dims[1]), ((), ())), preferred_element_type=F32)
 
 
-def route_kernel(owner_row, item_row, wanted, slots):
+def route_kernel(home, names, table, wanted, slots, near_table, owner_row, item_row, sems):
+    first = pltpu.make_async_copy(home, owner_row, sems.at[0])
+    second = pltpu.make_async_copy(names, item_row, sems.at[1])
+    move = pltpu.make_async_copy(table, near_table, sems.at[2])
+    first.start()
+    second.start()
+    move.start()
+    first.wait()
+    second.wait()
     row = owner_row[...]
     same = iota((REQ, REQ), 0) == iota((REQ, REQ), 1)
     col = jnp.sum(jnp.where(same, row.astype(F32), 0.0), axis=1, keepdims=True).astype(I32)
@@ -59,6 +67,7 @@
         named = jnp.sum(jnp.where(here & (rank == s), item, 0.0), axis=1, keepdims=True)
         out = jnp.where(lane == s, named - 1.0, out)
     wanted[...] = out.astype(I32)
+    move.wait()
 
 
 def onehot_items(asked):
@@ -256,15 +265,30 @@
 def on_device(table, home, item, speeds, forget, gain):
     shape = jax.ShapeDtypeStruct
     slot_rows = shape((DEVICES, CAP, D), BF16)
-    wanted, slots = call(
-        route_kernel, (shape((DEVICES, 128), I32), shape((1, REQ), I32)), "route"
-    )(home.reshape(1, REQ), item.reshape(1, REQ))
+    in_hbm = lambda a: pltpu.with_memory_space_constraint(a, pltpu.HBM)
+    wanted, slots, near_table = call(
+        route_kernel,
+        (shape((DEVICES, 128), I32), shape((1, REQ), I32), pltpu.VMEM((ITEMS, D), BF16)),
+        "route",
+        vmem=16,
+        in_specs=[pl.BlockSpec(memory_space=pltpu.HBM)] * 3,
+        out_specs=(
+            pl.BlockSpec(memory_space=pltpu.VMEM),
+            pl.BlockSpec(memory_space=pltpu.VMEM),
+            pl.BlockSpec(memory_space=pltpu.VMEM),
+        ),
+        scratch_shapes=[
+            pltpu.VMEM((1, REQ), I32),
+            pltpu.VMEM((1, REQ), I32),
+            pltpu.SemaphoreType.DMA((3,)),
+        ],
+    )(in_hbm(home.reshape(1, REQ)), in_hbm(item.reshape(1, REQ)), in_hbm(table))
     asked = exchange(wanted.reshape(DEVICES, 1, 128)).reshape(DEVICES, 128)
     picked = call(
         pick_kernel,
         slot_rows,
         "pick",
-    )(asked, table)
+    )(asked, near_table)
     fetched = exchange(picked)
     own = call(
         own_negatives_kernel,

time: 200 us -> 198 us (0.990)
  local copies, waits for them, and re-layouts: 6.48 us -> 2.94 us
    unnamed x16 -> x10, local copies, waits for them, and re-layouts: 6.28 us -> 2.74 us
  transfers between devices with their start and end apart: 14 -> 14, of which waited for: 9 -> 9; matrix products, arithmetic and copies ran while one was open for 0% -> 0% of each run, Pallas kernels for 5% -> 6%
where the time goes in v4:
time: 198 us
  blocking collectives  138 us (70%)
  Pallas kernels  25.2 us (13%)
  starting transfers between devices  14.8 us (7%)
  waiting for transfers between devices  14.6 us (7%)
  local copies, waits for them, and re-layouts  2.94 us (1%)
    all_to_all x3, blocking collectives, exchange(): return lax.all_to_all(rows, AXES, split_axis=0, concat_axis=0, tiled=True)  138 us
    ppermute x12, waiting for transfers between devices, turn(): return lax.ppermute(value, 'seq', pairs)  11.2 us
    ppermute x12, starting transfers between devices, turn(): return lax.ppermute(value, 'seq', pairs)  10.8 us
    pallas_call x1, Pallas kernels, on_device(): call(state_kernel, (shape((STEPS, D), BF16), shape((STEPS, D), BF16), sha...  6.69 us
  transfers between devices with their start and end apart: 14, of which 9 were waited for; matrix products, arithmetic and copies ran while one was open for 0% of the time, Pallas kernels for 6%

profile of v4, /device:TPU:1, one launch (start us, length us, event | category | flops | bytes accessed | tf_op | source)
XLA Modules:
  0.0 198.0 jit_solution(18402334961829304245)
XLA Ops:
  0.6 2.2 %route.1 = (s32[128,128]{1,0:T(8,128)S(1)}, s32[1,264]{1,0:T(1,128)S(1)}, bf16[512,4096]{1,0:T(8,128)(2,1)S(1)}) custom-call(s32[1,264]{1,0:T(1,128)} %bitcast.14, s32[1,264]{1,0:T(1,128)} %bitcast.15, bf16[512,4096]{1,0:T(8,128)(2,1)} %table.1), custom_call_target="tpu_custom_call" | custom-call | tf_op jit(solution)/shard_map/route/pallas_call | solution.py:269
  2.9 20.9 %all_to_all.15 = s32[128,1,128]{2,1,0:T(1,128)S(1)} all-to-all(s32[128,1,128]{2,1,0:T(1,128)S(1)} %bitcast.11), channel_id=1, replica_groups=mesh['dp'=4,'seq'=32] {'dp','seq'}, dimensions={0} | all-to-all | bytes 131072 | tf_op jit(solution)/shard_map/all_to_all | solution.py:246
  23.8 2.6 %pick.1 = bf16[128,4,4096]{2,1,0:T(4,128)(2,1)S(1)} custom-call(s32[128,128]{1,0:T(8,128)S(1)} %bitcast.9, bf16[512,4096]{1,0:T(8,128)(2,1)S(1)} %get-tuple-element.35.table), custom_call_target="tpu_custom_call" | custom-call | tf_op jit(solution)/shard_map/pick/pallas_call | solution.py:287
  26.4 57.4 %all_to_all.16.rows = bf16[128,4,4096]{2,1,0:T(4,128)(2,1)S(1)} all-to-all(bf16[128,4,4096]{2,1,0:T(4,128)(2,1)S(1)} %pick.1), channel_id=1, replica_groups=mesh['dp'=4,'seq'=32] {'dp','seq'}, dimensions={0} | all-to-all | bytes 8388608 | tf_op jit(solution)/shard_map/all_to_all | solution.py:246
  83.8 1.5 own_negatives.1
  86.4 1.1 collective-permute-start.1
  87.7 1.3 collective-permute-done.2
  88.9 2.1 %collective-permute-done.1 = bf16[8,4096]{1,0:T(8,128)(2,1)S(1)} collective-permute-done((bf16[8,4096]{1,0:T(8,128)(2,1)S(1)}, bf16[8,4096]{1,0:T(8,128)(2,1)S(1)}, u32[]{:S(2)}, u32[]{:S(2)}) %collective-permute-start.1) | collective-permute-done | bytes 65568 | tf_op jit(solution)/shard_map/ppermute | solution.py:225
  91.0 1.1 collective-permute-done
  92.2 2.0 %collective-permute-start.4 = (bf16[32,4096]{1,0:T(8,128)(2,1)S(1)}, bf16[32,4096]{1,0:T(8,128)(2,1)S(1)}, u32[]{:S(2)}, u32[]{:S(2)}) collective-permute-start(bf16[32,4096]{1,0:T(8,128)(2,1)S(1)} %pad_maximum_fusion.1), channel_id=1, source_target_pairs={{0,16},{1,5},{2,18},{3,7},{4,20},{5,1},{6,22},{7,3},{8,24},{9,13},... | collective-permute-start | bytes 786440 | tf_op jit(solution)/shard_map/ppermute | solution.py:225
  94.3 2.2 %copy-done.1 = bf16[128,4,4096]{2,1,0:T(4,128)(2,1)S(1)} copy-done((bf16[128,4,4096]{2,1,0:T(4,128)(2,1)S(1)}, bf16[128,4,4096]{2,1,0:T(4,128)(2,1)}, u32[]{:S(2)}) %copy-start.1) | copy-done | bytes 4194328
  96.4 6.7 %state.1 = (bf16[256,4096]{1,0:T(8,128)(2,1)S(1)}, bf16[256,4096]{1,0:T(8,128)(2,1)S(1)}, f32[256,1]{1,0:T(8,128)S(1)}) custom-call(s32[1,264]{1,0:T(1,128)S(1)} %get-tuple-element.33.slots.own_slots, bf16[128,4,4096]{2,1,0:T(4,128)(2,1)S(1)} %copy-done.1, f32[1,32]{1,0:T(1,128)S(1)} %copy-done.4, f32[1,256]{1,0:T(1,128)S(1)} %copy-done.2, ...), custom_call_target="tpu_custom_call" | custom-call | flops 3000000000 | bytes 20971520 | tf_op jit(solution)/shard_map/state/pallas_call | solution.py:306
  103.3 3.5 %collective-permute-start.6 = (bf16[128,4096]{1,0:T(8,128)(2,1)S(1)}, bf16[128,4096]{1,0:T(8,128)(2,1)S(1)}, u32[]{:S(2)}, u32[]{:S(2)}) collective-permute-start(bf16[128,4096]{1,0:T(8,128)(2,1)S(1)} %pad_maximum_fusion.negatives.near), channel_id=1, source_target_pairs={{0,1},{1,0},{2,3},{3,2},{4,5},{5,4},{6,7},{7,6},{8,9},{9,8},{10,11... | collective-permute-start | bytes 3145736 | tf_op jit(solution)/shard_map/ppermute | solution.py:229
  107.5 1.6 collective-permute-done.6.far
  109.0 2.0 %loss.1 = (f32[256,1]{1,0:T(8,128)S(1)}, f32[256,1]{1,0:T(8,128)S(1)}, bf16[256,256]{1,0:T(8,128)(2,1)S(1)}, bf16[128,4096]{1,0:T(8,128)(2,1)S(1)}) custom-call(bf16[256,4096]{1,0:T(8,128)(2,1)S(1)} %get-tuple-element.42.rep, f32[256,128]{1,0:T(8,128)S(1)} %near_logits.1.near_logit, bf16[128,4096]{1,0:T(8,128)(2,1)S(1)} %collective-permute-done.6.far, ...), custom_call_target="tpu_custom_call" | custom-call | tf_op jit(solution)/shard_map/loss/pallas_call | solution.py:333
  112.0 1.8 collective-permute-done.7
  116.3 2.7 %user_grad.1 = bf16[1,256,4096]{2,1,0:T(8,128)(2,1)} custom-call(bf16[256,4096]{1,0:T(8,128)(2,1)S(1)} %get-tuple-element.41.x, f32[256,1]{1,0:T(8,128)S(1)} %get-tuple-element.58.d_pos, bf16[256,256]{1,0:T(8,128)(2,1)S(1)} %get-tuple-element.48.d_neg, bf16[128,4096]{1,0:T(8,128)(2,1)S(1)} %pad_maximum_fusion.negatives.near, ...), custom_call_target="tpu_custom_call" | custom-call | flops 1000000000 | bytes 6291456 | tf_op jit(solution)/shard_map/user_grad/pallas_call | solution.py:348
  119.7 4.9 %collective-permute-done.10 = bf16[32,4096]{1,0:T(8,128)(2,1)S(1)} collective-permute-done((bf16[32,4096]{1,0:T(8,128)(2,1)S(1)}, bf16[32,4096]{1,0:T(8,128)(2,1)S(1)}, u32[]{:S(2)}, u32[]{:S(2)}) %collective-permute-start.10) | collective-permute-done | bytes 262176 | tf_op jit(solution)/shard_map/ppermute | solution.py:225
  124.8 1.4 collective-permute-start.13
  126.1 2.3 %collective-permute-start.12 = (bf16[8,4096]{1,0:T(8,128)(2,1)S(1)}, bf16[8,4096]{1,0:T(8,128)(2,1)S(1)}, u32[]{:S(2)}, u32[]{:S(2)}) collective-permute-start(bf16[8,4096]{1,0:T(8,128)(2,1)S(1)} %get-tuple-element.67), channel_id=1, source_target_pairs={{0,4},{1,17},{2,6},{3,19},{4,0},{5,21},{6,2},{7,23},{8,12},{9,25},... | collective-permute-start | bytes 196616 | tf_op jit(solution)/shard_map/ppermute | solution.py:225
  128.4 1.1 collective-permute-start.11
  131.9 2.1 %outgoing.1 = bf16[128,4,4096]{2,1,0:T(4,128)(2,1)S(1)} custom-call(s32[1,264]{1,0:T(1,128)S(1)} %get-tuple-element.33.slots.own_slots, s32[1,264]{1,0:T(1,128)S(1)} %get-tuple-element.33.slots.own_slots, bf16[256,4096]{1,0:T(8,128)(2,1)S(1)} %get-tuple-element.42.rep, f32[256,1]{1,0:T(8,128)S(1)} %get-tuple-element.58.d_pos, ...), custom_call_target="tpu_custom_call" | custom-call | tf_op jit(solution)/shard_map/outgoing/pallas_call | solution.py:369
  134.0 60.0 %all_to_all.17.arrived = bf16[128,4,4096]{2,1,0:T(4,128)(2,1)S(1)} all-to-all(bf16[128,4,4096]{2,1,0:T(4,128)(2,1)S(1)} %outgoing.1), channel_id=1, replica_groups=mesh['dp'=4,'seq'=32] {'dp','seq'}, dimensions={0} | all-to-all | bytes 8388608 | tf_op jit(solution)/shard_map/all_to_all | solution.py:246
  194.0 3.8 %place.1 = f32[512,4096]{1,0:T(8,128)} custom-call(bf16[512,512]{1,0:T(8,128)(2,1)S(1)} %marks.1.hot, bf16[128,4,4096]{2,1,0:T(4,128)(2,1)S(1)} %all_to_all.17.arrived), custom_call_target="tpu_custom_call" | custom-call | tf_op jit(solution)/shard_map/place/pallas_call | solution.py:377
  (36 shorter events, 8.7 us)
Async XLA Ops:
  83.8 2.0 %copy-start = (bf16[128,4,4096]{2,1,0:T(4,128)(2,1)}, bf16[128,4,4096]{2,1,0:T(4,128)(2,1)S(1)}, u32[]{:S(2)}) copy-start(bf16[128,4,4096]{2,1,0:T(4,128)(2,1)S(1)} %all_to_all.16.rows) | copy-start | bytes 12582916
  83.8 3.7 %copy-start.2 = (f32[1,256]{1,0:T(1,128)S(1)}, f32[1,256]{1,0:T(1,128)}, u32[]{:S(2)}) copy-start(f32[1,256]{1,0:T(1,128)} %forget_row.1) | copy-start | bytes 3076
  83.8 10.4 %copy-start.3 = (f32[4096]{0:T(1024)S(1)}, f32[4096]{0:T(1024)}, u32[]{:S(2)}) copy-start(f32[4096]{0:T(1024)} %param.11) | copy-start | bytes 49156
  83.8 10.4 %copy-start.4 = (f32[1,32]{1,0:T(1,128)S(1)}, f32[1,32]{1,0:T(1,128)}, u32[]{:S(2)}) copy-start(f32[1,32]{1,0:T(1,128)} %speeds) | copy-start | bytes 388
  85.8 3.1 %collective-permute-start.2 = (bf16[8,4096]{1,0:T(8,128)(2,1)S(1)}, bf16[8,4096]{1,0:T(8,128)(2,1)S(1)}, u32[]{:S(2)}, u32[]{:S(2)}) collective-permute-start(bf16[8,4096]{1,0:T(8,128)(2,1)S(1)} %own_negatives.1), channel_id=1, source_target_pairs={{0,6},{1,25},{2,0},{3,27},{4,2},{5,29},{6,4},{7,31},{8,14},{9,1},{... | collective-permute-start | bytes 196616 | tf_op jit(solution)/shard_map/ppermute | solution.py:225
  86.4 4.6 %collective-permute-start.1 = (bf16[8,4096]{1,0:T(8,128)(2,1)S(1)}, bf16[8,4096]{1,0:T(8,128)(2,1)S(1)}, u32[]{:S(2)}, u32[]{:S(2)}) collective-permute-start(bf16[8,4096]{1,0:T(8,128)(2,1)S(1)} %own_negatives.1), channel_id=1, source_target_pairs={{0,4},{1,17},{2,6},{3,19},{4,0},{5,21},{6,2},{7,23},{8,12},{9,25},... | collective-permute-start | bytes 196616 | tf_op jit(solution)/shard_map/ppermute | solution.py:225
  87.5 4.6 %collective-permute-start = (bf16[8,4096]{1,0:T(8,128)(2,1)S(1)}, bf16[8,4096]{1,0:T(8,128)(2,1)S(1)}, u32[]{:S(2)}, u32[]{:S(2)}) collective-permute-start(bf16[8,4096]{1,0:T(8,128)(2,1)S(1)} %own_negatives.1), channel_id=1, source_target_pairs={{0,2},{1,9},{2,4},{3,11},{4,6},{5,13},{6,0},{7,15},{8,10},{9,17},{... | collective-permute-start | bytes 196616 | tf_op jit(solution)/shard_map/ppermute | solution.py:225
  92.1 11.0 %collective-permute-start.5 = (bf16[32,4096]{1,0:T(8,128)(2,1)S(1)}, bf16[32,4096]{1,0:T(8,128)(2,1)S(1)}, u32[]{:S(2)}, u32[]{:S(2)}) collective-permute-start(bf16[32,4096]{1,0:T(8,128)(2,1)S(1)} %pad_maximum_fusion.1), channel_id=1, source_target_pairs={{0,24},{1,7},{2,26},{3,1},{4,28},{5,3},{6,30},{7,5},{8,0},{9,15},{... | collective-permute-start | bytes 786440 | tf_op jit(solution)/shard_map/ppermute | solution.py:225
  92.2 11.0 %collective-permute-start.4 = (bf16[32,4096]{1,0:T(8,128)(2,1)S(1)}, bf16[32,4096]{1,0:T(8,128)(2,1)S(1)}, u32[]{:S(2)}, u32[]{:S(2)}) collective-permute-start(bf16[32,4096]{1,0:T(8,128)(2,1)S(1)} %pad_maximum_fusion.1), channel_id=1, source_target_pairs={{0,16},{1,5},{2,18},{3,7},{4,20},{5,1},{6,22},{7,3},{8,24},{9,13},... | collective-permute-start | bytes 786440 | tf_op jit(solution)/shard_map/ppermute | solution.py:225
  94.2 8.9 %collective-permute-start.3 = (bf16[32,4096]{1,0:T(8,128)(2,1)S(1)}, bf16[32,4096]{1,0:T(8,128)(2,1)S(1)}, u32[]{:S(2)}, u32[]{:S(2)}) collective-permute-start(bf16[32,4096]{1,0:T(8,128)(2,1)S(1)} %pad_maximum_fusion.1), channel_id=1, source_target_pairs={{0,8},{1,3},{2,10},{3,5},{4,12},{5,7},{6,14},{7,1},{8,16},{9,11},{... | collective-permute-start | bytes 786440 | tf_op jit(solution)/shard_map/ppermute | solution.py:225
  94.3 2.2 %copy-start.1 = (bf16[128,4,4096]{2,1,0:T(4,128)(2,1)S(1)}, bf16[128,4,4096]{2,1,0:T(4,128)(2,1)}, u32[]{:S(2)}) copy-start(bf16[128,4,4096]{2,1,0:T(4,128)(2,1)} %copy-done) | copy-start | bytes 12582916
  103.3 5.8 %collective-permute-start.6 = (bf16[128,4096]{1,0:T(8,128)(2,1)S(1)}, bf16[128,4096]{1,0:T(8,128)(2,1)S(1)}, u32[]{:S(2)}, u32[]{:S(2)}) collective-permute-start(bf16[128,4096]{1,0:T(8,128)(2,1)S(1)} %pad_maximum_fusion.negatives.near), channel_id=1, source_target_pairs={{0,1},{1,0},{2,3},{3,2},{4,5},{5,4},{6,7},{7,6},{8,9},{9,8},{10,11... | collective-permute-start | bytes 3145736 | tf_op jit(solution)/shard_map/ppermute | solution.py:229
  111.0 2.7 %collective-permute-start.7 = (bf16[128,4096]{1,0:T(8,128)(2,1)S(1)}, bf16[128,4096]{1,0:T(8,128)(2,1)S(1)}, u32[]{:S(2)}, u32[]{:S(2)}) collective-permute-start(bf16[128,4096]{1,0:T(8,128)(2,1)S(1)} %get-tuple-element.49), channel_id=1, source_target_pairs={{0,1},{1,0},{2,3},{3,2},{4,5},{5,4},{6,7},{7,6},{8,9},{9,8},{10,11... | collective-permute-start | bytes 3145736 | tf_op jit(solution)/shard_map/ppermute | solution.py:229
  114.1 5.6 %collective-permute-start.8 = (bf16[32,4096]{1,0:T(8,128)(2,1)S(1)}, bf16[32,4096]{1,0:T(8,128)(2,1)S(1)}, u32[]{:S(2)}, u32[]{:S(2)}) collective-permute-start(bf16[32,4096]{1,0:T(8,128)(2,1)S(1)} %get-tuple-element.63), channel_id=1, source_target_pairs={{0,24},{1,7},{2,26},{3,1},{4,28},{5,3},{6,30},{7,5},{8,0},{9,15},{... | collective-permute-start | bytes 786440 | tf_op jit(solution)/shard_map/ppermute | solution.py:225
  115.1 9.5 %collective-permute-start.10 = (bf16[32,4096]{1,0:T(8,128)(2,1)S(1)}, bf16[32,4096]{1,0:T(8,128)(2,1)S(1)}, u32[]{:S(2)}, u32[]{:S(2)}) collective-permute-start(bf16[32,4096]{1,0:T(8,128)(2,1)S(1)} %get-tuple-element.64), channel_id=1, source_target_pairs={{0,8},{1,3},{2,10},{3,5},{4,12},{5,7},{6,14},{7,1},{8,16},{9,11},{... | collective-permute-start | bytes 786440 | tf_op jit(solution)/shard_map/ppermute | solution.py:225
  115.6 9.0 %collective-permute-start.9 = (bf16[32,4096]{1,0:T(8,128)(2,1)S(1)}, bf16[32,4096]{1,0:T(8,128)(2,1)S(1)}, u32[]{:S(2)}, u32[]{:S(2)}) collective-permute-start(bf16[32,4096]{1,0:T(8,128)(2,1)S(1)} %get-tuple-element.65), channel_id=1, source_target_pairs={{0,16},{1,5},{2,18},{3,7},{4,20},{5,1},{6,22},{7,3},{8,24},{9,13},... | collective-permute-start | bytes 786440 | tf_op jit(solution)/shard_map/ppermute | solution.py:225
  124.8 5.9 %collective-permute-start.13 = (bf16[8,4096]{1,0:T(8,128)(2,1)S(1)}, bf16[8,4096]{1,0:T(8,128)(2,1)S(1)}, u32[]{:S(2)}, u32[]{:S(2)}) collective-permute-start(bf16[8,4096]{1,0:T(8,128)(2,1)S(1)} %get-tuple-element.66), channel_id=1, source_target_pairs={{0,2},{1,9},{2,4},{3,11},{4,6},{5,13},{6,0},{7,15},{8,10},{9,17},{... | collective-permute-start | bytes 196616 | tf_op jit(solution)/shard_map/ppermute | solution.py:225
  126.1 4.7 %collective-permute-start.12 = (bf16[8,4096]{1,0:T(8,128)(2,1)S(1)}, bf16[8,4096]{1,0:T(8,128)(2,1)S(1)}, u32[]{:S(2)}, u32[]{:S(2)}) collective-permute-start(bf16[8,4096]{1,0:T(8,128)(2,1)S(1)} %get-tuple-element.67), channel_id=1, source_target_pairs={{0,4},{1,17},{2,6},{3,19},{4,0},{5,21},{6,2},{7,23},{8,12},{9,25},... | collective-permute-start | bytes 196616 | tf_op jit(solution)/shard_map/ppermute | solution.py:225
  128.4 3.4 %collective-permute-start.11 = (bf16[8,4096]{1,0:T(8,128)(2,1)S(1)}, bf16[8,4096]{1,0:T(8,128)(2,1)S(1)}, u32[]{:S(2)}, u32[]{:S(2)}) collective-permute-start(bf16[8,4096]{1,0:T(8,128)(2,1)S(1)} %get-tuple-element.68), channel_id=1, source_target_pairs={{0,6},{1,25},{2,0},{3,27},{4,2},{5,29},{6,4},{7,31},{8,14},{9,1},{... | collective-permute-start | bytes 196616 | tf_op jit(solution)/shard_map/ppermute | solution.py:225

commit v5 on v4

--- a/solution.py
+++ b/solution.py
@@ -12,6 +12,7 @@
 OWN_NEG = 8
 REQ = STEPS + OWN_NEG
 NEG = 256
+ORDER = ((1, 2, 3), (2, 1, 3))
 ITEMS = 512
 DEVICES = 128
 CAP = 4
@@ -230,7 +231,7 @@
 
 
 def spread(rows, stage):
-    return jnp.concatenate([rows] + [turn(rows, stage, k) for k in (1, 2, 3)], axis=0)
+    return jnp.concatenate([rows] + [turn(rows, stage, k) for k in ORDER[stage]], axis=0)
 
 
 def add(parts):
@@ -239,7 +240,9 @@
 
 def collect(rows, stage):
     n = rows.shape[0] // 4
-    return [rows[:n]] + [turn(rows[k * n : (k + 1) * n], stage, -k) for k in (1, 2, 3)]
+    return [rows[:n]] + [
+        turn(rows[k * n : (k + 1) * n], stage, -by) for k, by in enumerate(ORDER[stage], 1)
+    ]
 
 
 def exchange(rows):

time: 198 us -> 198 us (level)
  transfers between devices with their start and end apart: 14 -> 14, of which waited for: 9 -> 8; matrix products, arithmetic and copies ran while one was open for 0% -> 0% of each run, Pallas kernels for 6% -> 6%
where the time goes in v5:
time: 198 us
  blocking collectives  139 us (70%)
  Pallas kernels  25.2 us (13%)
  starting transfers between devices  15.5 us (8%)
  waiting for transfers between devices  12.8 us (6%)
  local copies, waits for them, and re-layouts  2.95 us (1%)
    all_to_all x3, blocking collectives, exchange(): return lax.all_to_all(rows, AXES, split_axis=0, concat_axis=0, tiled=True)  139 us
    ppermute x12, starting transfers between devices, turn(): return lax.ppermute(value, 'seq', pairs)  11.7 us
    ppermute x12, waiting for transfers between devices, turn(): return lax.ppermute(value, 'seq', pairs)  9.42 us
    pallas_call x1, Pallas kernels, on_device(): call(state_kernel, (shape((STEPS, D), BF16), shape((STEPS, D), BF16), sha...  6.69 us
  transfers between devices with their start and end apart: 14, of which 8 were waited for; matrix products, arithmetic and copies ran while one was open for 0% of the time, Pallas kernels for 6%

profile of v5, /device:TPU:1, one launch (start us, length us, event | category | flops | bytes accessed | tf_op | source)
XLA Modules:
  0.0 197.8 jit_solution(13602009785969848978)
XLA Ops:
  0.6 2.2 %route.1 = (s32[128,128]{1,0:T(8,128)S(1)}, s32[1,264]{1,0:T(1,128)S(1)}, bf16[512,4096]{1,0:T(8,128)(2,1)S(1)}) custom-call(s32[1,264]{1,0:T(1,128)} %bitcast.14, s32[1,264]{1,0:T(1,128)} %bitcast.15, bf16[512,4096]{1,0:T(8,128)(2,1)} %table.1), custom_call_target="tpu_custom_call" | custom-call | tf_op jit(solution)/shard_map/route/pallas_call | solution.py:272
  2.9 20.9 %all_to_all.15 = s32[128,1,128]{2,1,0:T(1,128)S(1)} all-to-all(s32[128,1,128]{2,1,0:T(1,128)S(1)} %bitcast.11), channel_id=1, replica_groups=mesh['dp'=4,'seq'=32] {'dp','seq'}, dimensions={0} | all-to-all | bytes 131072 | tf_op jit(solution)/shard_map/all_to_all | solution.py:249
  23.8 2.6 %pick.1 = bf16[128,4,4096]{2,1,0:T(4,128)(2,1)S(1)} custom-call(s32[128,128]{1,0:T(8,128)S(1)} %bitcast.9, bf16[512,4096]{1,0:T(8,128)(2,1)S(1)} %get-tuple-element.35.table), custom_call_target="tpu_custom_call" | custom-call | tf_op jit(solution)/shard_map/pick/pallas_call | solution.py:290
  26.4 57.4 %all_to_all.16.rows = bf16[128,4,4096]{2,1,0:T(4,128)(2,1)S(1)} all-to-all(bf16[128,4,4096]{2,1,0:T(4,128)(2,1)S(1)} %pick.1), channel_id=1, replica_groups=mesh['dp'=4,'seq'=32] {'dp','seq'}, dimensions={0} | all-to-all | bytes 8388608 | tf_op jit(solution)/shard_map/all_to_all | solution.py:249
  83.8 1.5 own_negatives.1
  87.7 1.3 collective-permute-done.2
  88.9 2.1 %collective-permute-done.1 = bf16[8,4096]{1,0:T(8,128)(2,1)S(1)} collective-permute-done((bf16[8,4096]{1,0:T(8,128)(2,1)S(1)}, bf16[8,4096]{1,0:T(8,128)(2,1)S(1)}, u32[]{:S(2)}, u32[]{:S(2)}) %collective-permute-start.1) | collective-permute-done | bytes 65568 | tf_op jit(solution)/shard_map/ppermute | solution.py:226
  92.2 1.5 collective-permute-start.4
  94.3 2.2 %copy-done.1 = bf16[128,4,4096]{2,1,0:T(4,128)(2,1)S(1)} copy-done((bf16[128,4,4096]{2,1,0:T(4,128)(2,1)S(1)}, bf16[128,4,4096]{2,1,0:T(4,128)(2,1)}, u32[]{:S(2)}) %copy-start.1) | copy-done | bytes 4194328
  96.4 6.7 %state.1 = (bf16[256,4096]{1,0:T(8,128)(2,1)S(1)}, bf16[256,4096]{1,0:T(8,128)(2,1)S(1)}, f32[256,1]{1,0:T(8,128)S(1)}) custom-call(s32[1,264]{1,0:T(1,128)S(1)} %get-tuple-element.33.slots.own_slots, bf16[128,4,4096]{2,1,0:T(4,128)(2,1)S(1)} %copy-done.1, f32[1,32]{1,0:T(1,128)S(1)} %copy-done.4, f32[1,256]{1,0:T(1,128)S(1)} %copy-done.2, ...), custom_call_target="tpu_custom_call" | custom-call | flops 3000000000 | bytes 20971520 | tf_op jit(solution)/shard_map/state/pallas_call | solution.py:309
  103.3 3.3 %collective-permute-start.6 = (bf16[128,4096]{1,0:T(8,128)(2,1)S(1)}, bf16[128,4096]{1,0:T(8,128)(2,1)S(1)}, u32[]{:S(2)}, u32[]{:S(2)}) collective-permute-start(bf16[128,4096]{1,0:T(8,128)(2,1)S(1)} %pad_maximum_fusion.negatives.near), channel_id=1, source_target_pairs={{0,1},{1,0},{2,3},{3,2},{4,5},{5,4},{6,7},{7,6},{8,9},{9,8},{10,11... | collective-permute-start | bytes 3145736 | tf_op jit(solution)/shard_map/ppermute | solution.py:230
  107.2 1.6 collective-permute-done.6.far
  108.8 2.0 %loss.1 = (f32[256,1]{1,0:T(8,128)S(1)}, f32[256,1]{1,0:T(8,128)S(1)}, bf16[256,256]{1,0:T(8,128)(2,1)S(1)}, bf16[128,4096]{1,0:T(8,128)(2,1)S(1)}) custom-call(bf16[256,4096]{1,0:T(8,128)(2,1)S(1)} %get-tuple-element.42.rep, f32[256,128]{1,0:T(8,128)S(1)} %near_logits.1.near_logit, bf16[128,4096]{1,0:T(8,128)(2,1)S(1)} %collective-permute-done.6.far, ...), custom_call_target="tpu_custom_call" | custom-call | tf_op jit(solution)/shard_map/loss/pallas_call | solution.py:336
  111.8 1.8 collective-permute-done.7
  115.4 1.8 collective-permute-start.9
  117.2 2.7 %user_grad.1 = bf16[1,256,4096]{2,1,0:T(8,128)(2,1)} custom-call(bf16[256,4096]{1,0:T(8,128)(2,1)S(1)} %get-tuple-element.41.x, f32[256,1]{1,0:T(8,128)S(1)} %get-tuple-element.58.d_pos, bf16[256,256]{1,0:T(8,128)(2,1)S(1)} %get-tuple-element.48.d_neg, bf16[128,4096]{1,0:T(8,128)(2,1)S(1)} %pad_maximum_fusion.negatives.near, ...), custom_call_target="tpu_custom_call" | custom-call | flops 1000000000 | bytes 6291456 | tf_op jit(solution)/shard_map/user_grad/pallas_call | solution.py:351
  119.9 1.1 collective-permute-done.8
  121.0 2.8 %collective-permute-done.10 = bf16[32,4096]{1,0:T(8,128)(2,1)S(1)} collective-permute-done((bf16[32,4096]{1,0:T(8,128)(2,1)S(1)}, bf16[32,4096]{1,0:T(8,128)(2,1)S(1)}, u32[]{:S(2)}, u32[]{:S(2)}) %collective-permute-start.10) | collective-permute-done | bytes 262176 | tf_op jit(solution)/shard_map/ppermute | solution.py:226
  124.0 2.0 %collective-permute-start.13 = (bf16[8,4096]{1,0:T(8,128)(2,1)S(1)}, bf16[8,4096]{1,0:T(8,128)(2,1)S(1)}, u32[]{:S(2)}, u32[]{:S(2)}) collective-permute-start(bf16[8,4096]{1,0:T(8,128)(2,1)S(1)} %get-tuple-element.66), channel_id=1, source_target_pairs={{0,2},{1,9},{2,4},{3,11},{4,6},{5,13},{6,0},{7,15},{8,10},{9,17},{... | collective-permute-start | bytes 196616 | tf_op jit(solution)/shard_map/ppermute | solution.py:226
  126.0 1.1 collective-permute-start.12
  127.1 1.4 collective-permute-start.11
  130.7 2.1 %outgoing.1 = bf16[128,4,4096]{2,1,0:T(4,128)(2,1)S(1)} custom-call(s32[1,264]{1,0:T(1,128)S(1)} %get-tuple-element.33.slots.own_slots, s32[1,264]{1,0:T(1,128)S(1)} %get-tuple-element.33.slots.own_slots, bf16[256,4096]{1,0:T(8,128)(2,1)S(1)} %get-tuple-element.42.rep, f32[256,1]{1,0:T(8,128)S(1)} %get-tuple-element.58.d_pos, ...), custom_call_target="tpu_custom_call" | custom-call | tf_op jit(solution)/shard_map/outgoing/pallas_call | solution.py:372
  132.9 60.9 %all_to_all.17.arrived = bf16[128,4,4096]{2,1,0:T(4,128)(2,1)S(1)} all-to-all(bf16[128,4,4096]{2,1,0:T(4,128)(2,1)S(1)} %outgoing.1), channel_id=1, replica_groups=mesh['dp'=4,'seq'=32] {'dp','seq'}, dimensions={0} | all-to-all | bytes 8388608 | tf_op jit(solution)/shard_map/all_to_all | solution.py:249
  193.8 3.8 %place.1 = f32[512,4096]{1,0:T(8,128)} custom-call(bf16[512,512]{1,0:T(8,128)(2,1)S(1)} %marks.1.hot, bf16[128,4,4096]{2,1,0:T(4,128)(2,1)S(1)} %all_to_all.17.arrived), custom_call_target="tpu_custom_call" | custom-call | tf_op jit(solution)/shard_map/place/pallas_call | solution.py:380
  (36 shorter events, 10.0 us)
Async XLA Ops:
  83.8 2.0 %copy-start = (bf16[128,4,4096]{2,1,0:T(4,128)(2,1)}, bf16[128,4,4096]{2,1,0:T(4,128)(2,1)S(1)}, u32[]{:S(2)}) copy-start(bf16[128,4,4096]{2,1,0:T(4,128)(2,1)S(1)} %all_to_all.16.rows) | copy-start | bytes 12582916
  83.8 3.7 %copy-start.2 = (f32[1,256]{1,0:T(1,128)S(1)}, f32[1,256]{1,0:T(1,128)}, u32[]{:S(2)}) copy-start(f32[1,256]{1,0:T(1,128)} %forget_row.1) | copy-start | bytes 3076
  83.8 10.4 %copy-start.3 = (f32[4096]{0:T(1024)S(1)}, f32[4096]{0:T(1024)}, u32[]{:S(2)}) copy-start(f32[4096]{0:T(1024)} %param.11) | copy-start | bytes 49156
  83.8 10.4 %copy-start.4 = (f32[1,32]{1,0:T(1,128)S(1)}, f32[1,32]{1,0:T(1,128)}, u32[]{:S(2)}) copy-start(f32[1,32]{1,0:T(1,128)} %speeds) | copy-start | bytes 388
  85.8 3.1 %collective-permute-start.2 = (bf16[8,4096]{1,0:T(8,128)(2,1)S(1)}, bf16[8,4096]{1,0:T(8,128)(2,1)S(1)}, u32[]{:S(2)}, u32[]{:S(2)}) collective-permute-start(bf16[8,4096]{1,0:T(8,128)(2,1)S(1)} %own_negatives.1), channel_id=1, source_target_pairs={{0,6},{1,25},{2,0},{3,27},{4,2},{5,29},{6,4},{7,31},{8,14},{9,1},{... | collective-permute-start | bytes 196616 | tf_op jit(solution)/shard_map/ppermute | solution.py:226
  86.4 4.6 %collective-permute-start.1 = (bf16[8,4096]{1,0:T(8,128)(2,1)S(1)}, bf16[8,4096]{1,0:T(8,128)(2,1)S(1)}, u32[]{:S(2)}, u32[]{:S(2)}) collective-permute-start(bf16[8,4096]{1,0:T(8,128)(2,1)S(1)} %own_negatives.1), channel_id=1, source_target_pairs={{0,4},{1,17},{2,6},{3,19},{4,0},{5,21},{6,2},{7,23},{8,12},{9,25},... | collective-permute-start | bytes 196616 | tf_op jit(solution)/shard_map/ppermute | solution.py:226
  87.5 4.6 %collective-permute-start = (bf16[8,4096]{1,0:T(8,128)(2,1)S(1)}, bf16[8,4096]{1,0:T(8,128)(2,1)S(1)}, u32[]{:S(2)}, u32[]{:S(2)}) collective-permute-start(bf16[8,4096]{1,0:T(8,128)(2,1)S(1)} %own_negatives.1), channel_id=1, source_target_pairs={{0,2},{1,9},{2,4},{3,11},{4,6},{5,13},{6,0},{7,15},{8,10},{9,17},{... | collective-permute-start | bytes 196616 | tf_op jit(solution)/shard_map/ppermute | solution.py:226
  92.1 11.0 %collective-permute-start.5 = (bf16[32,4096]{1,0:T(8,128)(2,1)S(1)}, bf16[32,4096]{1,0:T(8,128)(2,1)S(1)}, u32[]{:S(2)}, u32[]{:S(2)}) collective-permute-start(bf16[32,4096]{1,0:T(8,128)(2,1)S(1)} %pad_maximum_fusion.1), channel_id=1, source_target_pairs={{0,24},{1,7},{2,26},{3,1},{4,28},{5,3},{6,30},{7,5},{8,0},{9,15},{... | collective-permute-start | bytes 786440 | tf_op jit(solution)/shard_map/ppermute | solution.py:226
  92.2 10.9 %collective-permute-start.4 = (bf16[32,4096]{1,0:T(8,128)(2,1)S(1)}, bf16[32,4096]{1,0:T(8,128)(2,1)S(1)}, u32[]{:S(2)}, u32[]{:S(2)}) collective-permute-start(bf16[32,4096]{1,0:T(8,128)(2,1)S(1)} %pad_maximum_fusion.1), channel_id=1, source_target_pairs={{0,8},{1,3},{2,10},{3,5},{4,12},{5,7},{6,14},{7,1},{8,16},{9,11},{... | collective-permute-start | bytes 786440 | tf_op jit(solution)/shard_map/ppermute | solution.py:226
  93.7 9.5 %collective-permute-start.3 = (bf16[32,4096]{1,0:T(8,128)(2,1)S(1)}, bf16[32,4096]{1,0:T(8,128)(2,1)S(1)}, u32[]{:S(2)}, u32[]{:S(2)}) collective-permute-start(bf16[32,4096]{1,0:T(8,128)(2,1)S(1)} %pad_maximum_fusion.1), channel_id=1, source_target_pairs={{0,16},{1,5},{2,18},{3,7},{4,20},{5,1},{6,22},{7,3},{8,24},{9,13},... | collective-permute-start | bytes 786440 | tf_op jit(solution)/shard_map/ppermute | solution.py:226
  94.2 2.2 %copy-start.1 = (bf16[128,4,4096]{2,1,0:T(4,128)(2,1)S(1)}, bf16[128,4,4096]{2,1,0:T(4,128)(2,1)}, u32[]{:S(2)}) copy-start(bf16[128,4,4096]{2,1,0:T(4,128)(2,1)} %copy-done) | copy-start | bytes 12582916
  103.3 5.6 %collective-permute-start.6 = (bf16[128,4096]{1,0:T(8,128)(2,1)S(1)}, bf16[128,4096]{1,0:T(8,128)(2,1)S(1)}, u32[]{:S(2)}, u32[]{:S(2)}) collective-permute-start(bf16[128,4096]{1,0:T(8,128)(2,1)S(1)} %pad_maximum_fusion.negatives.near), channel_id=1, source_target_pairs={{0,1},{1,0},{2,3},{3,2},{4,5},{5,4},{6,7},{7,6},{8,9},{9,8},{10,11... | collective-permute-start | bytes 3145736 | tf_op jit(solution)/shard_map/ppermute | solution.py:230
  110.8 2.7 %collective-permute-start.7 = (bf16[128,4096]{1,0:T(8,128)(2,1)S(1)}, bf16[128,4096]{1,0:T(8,128)(2,1)S(1)}, u32[]{:S(2)}, u32[]{:S(2)}) collective-permute-start(bf16[128,4096]{1,0:T(8,128)(2,1)S(1)} %get-tuple-element.49), channel_id=1, source_target_pairs={{0,1},{1,0},{2,3},{3,2},{4,5},{5,4},{6,7},{7,6},{8,9},{9,8},{10,11... | collective-permute-start | bytes 3145736 | tf_op jit(solution)/shard_map/ppermute | solution.py:230
  113.9 7.1 %collective-permute-start.8 = (bf16[32,4096]{1,0:T(8,128)(2,1)S(1)}, bf16[32,4096]{1,0:T(8,128)(2,1)S(1)}, u32[]{:S(2)}, u32[]{:S(2)}) collective-permute-start(bf16[32,4096]{1,0:T(8,128)(2,1)S(1)} %get-tuple-element.63), channel_id=1, source_target_pairs={{0,16},{1,5},{2,18},{3,7},{4,20},{5,1},{6,22},{7,3},{8,24},{9,13},... | collective-permute-start | bytes 786440 | tf_op jit(solution)/shard_map/ppermute | solution.py:226
  114.5 9.3 %collective-permute-start.10 = (bf16[32,4096]{1,0:T(8,128)(2,1)S(1)}, bf16[32,4096]{1,0:T(8,128)(2,1)S(1)}, u32[]{:S(2)}, u32[]{:S(2)}) collective-permute-start(bf16[32,4096]{1,0:T(8,128)(2,1)S(1)} %get-tuple-element.64), channel_id=1, source_target_pairs={{0,8},{1,3},{2,10},{3,5},{4,12},{5,7},{6,14},{7,1},{8,16},{9,11},{... | collective-permute-start | bytes 786440 | tf_op jit(solution)/shard_map/ppermute | solution.py:226
  115.4 8.4 %collective-permute-start.9 = (bf16[32,4096]{1,0:T(8,128)(2,1)S(1)}, bf16[32,4096]{1,0:T(8,128)(2,1)S(1)}, u32[]{:S(2)}, u32[]{:S(2)}) collective-permute-start(bf16[32,4096]{1,0:T(8,128)(2,1)S(1)} %get-tuple-element.65), channel_id=1, source_target_pairs={{0,24},{1,7},{2,26},{3,1},{4,28},{5,3},{6,30},{7,5},{8,0},{9,15},{... | collective-permute-start | bytes 786440 | tf_op jit(solution)/shard_map/ppermute | solution.py:226
  124.0 5.7 %collective-permute-start.13 = (bf16[8,4096]{1,0:T(8,128)(2,1)S(1)}, bf16[8,4096]{1,0:T(8,128)(2,1)S(1)}, u32[]{:S(2)}, u32[]{:S(2)}) collective-permute-start(bf16[8,4096]{1,0:T(8,128)(2,1)S(1)} %get-tuple-element.66), channel_id=1, source_target_pairs={{0,2},{1,9},{2,4},{3,11},{4,6},{5,13},{6,0},{7,15},{8,10},{9,17},{... | collective-permute-start | bytes 196616 | tf_op jit(solution)/shard_map/ppermute | solution.py:226
  126.0 4.7 %collective-permute-start.12 = (bf16[8,4096]{1,0:T(8,128)(2,1)S(1)}, bf16[8,4096]{1,0:T(8,128)(2,1)S(1)}, u32[]{:S(2)}, u32[]{:S(2)}) collective-permute-start(bf16[8,4096]{1,0:T(8,128)(2,1)S(1)} %get-tuple-element.67), channel_id=1, source_target_pairs={{0,4},{1,17},{2,6},{3,19},{4,0},{5,21},{6,2},{7,23},{8,12},{9,25},... | collective-permute-start | bytes 196616 | tf_op jit(solution)/shard_map/ppermute | solution.py:226
  127.1 3.6 %collective-permute-start.11 = (bf16[8,4096]{1,0:T(8,128)(2,1)S(1)}, bf16[8,4096]{1,0:T(8,128)(2,1)S(1)}, u32[]{:S(2)}, u32[]{:S(2)}) collective-permute-start(bf16[8,4096]{1,0:T(8,128)(2,1)S(1)} %get-tuple-element.68), channel_id=1, source_target_pairs={{0,6},{1,25},{2,0},{3,27},{4,2},{5,29},{6,4},{7,31},{8,14},{9,1},{... | collective-permute-start | bytes 196616 | tf_op jit(solution)/shard_map/ppermute | solution.py:226

commit v6 on v5

--- a/solution.py
+++ b/solution.py
@@ -12,6 +12,7 @@
 OWN_NEG = 8
 REQ = STEPS + OWN_NEG
 NEG = 256
+MOVES = 8
 ORDER = ((1, 2, 3), (2, 1, 3))
 ITEMS = 512
 DEVICES = 128
@@ -44,10 +45,17 @@
 def route_kernel(home, names, table, wanted, slots, near_table, owner_row, item_row, sems):
     first = pltpu.make_async_copy(home, owner_row, sems.at[0])
     second = pltpu.make_async_copy(names, item_row, sems.at[1])
-    move = pltpu.make_async_copy(table, near_table, sems.at[2])
+    rows = ITEMS // MOVES
+    moves = [
+        pltpu.make_async_copy(
+            table.at[k * rows : (k + 1) * rows], near_table.at[k * rows : (k + 1) * rows], sems.at[2 + k]
+        )
+        for k in range(MOVES)
+    ]
     first.start()
     second.start()
-    move.start()
+    for move in moves:
+        move.start()
     first.wait()
     second.wait()
     row = owner_row[...]
@@ -68,7 +76,8 @@
         named = jnp.sum(jnp.where(here & (rank == s), item, 0.0), axis=1, keepdims=True)
         out = jnp.where(lane == s, named - 1.0, out)
     wanted[...] = out.astype(I32)
-    move.wait()
+    for move in moves:
+        move.wait()
 
 
 def onehot_items(asked):
@@ -283,7 +292,7 @@
         scratch_shapes=[
             pltpu.VMEM((1, REQ), I32),
             pltpu.VMEM((1, REQ), I32),
-            pltpu.SemaphoreType.DMA((3,)),
+            pltpu.SemaphoreType.DMA((2 + MOVES,)),
         ],
     )(in_hbm(home.reshape(1, REQ)), in_hbm(item.reshape(1, REQ)), in_hbm(table))
     asked = exchange(wanted.reshape(DEVICES, 1, 128)).reshape(DEVICES, 128)

time: 198 us -> 198 us (level)
  no operation moved by 1% of the time
where the time goes in v6:
time: 198 us
  blocking collectives  139 us (70%)
  Pallas kernels  25.2 us (13%)
  starting transfers between devices  15.5 us (8%)
  waiting for transfers between devices  12.8 us (6%)
  local copies, waits for them, and re-layouts  2.95 us (1%)
    all_to_all x3, blocking collectives, exchange(): return lax.all_to_all(rows, AXES, split_axis=0, concat_axis=0, tiled=True)  139 us
    ppermute x12, starting transfers between devices, turn(): return lax.ppermute(value, 'seq', pairs)  11.7 us
    ppermute x12, waiting for transfers between devices, turn(): return lax.ppermute(value, 'seq', pairs)  9.42 us
    pallas_call x1, Pallas kernels, on_device(): call(state_kernel, (shape((STEPS, D), BF16), shape((STEPS, D), BF16), sha...  6.69 us
  transfers between devices with their start and end apart: 14, of which 8 were waited for; matrix products, arithmetic and copies ran while one was open for 0% of the time, Pallas kernels for 6%

profile of v6, /device:TPU:1, one launch (start us, length us, event | category | flops | bytes accessed | tf_op | source)
XLA Modules:
  0.0 197.8 jit_solution(17864277324182595374)
XLA Ops:
  0.6 2.3 %route.1 = (s32[128,128]{1,0:T(8,128)S(1)}, s32[1,264]{1,0:T(1,128)S(1)}, bf16[512,4096]{1,0:T(8,128)(2,1)S(1)}) custom-call(s32[1,264]{1,0:T(1,128)} %bitcast.14, s32[1,264]{1,0:T(1,128)} %bitcast.15, bf16[512,4096]{1,0:T(8,128)(2,1)} %table.1), custom_call_target="tpu_custom_call" | custom-call | tf_op jit(solution)/shard_map/route/pallas_call | solution.py:281
  2.9 20.9 %all_to_all.15 = s32[128,1,128]{2,1,0:T(1,128)S(1)} all-to-all(s32[128,1,128]{2,1,0:T(1,128)S(1)} %bitcast.11), channel_id=1, replica_groups=mesh['dp'=4,'seq'=32] {'dp','seq'}, dimensions={0} | all-to-all | bytes 131072 | tf_op jit(solution)/shard_map/all_to_all | solution.py:258
  23.8 2.6 %pick.1 = bf16[128,4,4096]{2,1,0:T(4,128)(2,1)S(1)} custom-call(s32[128,128]{1,0:T(8,128)S(1)} %bitcast.9, bf16[512,4096]{1,0:T(8,128)(2,1)S(1)} %get-tuple-element.35.table), custom_call_target="tpu_custom_call" | custom-call | tf_op jit(solution)/shard_map/pick/pallas_call | solution.py:299
  26.5 57.4 %all_to_all.16.rows = bf16[128,4,4096]{2,1,0:T(4,128)(2,1)S(1)} all-to-all(bf16[128,4,4096]{2,1,0:T(4,128)(2,1)S(1)} %pick.1), channel_id=1, replica_groups=mesh['dp'=4,'seq'=32] {'dp','seq'}, dimensions={0} | all-to-all | bytes 8388608 | tf_op jit(solution)/shard_map/all_to_all | solution.py:258
  83.8 1.5 own_negatives.1
  87.7 1.3 collective-permute-done.2
  89.0 2.1 %collective-permute-done.1 = bf16[8,4096]{1,0:T(8,128)(2,1)S(1)} collective-permute-done((bf16[8,4096]{1,0:T(8,128)(2,1)S(1)}, bf16[8,4096]{1,0:T(8,128)(2,1)S(1)}, u32[]{:S(2)}, u32[]{:S(2)}) %collective-permute-start.1) | collective-permute-done | bytes 65568 | tf_op jit(solution)/shard_map/ppermute | solution.py:235
  92.2 1.5 collective-permute-start.4
  94.3 2.2 %copy-done.1 = bf16[128,4,4096]{2,1,0:T(4,128)(2,1)S(1)} copy-done((bf16[128,4,4096]{2,1,0:T(4,128)(2,1)S(1)}, bf16[128,4,4096]{2,1,0:T(4,128)(2,1)}, u32[]{:S(2)}) %copy-start.1) | copy-done | bytes 4194328
  96.5 6.7 %state.1 = (bf16[256,4096]{1,0:T(8,128)(2,1)S(1)}, bf16[256,4096]{1,0:T(8,128)(2,1)S(1)}, f32[256,1]{1,0:T(8,128)S(1)}) custom-call(s32[1,264]{1,0:T(1,128)S(1)} %get-tuple-element.33.slots.own_slots, bf16[128,4,4096]{2,1,0:T(4,128)(2,1)S(1)} %copy-done.1, f32[1,32]{1,0:T(1,128)S(1)} %copy-done.4, f32[1,256]{1,0:T(1,128)S(1)} %copy-done.2, ...), custom_call_target="tpu_custom_call" | custom-call | flops 3000000000 | bytes 20971520 | tf_op jit(solution)/shard_map/state/pallas_call | solution.py:318
  103.3 3.3 %collective-permute-start.6 = (bf16[128,4096]{1,0:T(8,128)(2,1)S(1)}, bf16[128,4096]{1,0:T(8,128)(2,1)S(1)}, u32[]{:S(2)}, u32[]{:S(2)}) collective-permute-start(bf16[128,4096]{1,0:T(8,128)(2,1)S(1)} %pad_maximum_fusion.negatives.near), channel_id=1, source_target_pairs={{0,1},{1,0},{2,3},{3,2},{4,5},{5,4},{6,7},{7,6},{8,9},{9,8},{10,11... | collective-permute-start | bytes 3145736 | tf_op jit(solution)/shard_map/ppermute | solution.py:239
  107.3 1.6 collective-permute-done.6.far
  108.8 2.0 %loss.1 = (f32[256,1]{1,0:T(8,128)S(1)}, f32[256,1]{1,0:T(8,128)S(1)}, bf16[256,256]{1,0:T(8,128)(2,1)S(1)}, bf16[128,4096]{1,0:T(8,128)(2,1)S(1)}) custom-call(bf16[256,4096]{1,0:T(8,128)(2,1)S(1)} %get-tuple-element.42.rep, f32[256,128]{1,0:T(8,128)S(1)} %near_logits.1.near_logit, bf16[128,4096]{1,0:T(8,128)(2,1)S(1)} %collective-permute-done.6.far, ...), custom_call_target="tpu_custom_call" | custom-call | tf_op jit(solution)/shard_map/loss/pallas_call | solution.py:345
  111.8 1.8 collective-permute-done.7
  115.5 1.8 collective-permute-start.9
  117.2 2.7 %user_grad.1 = bf16[1,256,4096]{2,1,0:T(8,128)(2,1)} custom-call(bf16[256,4096]{1,0:T(8,128)(2,1)S(1)} %get-tuple-element.41.x, f32[256,1]{1,0:T(8,128)S(1)} %get-tuple-element.58.d_pos, bf16[256,256]{1,0:T(8,128)(2,1)S(1)} %get-tuple-element.48.d_neg, bf16[128,4096]{1,0:T(8,128)(2,1)S(1)} %pad_maximum_fusion.negatives.near, ...), custom_call_target="tpu_custom_call" | custom-call | flops 1000000000 | bytes 6291456 | tf_op jit(solution)/shard_map/user_grad/pallas_call | solution.py:360
  119.9 1.1 collective-permute-done.8
  121.0 2.8 %collective-permute-done.10 = bf16[32,4096]{1,0:T(8,128)(2,1)S(1)} collective-permute-done((bf16[32,4096]{1,0:T(8,128)(2,1)S(1)}, bf16[32,4096]{1,0:T(8,128)(2,1)S(1)}, u32[]{:S(2)}, u32[]{:S(2)}) %collective-permute-start.10) | collective-permute-done | bytes 262176 | tf_op jit(solution)/shard_map/ppermute | solution.py:235
  124.0 2.0 %collective-permute-start.13 = (bf16[8,4096]{1,0:T(8,128)(2,1)S(1)}, bf16[8,4096]{1,0:T(8,128)(2,1)S(1)}, u32[]{:S(2)}, u32[]{:S(2)}) collective-permute-start(bf16[8,4096]{1,0:T(8,128)(2,1)S(1)} %get-tuple-element.66), channel_id=1, source_target_pairs={{0,2},{1,9},{2,4},{3,11},{4,6},{5,13},{6,0},{7,15},{8,10},{9,17},{... | collective-permute-start | bytes 196616 | tf_op jit(solution)/shard_map/ppermute | solution.py:235
  126.0 1.1 collective-permute-start.12
  127.2 1.4 collective-permute-start.11
  130.8 2.1 %outgoing.1 = bf16[128,4,4096]{2,1,0:T(4,128)(2,1)S(1)} custom-call(s32[1,264]{1,0:T(1,128)S(1)} %get-tuple-element.33.slots.own_slots, s32[1,264]{1,0:T(1,128)S(1)} %get-tuple-element.33.slots.own_slots, bf16[256,4096]{1,0:T(8,128)(2,1)S(1)} %get-tuple-element.42.rep, f32[256,1]{1,0:T(8,128)S(1)} %get-tuple-element.58.d_pos, ...), custom_call_target="tpu_custom_call" | custom-call | tf_op jit(solution)/shard_map/outgoing/pallas_call | solution.py:381
  132.9 60.9 %all_to_all.17.arrived = bf16[128,4,4096]{2,1,0:T(4,128)(2,1)S(1)} all-to-all(bf16[128,4,4096]{2,1,0:T(4,128)(2,1)S(1)} %outgoing.1), channel_id=1, replica_groups=mesh['dp'=4,'seq'=32] {'dp','seq'}, dimensions={0} | all-to-all | bytes 8388608 | tf_op jit(solution)/shard_map/all_to_all | solution.py:258
  193.8 3.8 %place.1 = f32[512,4096]{1,0:T(8,128)} custom-call(bf16[512,512]{1,0:T(8,128)(2,1)S(1)} %marks.1.hot, bf16[128,4,4096]{2,1,0:T(4,128)(2,1)S(1)} %all_to_all.17.arrived), custom_call_target="tpu_custom_call" | custom-call | tf_op jit(solution)/shard_map/place/pallas_call | solution.py:389
  (36 shorter events, 10.0 us)
Async XLA Ops:
  83.8 2.0 %copy-start = (bf16[128,4,4096]{2,1,0:T(4,128)(2,1)}, bf16[128,4,4096]{2,1,0:T(4,128)(2,1)S(1)}, u32[]{:S(2)}) copy-start(bf16[128,4,4096]{2,1,0:T(4,128)(2,1)S(1)} %all_to_all.16.rows) | copy-start | bytes 12582916
  83.8 3.7 %copy-start.2 = (f32[1,256]{1,0:T(1,128)S(1)}, f32[1,256]{1,0:T(1,128)}, u32[]{:S(2)}) copy-start(f32[1,256]{1,0:T(1,128)} %forget_row.1) | copy-start | bytes 3076
  83.8 10.4 %copy-start.3 = (f32[4096]{0:T(1024)S(1)}, f32[4096]{0:T(1024)}, u32[]{:S(2)}) copy-start(f32[4096]{0:T(1024)} %param.11) | copy-start | bytes 49156
  83.8 10.4 %copy-start.4 = (f32[1,32]{1,0:T(1,128)S(1)}, f32[1,32]{1,0:T(1,128)}, u32[]{:S(2)}) copy-start(f32[1,32]{1,0:T(1,128)} %speeds) | copy-start | bytes 388
  85.8 3.1 %collective-permute-start.2 = (bf16[8,4096]{1,0:T(8,128)(2,1)S(1)}, bf16[8,4096]{1,0:T(8,128)(2,1)S(1)}, u32[]{:S(2)}, u32[]{:S(2)}) collective-permute-start(bf16[8,4096]{1,0:T(8,128)(2,1)S(1)} %own_negatives.1), channel_id=1, source_target_pairs={{0,6},{1,25},{2,0},{3,27},{4,2},{5,29},{6,4},{7,31},{8,14},{9,1},{... | collective-permute-start | bytes 196616 | tf_op jit(solution)/shard_map/ppermute | solution.py:235
  86.4 4.6 %collective-permute-start.1 = (bf16[8,4096]{1,0:T(8,128)(2,1)S(1)}, bf16[8,4096]{1,0:T(8,128)(2,1)S(1)}, u32[]{:S(2)}, u32[]{:S(2)}) collective-permute-start(bf16[8,4096]{1,0:T(8,128)(2,1)S(1)} %own_negatives.1), channel_id=1, source_target_pairs={{0,4},{1,17},{2,6},{3,19},{4,0},{5,21},{6,2},{7,23},{8,12},{9,25},... | collective-permute-start | bytes 196616 | tf_op jit(solution)/shard_map/ppermute | solution.py:235
  87.5 4.6 %collective-permute-start = (bf16[8,4096]{1,0:T(8,128)(2,1)S(1)}, bf16[8,4096]{1,0:T(8,128)(2,1)S(1)}, u32[]{:S(2)}, u32[]{:S(2)}) collective-permute-start(bf16[8,4096]{1,0:T(8,128)(2,1)S(1)} %own_negatives.1), channel_id=1, source_target_pairs={{0,2},{1,9},{2,4},{3,11},{4,6},{5,13},{6,0},{7,15},{8,10},{9,17},{... | collective-permute-start | bytes 196616 | tf_op jit(solution)/shard_map/ppermute | solution.py:235
  92.1 11.0 %collective-permute-start.5 = (bf16[32,4096]{1,0:T(8,128)(2,1)S(1)}, bf16[32,4096]{1,0:T(8,128)(2,1)S(1)}, u32[]{:S(2)}, u32[]{:S(2)}) collective-permute-start(bf16[32,4096]{1,0:T(8,128)(2,1)S(1)} %pad_maximum_fusion.1), channel_id=1, source_target_pairs={{0,24},{1,7},{2,26},{3,1},{4,28},{5,3},{6,30},{7,5},{8,0},{9,15},{... | collective-permute-start | bytes 786440 | tf_op jit(solution)/shard_map/ppermute | solution.py:235
  92.2 10.9 %collective-permute-start.4 = (bf16[32,4096]{1,0:T(8,128)(2,1)S(1)}, bf16[32,4096]{1,0:T(8,128)(2,1)S(1)}, u32[]{:S(2)}, u32[]{:S(2)}) collective-permute-start(bf16[32,4096]{1,0:T(8,128)(2,1)S(1)} %pad_maximum_fusion.1), channel_id=1, source_target_pairs={{0,8},{1,3},{2,10},{3,5},{4,12},{5,7},{6,14},{7,1},{8,16},{9,11},{... | collective-permute-start | bytes 786440 | tf_op jit(solution)/shard_map/ppermute | solution.py:235
  93.7 9.5 %collective-permute-start.3 = (bf16[32,4096]{1,0:T(8,128)(2,1)S(1)}, bf16[32,4096]{1,0:T(8,128)(2,1)S(1)}, u32[]{:S(2)}, u32[]{:S(2)}) collective-permute-start(bf16[32,4096]{1,0:T(8,128)(2,1)S(1)} %pad_maximum_fusion.1), channel_id=1, source_target_pairs={{0,16},{1,5},{2,18},{3,7},{4,20},{5,1},{6,22},{7,3},{8,24},{9,13},... | collective-permute-start | bytes 786440 | tf_op jit(solution)/shard_map/ppermute | solution.py:235
  94.3 2.2 %copy-start.1 = (bf16[128,4,4096]{2,1,0:T(4,128)(2,1)S(1)}, bf16[128,4,4096]{2,1,0:T(4,128)(2,1)}, u32[]{:S(2)}) copy-start(bf16[128,4,4096]{2,1,0:T(4,128)(2,1)} %copy-done) | copy-start | bytes 12582916
  103.3 5.6 %collective-permute-start.6 = (bf16[128,4096]{1,0:T(8,128)(2,1)S(1)}, bf16[128,4096]{1,0:T(8,128)(2,1)S(1)}, u32[]{:S(2)}, u32[]{:S(2)}) collective-permute-start(bf16[128,4096]{1,0:T(8,128)(2,1)S(1)} %pad_maximum_fusion.negatives.near), channel_id=1, source_target_pairs={{0,1},{1,0},{2,3},{3,2},{4,5},{5,4},{6,7},{7,6},{8,9},{9,8},{10,11... | collective-permute-start | bytes 3145736 | tf_op jit(solution)/shard_map/ppermute | solution.py:239
  110.8 2.7 %collective-permute-start.7 = (bf16[128,4096]{1,0:T(8,128)(2,1)S(1)}, bf16[128,4096]{1,0:T(8,128)(2,1)S(1)}, u32[]{:S(2)}, u32[]{:S(2)}) collective-permute-start(bf16[128,4096]{1,0:T(8,128)(2,1)S(1)} %get-tuple-element.49), channel_id=1, source_target_pairs={{0,1},{1,0},{2,3},{3,2},{4,5},{5,4},{6,7},{7,6},{8,9},{9,8},{10,11... | collective-permute-start | bytes 3145736 | tf_op jit(solution)/shard_map/ppermute | solution.py:239
  113.9 7.1 %collective-permute-start.8 = (bf16[32,4096]{1,0:T(8,128)(2,1)S(1)}, bf16[32,4096]{1,0:T(8,128)(2,1)S(1)}, u32[]{:S(2)}, u32[]{:S(2)}) collective-permute-start(bf16[32,4096]{1,0:T(8,128)(2,1)S(1)} %get-tuple-element.63), channel_id=1, source_target_pairs={{0,16},{1,5},{2,18},{3,7},{4,20},{5,1},{6,22},{7,3},{8,24},{9,13},... | collective-permute-start | bytes 786440 | tf_op jit(solution)/shard_map/ppermute | solution.py:235
  114.6 9.3 %collective-permute-start.10 = (bf16[32,4096]{1,0:T(8,128)(2,1)S(1)}, bf16[32,4096]{1,0:T(8,128)(2,1)S(1)}, u32[]{:S(2)}, u32[]{:S(2)}) collective-permute-start(bf16[32,4096]{1,0:T(8,128)(2,1)S(1)} %get-tuple-element.64), channel_id=1, source_target_pairs={{0,8},{1,3},{2,10},{3,5},{4,12},{5,7},{6,14},{7,1},{8,16},{9,11},{... | collective-permute-start | bytes 786440 | tf_op jit(solution)/shard_map/ppermute | solution.py:235
  115.5 8.4 %collective-permute-start.9 = (bf16[32,4096]{1,0:T(8,128)(2,1)S(1)}, bf16[32,4096]{1,0:T(8,128)(2,1)S(1)}, u32[]{:S(2)}, u32[]{:S(2)}) collective-permute-start(bf16[32,4096]{1,0:T(8,128)(2,1)S(1)} %get-tuple-element.65), channel_id=1, source_target_pairs={{0,24},{1,7},{2,26},{3,1},{4,28},{5,3},{6,30},{7,5},{8,0},{9,15},{... | collective-permute-start | bytes 786440 | tf_op jit(solution)/shard_map/ppermute | solution.py:235
  124.0 5.7 %collective-permute-start.13 = (bf16[8,4096]{1,0:T(8,128)(2,1)S(1)}, bf16[8,4096]{1,0:T(8,128)(2,1)S(1)}, u32[]{:S(2)}, u32[]{:S(2)}) collective-permute-start(bf16[8,4096]{1,0:T(8,128)(2,1)S(1)} %get-tuple-element.66), channel_id=1, source_target_pairs={{0,2},{1,9},{2,4},{3,11},{4,6},{5,13},{6,0},{7,15},{8,10},{9,17},{... | collective-permute-start | bytes 196616 | tf_op jit(solution)/shard_map/ppermute | solution.py:235
  126.0 4.7 %collective-permute-start.12 = (bf16[8,4096]{1,0:T(8,128)(2,1)S(1)}, bf16[8,4096]{1,0:T(8,128)(2,1)S(1)}, u32[]{:S(2)}, u32[]{:S(2)}) collective-permute-start(bf16[8,4096]{1,0:T(8,128)(2,1)S(1)} %get-tuple-element.67), channel_id=1, source_target_pairs={{0,4},{1,17},{2,6},{3,19},{4,0},{5,21},{6,2},{7,23},{8,12},{9,25},... | collective-permute-start | bytes 196616 | tf_op jit(solution)/shard_map/ppermute | solution.py:235
  127.2 3.6 %collective-permute-start.11 = (bf16[8,4096]{1,0:T(8,128)(2,1)S(1)}, bf16[8,4096]{1,0:T(8,128)(2,1)S(1)}, u32[]{:S(2)}, u32[]{:S(2)}) collective-permute-start(bf16[8,4096]{1,0:T(8,128)(2,1)S(1)} %get-tuple-element.68), channel_id=1, source_target_pairs={{0,6},{1,25},{2,0},{3,27},{4,2},{5,29},{6,4},{7,31},{8,14},{9,1},{... | collective-permute-start | bytes 196616 | tf_op jit(solution)/shard_map/ppermute | solution.py:235
